TPU v7x, 128 devices: a whole 4x4x4 slice. The times are simulated.
128 devices in a mesh: ctx: 8 (over y_lo, z), head: 16 (over x, y_hi, core).
Axes of the slice: x: 4, y: 4 (y_hi: 2, y_lo: 2; y = y_hi * 2 + y_lo), z: 4, core: 2. Of those that a mesh axis runs over, the one named last changes fastest.
Arguments:
- residual: bfloat16 [8192, 8192], P(('ctx', 'head')), may hold values from -6 to 6
- q_win: bfloat16 [8192, 16, 256], P('ctx', 'head'), may hold values from -10 to 10
- kv_win: bfloat16 [8192, 16, 2, 256], P('ctx', 'head'), may hold values from -28 to 28
- lam_win: float32 [4, 128], replicated, may hold values from -1.2 to 1.2
- gn_gain: float32 [256], replicated, may hold values from 0.1 to 1.9
- w_out_a: bfloat16 [4096, 8192], P('head'), may hold values from -0.09375 to 0.09375
- norm_gain: float32 [8192], replicated, may hold values from 0.1 to 1.9
- w_qkv: bfloat16 [8192, 16, 3, 256], P(None, 'head'), may hold values from -4 to 4, as said below
Outputs:
- hidden: bfloat16 [8192, 8192], P(('ctx', 'head'))
- part_out: float32 [2, 8192, 16, 256], P(None, 'ctx', 'head')
- log_sums: float32 [2, 16, 8192], P(None, 'head', 'ctx')
Inputs may be any that keep to these rules, and one draw needn't show every extreme that they name: `w_qkv`: projection weights of the next layer.
All inputs are finite; a program needn't handle non-finite values.
Results may differ from a plain program's by a relative error of at most 0.04.
Values may be sent and summed in bfloat16 or wider, within the bound.
A program may use at most 192 MiB of HBM per device.

v0:
```python
from functools import reduce
import math

import jax
import jax.numpy as jnp
from jax import lax
from jax.sharding import PartitionSpec as P

HDIM = 128
WINDOW = 4096


EPSILON = 1e-05
LAMBDA_INIT = 0.8 - 0.6 * math.exp(-3.3)


def passed_along(block, axis, distance):
    devices = range(lax.axis_size(axis))
    route = [(i - distance, i) for i in devices if i - distance in devices]
    return lax.ppermute(block, axis, route)


def window_rows(
    queries, key_part, value_part, row_first, key_first, lambda_full, group_gain, rows_block
):
    heads_here = queries.shape[1]
    key_pos = key_first + jnp.arange(key_part.shape[0], dtype=jnp.int32)

    def window_one_block(number):
        row_start = number * rows_block
        picked = lax.dynamic_slice_in_dim(queries, row_start, rows_block, 0)
        row_pos = row_first + row_start + jnp.arange(rows_block, dtype=jnp.int32)
        scores = jnp.einsum(
            "qhjd,khjd->hjqk", picked, key_part, preferred_element_type=jnp.float32
        ) / math.sqrt(HDIM)
        allowed = (
            (key_pos[None, :] <= row_pos[:, None])
            & (key_pos[None, :] > row_pos[:, None] - WINDOW)
            & (key_pos[None, :] >= 0)
        )
        scores = jnp.where(allowed, scores, -jnp.inf)
        highest = jnp.max(scores, axis=-1, keepdims=True)
        shifted = jnp.exp(scores - highest)
        probs = shifted / jnp.sum(shifted, axis=-1, keepdims=True)
        combined = (probs[:, 0] - lambda_full * probs[:, 1]).astype(jnp.bfloat16)
        attended = jnp.einsum(
            "hqk,khe->qhe", combined, value_part, preferred_element_type=jnp.float32
        )
        factor = lax.rsqrt(jnp.mean(attended * attended, axis=-1, keepdims=True) + EPSILON)
        normed = attended * factor * group_gain * (1.0 - LAMBDA_INIT)
        return normed.astype(jnp.bfloat16).reshape(rows_block, heads_here * value_part.shape[2])

    pieces = lax.map(window_one_block, jnp.arange(queries.shape[0] // rows_block, dtype=jnp.int32))
    return pieces.reshape(queries.shape[0], -1)


def rms_rows(values_in, gain_row):
    widened = values_in.astype(jnp.float32)
    factor = lax.rsqrt(jnp.mean(widened * widened, axis=-1, keepdims=True) + EPSILON)
    return (widened * factor * gain_row).astype(jnp.bfloat16)


def cycle_block_stats(queries, kv_rows, row_first, key_first, present, rows_block):
    tokens_here = kv_rows.shape[0]
    heads_here = kv_rows.shape[1]
    key_part = kv_rows[:, :, 0].reshape(tokens_here, heads_here, 2, HDIM)
    value_part = kv_rows[:, :, 1]
    key_pos = key_first + jnp.arange(tokens_here, dtype=jnp.int32)

    def cycle_one_block(number):
        row_start = number * rows_block
        picked = lax.dynamic_slice_in_dim(queries, row_start, rows_block, 0)
        row_pos = row_first + row_start + jnp.arange(rows_block, dtype=jnp.int32)
        scores = jnp.einsum(
            "qhjd,khjd->hjqk", picked, key_part, preferred_element_type=jnp.float32
        ) / math.sqrt(HDIM)
        allowed = jnp.broadcast_to(present & (key_pos[None, :] <= row_pos[:, None]), scores.shape)
        any_seen = jnp.any(allowed, axis=-1)
        highest = jnp.where(any_seen, jnp.max(jnp.where(allowed, scores, -jnp.inf), axis=-1), 0.0)
        weights = jnp.where(allowed, jnp.exp(scores - highest[..., None]), 0.0)
        totals = jnp.sum(weights, axis=-1)
        summed = jnp.einsum(
            "hjqk,khe->hjqe",
            weights.astype(jnp.bfloat16),
            value_part,
            preferred_element_type=jnp.float32,
        )
        return (highest, any_seen, totals, summed)

    return lax.map(cycle_one_block, jnp.arange(queries.shape[0] // rows_block, dtype=jnp.int32))


def cycle_finish(collected):
    marked = [jnp.where(member[1], member[0], -jnp.inf) for member in collected]
    overall = reduce(jnp.maximum, marked)
    weight_sum = reduce(
        jnp.add,
        [
            jnp.where(member[1], member[2] * jnp.exp(member[0] - overall), 0.0)
            for member in collected
        ],
    )
    log_total = overall + jnp.log(weight_sum)
    result = reduce(
        jnp.add,
        [
            jnp.where(
                member[1][..., None], jnp.exp(member[0] - log_total)[..., None] * member[3], 0.0
            )
            for member in collected
        ],
    )
    return (result, log_total)


def on_device(residual, q_win, kv_win, lam_win, gn_gain, w_out_a, norm_gain, w_qkv):
    tokens_here = q_win.shape[0]
    heads_here = q_win.shape[1]
    rows_block = min(512, tokens_here)
    ctx_pos = lax.axis_index("ctx")
    back_blocks = WINDOW // tokens_here
    lambda_full = (
        jnp.exp(jnp.sum(lam_win[0] * lam_win[1]))
        - jnp.exp(jnp.sum(lam_win[2] * lam_win[3]))
        + LAMBDA_INIT
    )
    queries = q_win.reshape(tokens_here, heads_here, 2, HDIM)
    window_blocks = []
    for behind in range(back_blocks, 0, -1):
        window_blocks.append(passed_along(kv_win, "ctx", behind))
    window_blocks.append(kv_win)
    window_kv_rows = jnp.concatenate(window_blocks, axis=0)
    key_first = (ctx_pos - back_blocks) * tokens_here
    key_part = window_kv_rows[:, :, 0].reshape(-1, heads_here, 2, HDIM)
    value_part = window_kv_rows[:, :, 1]
    normed = window_rows(
        queries,
        key_part,
        value_part,
        ctx_pos * tokens_here,
        key_first,
        lambda_full,
        gn_gain,
        rows_block,
    )
    w_flat = w_qkv.reshape(w_qkv.shape[0], -1)
    summed_out = lax.psum_scatter(
        jnp.dot(normed, w_out_a, preferred_element_type=jnp.float32).astype(jnp.bfloat16),
        "head",
        scatter_dimension=0,
        tiled=True,
    ).astype(jnp.float32)
    h_rows = (residual.astype(jnp.float32) + summed_out).astype(jnp.bfloat16)
    normal_rows = rms_rows(h_rows, norm_gain)
    qkv_float = jnp.dot(
        lax.all_gather(normal_rows, "head", axis=0, tiled=True),
        w_flat,
        preferred_element_type=jnp.float32,
    )
    qkv = qkv_float.astype(jnp.bfloat16).reshape(tokens_here, heads_here, 3, 2 * HDIM)
    cycle_queries = qkv[:, :, 0].reshape(tokens_here, heads_here, 2, HDIM)
    cycle_kv = qkv[:, :, 1:3]
    row_first = ctx_pos * tokens_here
    collected = [
        cycle_block_stats(cycle_queries, cycle_kv, row_first, row_first, ctx_pos >= 0, rows_block)
    ]
    travelling = cycle_kv
    for behind in (1, 2):
        travelling = passed_along(travelling, "ctx", 1)
        collected.append(
            cycle_block_stats(
                cycle_queries,
                travelling,
                row_first,
                row_first - behind * tokens_here,
                ctx_pos >= behind,
                rows_block,
            )
        )
    outputs, log_parts = cycle_finish(collected)
    part_out = outputs.transpose(2, 0, 3, 1, 4).reshape(2, tokens_here, heads_here, 2 * HDIM)
    log_out = log_parts.transpose(2, 1, 0, 3).reshape(2, heads_here, tokens_here)
    return (h_rows, part_out, log_out)


def solution(mesh):
    in_specs = (
        P(("ctx", "head"), None),
        P("ctx", "head", None),
        P("ctx", "head", None, None),
        P(),
        P(),
        P("head", None),
        P(),
        P(None, "head", None, None),
    )
    out_specs = (P(("ctx", "head"), None), P(None, "ctx", "head", None), P(None, "head", "ctx"))
    return jax.shard_map(
        on_device, mesh=mesh, in_specs=in_specs, out_specs=out_specs, check_vma=False
    )
```

profile of v0, /device:TPU:24, one launch (start us, length us, event | category | flops | bytes accessed | tf_op | source)
XLA Modules:
  0.0 663.4 jit_solution(17304475888996035884)
XLA Ops:
  7.2 2.5 copy.22
  9.7 1.3 collective-permute-start
  11.0 5.9 collective-permute-start.1
  16.9 1.9 collective-permute-start.2
  18.9 2.1 collective-permute-start.3
  21.0 1.4 multiply_reduce_fusion.1
  23.8 2.0 copy.21
  25.9 10.7 %collective-permute-done = bf16[1024,1,2,256]{0,3,2,1:T(8,128)(2,1)} collective-permute-done((bf16[1024,1,2,256]{0,3,2,1:T(8,128)(2,1)S(1)}, bf16[1024,1,2,256]{0,3,2,1:T(8,128)(2,1)}, u32[]{:S(2)}, u32[]{:S(2)}) %collective-permute-start) | collective-permute-done | bytes 1048608 | tf_op jit(solution)/shard_map/ppermute | solution.py:20
  36.6 1.3 constant_dynamic-update-slice_fusion.5
  37.9 22.6 %collective-permute-done.1 = bf16[1024,1,2,256]{0,3,2,1:T(8,128)(2,1)} collective-permute-done((bf16[1024,1,2,256]{0,3,2,1:T(8,128)(2,1)S(1)}, bf16[1024,1,2,256]{0,3,2,1:T(8,128)(2,1)}, u32[]{:S(2)}, u32[]{:S(2)}) %collective-permute-start.1) | collective-permute-done | bytes 1048608 | tf_op jit(solution)/shard_map/ppermute | solution.py:20
  60.5 1.3 constant_dynamic-update-slice_fusion.4
  61.8 23.5 %collective-permute-done.2 = bf16[1024,1,2,256]{0,3,2,1:T(8,128)(2,1)} collective-permute-done((bf16[1024,1,2,256]{0,3,2,1:T(8,128)(2,1)S(1)}, bf16[1024,1,2,256]{0,3,2,1:T(8,128)(2,1)}, u32[]{:S(2)}, u32[]{:S(2)}) %collective-permute-start.2) | collective-permute-done | bytes 1048608 | tf_op jit(solution)/shard_map/ppermute | solution.py:20
  85.3 1.3 constant_dynamic-update-slice_fusion.3
  86.6 20.7 %collective-permute-done.3 = bf16[1024,1,2,256]{0,3,2,1:T(8,128)(2,1)S(1)} collective-permute-done((bf16[1024,1,2,256]{0,3,2,1:T(8,128)(2,1)S(1)}, bf16[1024,1,2,256]{0,3,2,1:T(8,128)(2,1)S(1)}, u32[]{:S(2)}, u32[]{:S(2)}) %collective-permute-start.3) | collective-permute-done | bytes 1048608 | tf_op jit(solution)/shard_map/ppermute | solution.py:20
  107.5 1.8 fusion.108
  109.4 2.6 copy.27
  111.9 3.2 copy.29
  115.2 163.8 %while.65 = (s32[]{:T(128)}, bf16[2,512,256]{2,1,0:T(8,128)(2,1)}, s32[2]{0:T(128)S(1)}, s32[]{:T(128)}, bf16[1024,1,2,128]{0,3,2,1:T(8,128)(2,1)}, /*index=5*/b...) while((s32[]{:T(128)}, bf16[2,512,256]{2,1,0:T(8,128)(2,1)}, ...), condition=%wide.region_6.7_spmd.clone, body=%wide.region_2.6_spmd.clone.sunk | while | flops 2734977536 | bytes 139005664 | solution.py:53
  116.5 9.5 %fusion.137 = f32[2,512,5120]{2,1,0:T(8,128)} fusion(bf16[5120,1,2,128]{3,0,2,1:T(8,128)(2,1)S(1)} %get-tuple-element.1003, bf16[1024,1,2,128]{0,3,2,1:T(8,128)(2,1)} %get-tuple-element.1002, s32[]{:T(128)S(6)} %select_n.251), kind=kOutput, calls=%fused_computation.20.clone.1 | convolution fusion | flops 1342177280 | bytes 23855108 | tf_op jit(solution)/shard_map/while/body/eval_jaxpr/qhjd,khjd->hjqk/dot_general | solution.py:33
  126.0 4.5 and_and_fusion.2
  130.5 29.9 %subtract_exponential_fusion.2 = f32[2,512,5120]{2,1,0:T(8,128)} fusion(f32[2,512,5120]{2,1,0:T(8,128)} %fusion.137, pred[512,5120]{1,0:T(8,128)(4,1)} %and_and_fusion.2), kind=kOutput, calls=%fused_computation.7.clone.1 | output fusion | flops 26220544 | bytes 44564480 | tf_op jit(solution)/shard_map/while/body/eval_jaxpr/sub | solution.py:43
  160.4 21.0 %divide_bitcast_fusion.2 = f32[1,2,512,5120]{3,2,1,0:T(8,128)} fusion(f32[2,512,5120]{2,1,0:T(8,128)} %subtract_exponential_fusion.2), kind=kOutput, calls=%fused_computation.6.clone.1 | output fusion | flops 5249023 | bytes 41943040 | tf_op jit(solution)/shard_map/while/body/eval_jaxpr/div | solution.py:44
  181.4 8.9 %multiply_reduce_fusion.4 = (f32[512]{0:T(512)S(1)}, f32[1,256,512]{2,1,0:T(8,128)S(1)}) fusion(bf16[5120,1,256]{2,0,1:T(8,128)(2,1)} %get-tuple-element.1005, f32[1,2,512,5120]{3,2,1,0:T(8,128)} %divide_bitcast_fusion.2, f32[]{:T(128)} %get-tuple-element.1004), kind=kOutput, calls=%fused_computation.24.clone.1 | convolution fusion | flops 1350303232 | bytes 24119300 | tf_op jit(solution)/shard_map/while/body/eval_jaxpr/hqk,khe->qhe/dot_general | solution.py:46
  192.6 9.5 %fusion.137 = f32[2,512,5120]{2,1,0:T(8,128)} fusion(bf16[5120,1,2,128]{3,0,2,1:T(8,128)(2,1)S(1)} %get-tuple-element.1003, bf16[1024,1,2,128]{0,3,2,1:T(8,128)(2,1)} %get-tuple-element.1002, s32[]{:T(128)S(6)} %select_n.251), kind=kOutput, calls=%fused_computation.20.clone.1 | convolution fusion | flops 1342177280 | bytes 23855108 | tf_op jit(solution)/shard_map/while/body/eval_jaxpr/qhjd,khjd->hjqk/dot_general | solution.py:33
  202.2 4.5 and_and_fusion.2
  206.7 29.9 %subtract_exponential_fusion.2 = f32[2,512,5120]{2,1,0:T(8,128)} fusion(f32[2,512,5120]{2,1,0:T(8,128)} %fusion.137, pred[512,5120]{1,0:T(8,128)(4,1)} %and_and_fusion.2), kind=kOutput, calls=%fused_computation.7.clone.1 | output fusion | flops 26220544 | bytes 44564480 | tf_op jit(solution)/shard_map/while/body/eval_jaxpr/sub | solution.py:43
  236.6 21.0 %divide_bitcast_fusion.2 = f32[1,2,512,5120]{3,2,1,0:T(8,128)} fusion(f32[2,512,5120]{2,1,0:T(8,128)} %subtract_exponential_fusion.2), kind=kOutput, calls=%fused_computation.6.clone.1 | output fusion | flops 5249023 | bytes 41943040 | tf_op jit(solution)/shard_map/while/body/eval_jaxpr/div | solution.py:44
  257.6 8.9 %multiply_reduce_fusion.4 = (f32[512]{0:T(512)S(1)}, f32[1,256,512]{2,1,0:T(8,128)S(1)}) fusion(bf16[5120,1,256]{2,0,1:T(8,128)(2,1)} %get-tuple-element.1005, f32[1,2,512,5120]{3,2,1,0:T(8,128)} %divide_bitcast_fusion.2, f32[]{:T(128)} %get-tuple-element.1004), kind=kOutput, calls=%fused_computation.24.clone.1 | convolution fusion | flops 1350303232 | bytes 24119300 | tf_op jit(solution)/shard_map/while/body/eval_jaxpr/hqk,khe->qhe/dot_general | solution.py:46
  279.0 12.6 %convolution_convert_fusion = bf16[1024,8192]{1,0:T(8,128)(2,1)} fusion(bf16[1024,256]{1,0:T(8,128)(2,1)} %bitcast.205, bf16[256,8192]{1,0:T(8,128)(2,1)} %param.21), kind=kOutput, calls=%fused_computation.121 | convolution fusion | flops 4303355904 | bytes 21495808 | tf_op jit(solution)/shard_map/dot_general | solution.py:148
  291.7 144.1 %reduce-scatter.2.cloned.1.call-done = bf16[64,8192]{1,0:T(8,128)(2,1)} async-done(((bf16[1024,8192]{1,0:T(8,128)(2,1)}), bf16[64,8192]{1,0:T(8,128)(2,1)}) %reduce-scatter.2.cloned.1.call-update) | async-done | bytes 1048592 | tf_op jit(solution)/shard_map/reduce_scatter | solution.py:147
  435.8 1.7 fusion.105
  438.5 1.3 fusion.107
  439.8 16.8 %copy.31 = bf16[8192,1,3,256]{0,3,2,1:T(8,128)(2,1)} copy(bf16[8192,1,3,256]{3,0,2,1:T(8,128)(2,1)} %param.23) | data formatting | bytes 25165824 | tf_op args[7]
  456.6 91.4 %all-gather.2.cloned.1.call-done = bf16[1024,8192]{1,0:T(8,128)(2,1)} async-done(((bf16[64,8192]{1,0:T(8,128)(2,1)}), bf16[1024,8192]{1,0:T(8,128)(2,1)}) %all-gather.2.cloned.1.call-update) | async-done | bytes 16777232 | tf_op jit(solution)/shard_map/all_gather | solution.py:156
  548.0 18.8 %convolution_convert_fusion.1 = bf16[1024,768]{0,1:T(8,128)(2,1)S(1)} fusion(bf16[1024,8192]{1,0:T(8,128)(2,1)} %all-gather.2.cloned.1.call-done, bf16[8192,768]{0,1:T(8,128)(2,1)} %bitcast.195), kind=kOutput, calls=%fused_computation.129 | convolution fusion | flops 12885688320 | bytes 30932992 | tf_op jit(solution)/shard_map/dot_general | solution.py:155
  566.9 1.0 slice.79
  569.5 3.5 collective-permute-start.4
  573.2 11.6 %while.68 = (s32[]{:T(128)}, f32[2,1,2,512]{3,2,1,0:T(2,128)S(1)}, pred[2,1,2,512]{3,2,1,0:T(4,128)(4,1)S(1)}, f32[2,1,2,512]{3,2,1,0:T(2,128)S(1)}, f32[2,1,2,5...) while((s32[]{:T(128)}, f32[2,1,2,512]{3,2,1,0:T(2,128)S(1)}, ...), condition=%wide.region_13.14_spmd.clone.clone, body=%wide.region_9.13_spmd.clone.clone.sunk | while | flops 818414592 | bytes 19194120 | solution.py:90
  576.2 1.4 fusion.153
  577.6 1.4 fusion.152
  581.0 1.0 select_reduce_fusion.8
  582.0 1.4 fusion.153
  583.4 1.4 fusion.152
  584.9 14.3 %collective-permute-done.4 = bf16[1024,1,2,256]{0,3,2,1:T(8,128)(2,1)} collective-permute-done((bf16[1024,1,2,256]{0,3,2,1:T(8,128)(2,1)}, bf16[1024,1,2,256]{0,3,2,1:T(8,128)(2,1)}, u32[]{:S(2)}, u32[]{:S(2)}) %collective-permute-start.4) | collective-permute-done | bytes 1048608 | tf_op jit(solution)/shard_map/ppermute | solution.py:20
  599.2 2.2 slice_bitcast_fusion.1
  601.4 1.3 copy.36
  602.7 2.0 copy.37
  604.8 1.9 collective-permute-start.5
  606.7 1.5 broadcast.344.clone.1
  608.2 13.1 %while.66 = (s32[]{:T(128)}, f32[2,1,2,512]{3,2,1,0:T(2,128)S(1)}, pred[2,1,2,512]{3,2,1,0:T(4,128)(4,1)S(1)}, f32[2,1,2,512]{3,2,1,0:T(2,128)S(1)}, f32[2,1,2,5...) while((s32[]{:T(128)}, f32[2,1,2,512]{3,2,1,0:T(2,128)S(1)}, ...), condition=%wide.region_18.19_spmd.clone, body=%wide.region_14.18_spmd.clone.sunk | while | flops 818414592 | bytes 19194636 | solution.py:90
  611.3 2.1 fusion.143
  613.5 1.4 fusion.142
  617.8 2.1 fusion.143
  619.9 1.4 fusion.142
  621.4 12.2 %collective-permute-done.5 = bf16[1024,1,2,256]{0,3,2,1:T(8,128)(2,1)} collective-permute-done((bf16[1024,1,2,256]{0,3,2,1:T(8,128)(2,1)}, bf16[1024,1,2,256]{0,3,2,1:T(8,128)(2,1)}, u32[]{:S(2)}, u32[]{:S(2)}) %collective-permute-start.5) | collective-permute-done | bytes 1048608 | tf_op jit(solution)/shard_map/ppermute | solution.py:20
  633.6 1.3 slice_bitcast_fusion
  636.3 11.6 %while.67 = (s32[]{:T(128)}, f32[2,1,2,512]{3,2,1,0:T(2,128)S(1)}, pred[2,1,2,512]{3,2,1,0:T(4,128)(4,1)S(1)}, f32[2,1,2,512]{3,2,1,0:T(2,128)S(1)}, f32[2,1,2,5...) while((s32[]{:T(128)}, f32[2,1,2,512]{3,2,1,0:T(2,128)S(1)}, ...), condition=%wide.region_23.24_spmd.clone, body=%wide.region_19.23_spmd.clone.sunk | while | flops 818414592 | bytes 19194128 | solution.py:90
  638.3 1.0 select_reduce_fusion.7
  639.4 1.4 fusion.148
  640.7 1.4 fusion.147
  645.2 1.4 fusion.148
  646.6 1.4 fusion.147
  648.1 4.0 add_bitcast_fusion
  652.1 3.5 copy.41
  (117 shorter events, 20.2 us)
Async XLA Ops:
  7.2 428.6 %reduce-scatter.2.cloned.1.call-start = ((), (), s32[]{:S(2)}) async-start(), calls=%async_computation.1 | async-start | bytes 17825792 | tf_op jit(solution)/shard_map/reduce_scatter | solution.py:147
  9.7 26.9 %collective-permute-start = (bf16[1024,1,2,256]{0,3,2,1:T(8,128)(2,1)S(1)}, bf16[1024,1,2,256]{0,3,2,1:T(8,128)(2,1)}, u32[]{:S(2)}, u32[]{:S(2)}) collective-permute-start(bf16[1024,1,2,256]{0,3,2,1:T(8,128)(2,1)S(1)} %copy.22), channel_id=1, source_target_pairs={{0,64},{16,80},{32,96},{48,112},{1,65},{17,81},{33,97},{49,113},{2... | collective-permute-start | bytes 3145736 | tf_op jit(solution)/shard_map/ppermute | solution.py:20
  11.0 49.5 %collective-permute-start.1 = (bf16[1024,1,2,256]{0,3,2,1:T(8,128)(2,1)S(1)}, bf16[1024,1,2,256]{0,3,2,1:T(8,128)(2,1)}, u32[]{:S(2)}, u32[]{:S(2)}) collective-permute-start(bf16[1024,1,2,256]{0,3,2,1:T(8,128)(2,1)S(1)} %copy.22), channel_id=1, source_target_pairs={{0,48},{16,64},{32,80},{48,96},{64,112},{1,49},{17,65},{33,81},{49... | collective-permute-start | bytes 3145736 | tf_op jit(solution)/shard_map/ppermute | solution.py:20
  16.9 68.4 %collective-permute-start.2 = (bf16[1024,1,2,256]{0,3,2,1:T(8,128)(2,1)S(1)}, bf16[1024,1,2,256]{0,3,2,1:T(8,128)(2,1)}, u32[]{:S(2)}, u32[]{:S(2)}) collective-permute-start(bf16[1024,1,2,256]{0,3,2,1:T(8,128)(2,1)S(1)} %copy.22), channel_id=1, source_target_pairs={{0,32},{16,48},{32,64},{48,80},{64,96},{80,112},{1,33},{17,49},{33... | collective-permute-start | bytes 3145736 | tf_op jit(solution)/shard_map/ppermute | solution.py:20
  18.9 88.5 %collective-permute-start.3 = (bf16[1024,1,2,256]{0,3,2,1:T(8,128)(2,1)S(1)}, bf16[1024,1,2,256]{0,3,2,1:T(8,128)(2,1)S(1)}, u32[]{:S(2)}, u32[]{:S(2)}) collective-permute-start(bf16[1024,1,2,256]{0,3,2,1:T(8,128)(2,1)S(1)} %copy.22), channel_id=1, source_target_pairs={{0,16},{16,32},{32,48},{48,64},{64,80},{80,96},{96,112},{1,17},{17... | collective-permute-start | bytes 3145736 | tf_op jit(solution)/shard_map/ppermute | solution.py:20
  109.3 5.8 copy-start.7
  291.6 144.2 %copy-start.2 = (bf16[64,8192]{1,0:T(8,128)(2,1)S(1)}, bf16[64,8192]{1,0:T(8,128)(2,1)}, u32[]{:S(2)}) copy-start(bf16[64,8192]{1,0:T(8,128)(2,1)} %param.16) | copy-start | bytes 3145732
  291.6 146.9 %copy-start.6 = (f32[8192]{0:T(1024)S(1)}, f32[8192]{0:T(1024)}, u32[]{:S(2)}) copy-start(f32[8192]{0:T(1024)} %param.22) | copy-start | bytes 98308
  291.6 256.4 %all-gather.2.cloned.1.call-start = ((), (), s32[]{:S(2)}) async-start(), calls=%async_computation.2 | async-start | bytes 17825792 | tf_op jit(solution)/shard_map/all_gather | solution.py:156
  437.5 1.0 copy-start.1
  569.5 29.6 %collective-permute-start.4 = (bf16[1024,1,2,256]{0,3,2,1:T(8,128)(2,1)}, bf16[1024,1,2,256]{0,3,2,1:T(8,128)(2,1)}, u32[]{:S(2)}, u32[]{:S(2)}) collective-permute-start(bf16[1024,1,2,256]{0,3,2,1:T(8,128)(2,1)} %slice.79), channel_id=1, source_target_pairs={{0,16},{16,32},{32,48},{48,64},{64,80},{80,96},{96,112},{1,17},{17... | collective-permute-start | bytes 3145736 | tf_op jit(solution)/shard_map/ppermute | solution.py:20
  574.6 1.6 copy-start.5
  580.4 1.6 copy-start.5
  584.9 23.3 %copy-start = (f32[2,1,2,512,256]{4,3,2,1,0:T(8,128)}, f32[2,1,2,512,256]{4,3,2,1,0:T(8,128)S(1)}, u32[]{:S(2)}) copy-start(f32[2,1,2,512,256]{4,3,2,1,0:T(8,128)S(1)} %get-tuple-element.333) | copy-start | bytes 6291460
  604.8 28.8 %collective-permute-start.5 = (bf16[1024,1,2,256]{0,3,2,1:T(8,128)(2,1)}, bf16[1024,1,2,256]{0,3,2,1:T(8,128)(2,1)}, u32[]{:S(2)}, u32[]{:S(2)}) collective-permute-start(bf16[1024,1,2,256]{0,3,2,1:T(8,128)(2,1)} %collective-permute-done.4), channel_id=1, source_target_pairs={{0,16},{16,32},{32,48},{48,64},{64,80},{80,96},{96,112},{1,17},{17... | collective-permute-start | bytes 3145736 | tf_op jit(solution)/shard_map/ppermute | solution.py:20
  609.7 1.6 copy-start.4
  616.2 1.6 copy-start.4
  637.7 1.6 copy-start.3
  643.5 1.6 copy-start.3
Sparse Core Ops, SparseCore 0:
  291.7 144.0 reduce-scatter.1
  439.9 108.0 all-gather.1
where the time goes:
time: 675 us; the launch traced here: 663 us
  waiting for transfers between devices  340 us (50%)
  other arithmetic  131 us (19%)
  matrix products  84.1 us (12%)
  local copies, waits for them, and re-layouts  57.8 us (9%)
  loops' own time  17.4 us (3%)
  starting transfers between devices  16.7 us (2%)
  between operations  16.1 us (2%)
    reduce_scatter x1, waiting for transfers between devices, on_device(): lax.psum_scatter(jnp.dot(normed, w_out_a, preferred_element_type=jnp.floa...  144 us
    ppermute x6, waiting for transfers between devices, passed_along(): return lax.ppermute(block, axis, route)  104 us
    all_gather x1, waiting for transfers between devices, on_device(): lax.all_gather(normal_rows, 'head', axis=0, tiled=True)  91.4 us
    sub x2, other arithmetic, window_one_block(): shifted = jnp.exp(scores - highest)  59.8 us
    div x2, other arithmetic, window_one_block(): probs = shifted / jnp.sum(shifted, axis=-1, keepdims=True)  42 us
    unnamed x25, local copies, waits for them, and re-layouts  35.6 us
    dot_general x2, matrix products, window_one_block(): jnp.einsum('qhjd,khjd->hjqk', picked, key_part, preferred_element_type=jn...  19 us
    dot_general x1, matrix products, on_device(): jnp.dot(lax.all_gather(normal_rows, 'head', axis=0, tiled=True), w_flat,...  18.8 us
  transfers between devices with their start and end apart: 8, of which 8 were waited for; matrix products, arithmetic and copies ran while one was open for 7% of the time, Pallas kernels for 0%

commit v1 on v0

v1 whole, which is shorter than its diff:
```python
import functools
import math

import jax
import jax.numpy as jnp
from jax import lax
from jax.experimental import pallas as pl
from jax.experimental.pallas import tpu as pltpu
from jax.sharding import PartitionSpec as P

HDIM = 128
WINDOW = 4096
EPSILON = 1e-05
LAMBDA_INIT = 0.8 - 0.6 * math.exp(-3.3)
SCALE = math.log2(math.e) / math.sqrt(HDIM)
LN2 = math.log(2.0)
NEG = -1e30
ONES = 16
ROWS = 256


def passed_along(block, axis, distance):
    devices = range(lax.axis_size(axis))
    route = [(i - distance, i) for i in devices if i - distance in devices]
    return lax.ppermute(block, axis, route)


def with_ones(values):
    flipped = values.astype(jnp.float32).T.astype(jnp.bfloat16)
    return jnp.concatenate([flipped, jnp.ones((ONES, values.shape[0]), jnp.bfloat16)], axis=0)


def scaled_queries(picked):
    return (picked.astype(jnp.float32) * SCALE).astype(jnp.bfloat16)


def online_step(queries, keys, values_up, m_ref, acc_ref, mask):
    for j in range(2):
        scores = lax.dot_general(
            keys[:, j * HDIM : (j + 1) * HDIM],
            queries[:, j * HDIM : (j + 1) * HDIM],
            (((1,), (1,)), ((), ())),
            preferred_element_type=jnp.float32,
        )
        if mask is not None:
            scores = jnp.where(mask, scores, NEG)
        before = m_ref[j]
        after = jnp.maximum(before, jnp.max(scores, axis=0, keepdims=True))
        weights = jnp.exp2(scores - after).astype(jnp.bfloat16)
        acc_ref[j] = acc_ref[j] * jnp.exp2(before - after) + jnp.dot(
            values_up, weights, preferred_element_type=jnp.float32
        )
        m_ref[j] = after


def window_kernel(lam_ref, q_ref, gain_ref, *refs):
    kv_refs, (out_ref, vt_ref, m_ref, acc_ref) = refs[:5], refs[5:]
    number = pl.program_id(0)
    ctx = lax.axis_index("ctx")

    @pl.when(number == 0)
    def _():
        for n in range(5):
            vt_ref[n] = with_ones(kv_refs[n][:, 256:])

    queries = scaled_queries(q_ref[...])
    m_ref[...] = jnp.full_like(m_ref, NEG)
    acc_ref[...] = jnp.zeros_like(acc_ref)
    tokens = kv_refs[0].shape[0]
    key_pos = lax.broadcasted_iota(jnp.int32, (tokens, ROWS), 0)
    row_pos = lax.broadcasted_iota(jnp.int32, (tokens, ROWS), 1) + number * ROWS
    online_step(queries, kv_refs[0], vt_ref[0], m_ref, acc_ref, key_pos <= row_pos)
    for n in range(1, 5):

        @pl.when(ctx >= n)
        def _():
            online_step(
                queries, kv_refs[n], vt_ref[n], m_ref, acc_ref, key_pos > row_pos if n == 4 else None
            )

    one = acc_ref[0, :256] / acc_ref[0, 256:257]
    two = acc_ref[1, :256] / acc_ref[1, 256:257]
    attended = one - lam_ref[0] * two
    factor = lax.rsqrt(jnp.mean(attended * attended, axis=0, keepdims=True) + EPSILON)
    normed = (attended * factor).T * (gain_ref[...] * (1.0 - LAMBDA_INIT))
    out_ref[...] = normed.astype(jnp.bfloat16)


def window_attention(queries, blocks, lam, gain):
    tokens = queries.shape[0]
    whole = pl.BlockSpec((tokens, 512), lambda i: (0, 0))
    return pl.pallas_call(
        window_kernel,
        name="window",
        grid=(tokens // ROWS,),
        out_shape=jax.ShapeDtypeStruct((tokens, 256), jnp.bfloat16),
        in_specs=[
            pl.BlockSpec(memory_space=pltpu.SMEM),
            pl.BlockSpec((ROWS, 256), lambda i: (i, 0)),
            pl.BlockSpec((1, 256), lambda i: (0, 0)),
        ]
        + [whole] * 5,
        out_specs=pl.BlockSpec((ROWS, 256), lambda i: (i, 0)),
        scratch_shapes=[
            pltpu.VMEM((5, 256 + ONES, tokens), jnp.bfloat16),
            pltpu.VMEM((2, 1, ROWS), jnp.float32),
            pltpu.VMEM((2, 256 + ONES, ROWS), jnp.float32),
        ],
        compiler_params=pltpu.CompilerParams(vmem_limit_bytes=48 * 2**20),
    )(lam.reshape(1), queries, gain.reshape(1, 256), *blocks)


def cycle_kernel(q_ref, kv0_ref, kv1_ref, kv2_ref, out_ref, log_ref, vt_ref, m_ref, acc_ref):
    number = pl.program_id(0)
    ctx = lax.axis_index("ctx")
    kv_refs = (kv0_ref, kv1_ref, kv2_ref)

    @pl.when(number == 0)
    def _():
        for n in range(3):
            vt_ref[n] = with_ones(kv_refs[n][:, 256:])

    queries = scaled_queries(q_ref[...])
    m_ref[...] = jnp.full_like(m_ref, NEG)
    acc_ref[...] = jnp.zeros_like(acc_ref)
    tokens = kv0_ref.shape[0]
    key_pos = lax.broadcasted_iota(jnp.int32, (tokens, ROWS), 0)
    row_pos = lax.broadcasted_iota(jnp.int32, (tokens, ROWS), 1) + number * ROWS
    online_step(queries, kv0_ref, vt_ref[0], m_ref, acc_ref, key_pos <= row_pos)
    for n in (1, 2):

        @pl.when(ctx >= n)
        def _():
            online_step(queries, kv_refs[n], vt_ref[n], m_ref, acc_ref, None)

    for j in range(2):
        total = acc_ref[j, 256:257]
        out_ref[j] = (acc_ref[j, :256] / total).T
        log_ref[j : j + 1, :] = (m_ref[j] + jnp.log2(total)) * LN2


def cycle_attention(queries, blocks):
    tokens = queries.shape[0]
    whole = pl.BlockSpec((tokens, 512), lambda i: (0, 0))
    return pl.pallas_call(
        cycle_kernel,
        name="cycle",
        grid=(tokens // ROWS,),
        out_shape=(
            jax.ShapeDtypeStruct((2, tokens, 256), jnp.float32),
            jax.ShapeDtypeStruct((2, tokens), jnp.float32),
        ),
        in_specs=[pl.BlockSpec((ROWS, 256), lambda i: (i, 0))] + [whole] * 3,
        out_specs=(
            pl.BlockSpec((2, ROWS, 256), lambda i: (0, i, 0)),
            pl.BlockSpec((2, ROWS), lambda i: (0, i)),
        ),
        scratch_shapes=[
            pltpu.VMEM((3, 256 + ONES, tokens), jnp.bfloat16),
            pltpu.VMEM((2, 1, ROWS), jnp.float32),
            pltpu.VMEM((2, 256 + ONES, ROWS), jnp.float32),
        ],
        compiler_params=pltpu.CompilerParams(vmem_limit_bytes=48 * 2**20),
    )(queries, *blocks)


def rms_rows(values_in, gain_row):
    widened = values_in.astype(jnp.float32)
    factor = lax.rsqrt(jnp.mean(widened * widened, axis=-1, keepdims=True) + EPSILON)
    return (widened * factor * gain_row).astype(jnp.bfloat16)


def on_device(residual, q_win, kv_win, lam_win, gn_gain, w_out_a, norm_gain, w_qkv):
    tokens_here = q_win.shape[0]
    lambda_full = (
        jnp.exp(jnp.sum(lam_win[0] * lam_win[1]))
        - jnp.exp(jnp.sum(lam_win[2] * lam_win[3]))
        + LAMBDA_INIT
    )
    kv_here = kv_win.reshape(tokens_here, 512)
    blocks = [kv_here] + [passed_along(kv_here, "ctx", behind) for behind in (1, 2, 3, 4)]
    normed = window_attention(q_win.reshape(tokens_here, 256), blocks, lambda_full, gn_gain)
    w_flat = w_qkv.reshape(w_qkv.shape[0], -1)
    summed_out = lax.psum_scatter(
        jnp.dot(normed, w_out_a, preferred_element_type=jnp.float32).astype(jnp.bfloat16),
        "head",
        scatter_dimension=0,
        tiled=True,
    ).astype(jnp.float32)
    h_rows = (residual.astype(jnp.float32) + summed_out).astype(jnp.bfloat16)
    normal_rows = rms_rows(h_rows, norm_gain)
    qkv = jnp.dot(
        lax.all_gather(normal_rows, "head", axis=0, tiled=True),
        w_flat,
        preferred_element_type=jnp.float32,
    ).astype(jnp.bfloat16)
    kv_next = qkv[:, 256:]
    next_blocks = [kv_next] + [passed_along(kv_next, "ctx", behind) for behind in (1, 2)]
    part_out, log_out = cycle_attention(qkv[:, :256], next_blocks)
    return (
        h_rows,
        part_out.reshape(2, tokens_here, 1, 256),
        log_out.reshape(2, 1, tokens_here),
    )


def solution(mesh):
    in_specs = (
        P(("ctx", "head"), None),
        P("ctx", "head", None),
        P("ctx", "head", None, None),
        P(),
        P(),
        P("head", None),
        P(),
        P(None, "head", None, None),
    )
    out_specs = (P(("ctx", "head"), None), P(None, "ctx", "head", None), P(None, "head", "ctx"))
    return jax.shard_map(
        on_device, mesh=mesh, in_specs=in_specs, out_specs=out_specs, check_vma=False
    )
```

time: 675 us -> 507 us (0.75); the launches traced: 663 us -> 505 us
  other arithmetic: 131 us -> 4.43 us
  matrix products: 84.1 us -> 29.1 us
  Pallas kernels: 0 us -> 48.5 us
  local copies, waits for them, and re-layouts: 57.8 us -> 24.2 us
  waiting for transfers between devices: 340 us -> 364 us
  loops' own time: 17.4 us -> 0 us
    sub x2 -> x0, other arithmetic: 59.8 us -> none  [window_one_block(): shifted = jnp.exp(scores - highest)]
    dot_general x16 -> x0, matrix products: 52.7 us -> none  [the longest x2 19 us: window_one_block(): jnp.einsum('qhjd,khjd->hjqk', picked, key_part, preferred_element_type=jn...]
    pallas_call x0 -> x2, Pallas kernels: none -> 48.5 us  [the longest x1 30.8 us: window_attention(): pl.pallas_call(window_kernel, name='window', grid=(tokens // ROWS,), out_...]
    div x2 -> x0, other arithmetic: 42 us -> none  [window_one_block(): probs = shifted / jnp.sum(shifted, axis=-1, keepdims=True)]
    ppermute x6, waiting for transfers between devices: 104 us -> 129 us  [passed_along(): return lax.ppermute(block, axis, route)]
    another operation x4 -> x0, loops' own time: 17.4 us -> none  [the longest x1 12.8 us: window_rows(): lax.map(window_one_block, jnp.arange(queries.shape[0] // rows_block, dtyp...]
    unnamed x25 -> x16, local copies, waits for them, and re-layouts: 35.6 us -> 24.1 us
    and x2 -> x0, other arithmetic: 9 us -> none  [window_one_block(): (key_pos[None, :] <= row_pos[:, None]) & (key_pos[None, :] > row_pos[:, N...]
  transfers between devices with their start and end apart: 8 -> 8, of which waited for: 8 -> 8; matrix products, arithmetic and copies ran while one was open for 7% -> 4% of each run, Pallas kernels for 0% -> 0%
where the time goes in v1:
time: 507 us; the launch traced here: 505 us
  waiting for transfers between devices  364 us (72%)
  Pallas kernels  48.5 us (10%)
  matrix products  29.1 us (6%)
  local copies, waits for them, and re-layouts  24.2 us (5%)
  starting transfers between devices  19.4 us (4%)
  between operations  15.5 us (3%)
    reduce_scatter x1, waiting for transfers between devices, on_device(): lax.psum_scatter(jnp.dot(normed, w_out_a, preferred_element_type=jnp.floa...  144 us
    ppermute x6, waiting for transfers between devices, passed_along(): return lax.ppermute(block, axis, route)  129 us
    all_gather x1, waiting for transfers between devices, on_device(): lax.all_gather(normal_rows, 'head', axis=0, tiled=True)  91.5 us
    pallas_call x1, Pallas kernels, window_attention(): pl.pallas_call(window_kernel, name='window', grid=(tokens // ROWS,), out_...  30.8 us
    unnamed x16, local copies, waits for them, and re-layouts  24.1 us
    ppermute x6, starting transfers between devices, passed_along(): return lax.ppermute(block, axis, route)  19.1 us
    dot_general x1, matrix products, on_device(): jnp.dot(lax.all_gather(normal_rows, 'head', axis=0, tiled=True), w_flat,...  18.8 us
    pallas_call x1, Pallas kernels, cycle_attention(): pl.pallas_call(cycle_kernel, name='cycle', grid=(tokens // ROWS,), out_sh...  17.7 us
  transfers between devices with their start and end apart: 8, of which 8 were waited for; matrix products, arithmetic and copies ran while one was open for 4% of the time, Pallas kernels for 0%

profile of v1, /device:TPU:24, one launch (start us, length us, event | category | flops | bytes accessed | tf_op | source)
XLA Modules:
  0.0 505.4 jit_solution(4329198207434231625)
XLA Ops:
  7.2 0.0 reduce-scatter.2.cloned.1.call-start
  7.2 1.4 copy.16
  8.7 1.3 collective-permute-start.3
  10.0 5.9 %collective-permute-start.2 = (bf16[1024,512]{1,0:T(8,128)(2,1)S(1)}, bf16[1024,512]{1,0:T(8,128)(2,1)S(1)}, u32[]{:S(2)}, u32[]{:S(2)}) collective-permute-start(bf16[1024,512]{1,0:T(8,128)(2,1)S(1)} %bitcast.14), channel_id=1, source_target_pairs={{0,48},{16,64},{32,80},{48,96},{64,112},{1,49},{17,65},{33,81},{49... | collective-permute-start | bytes 3145736 | tf_op jit(solution)/shard_map/ppermute | solution.py:25
  15.9 1.9 collective-permute-start.1
  17.8 2.1 collective-permute-start
  20.0 1.4 multiply_reduce_fusion
  22.8 12.6 %collective-permute-done.3.refs_4_ = bf16[1024,512]{1,0:T(8,128)(2,1)S(1)} collective-permute-done((bf16[1024,512]{1,0:T(8,128)(2,1)S(1)}, bf16[1024,512]{1,0:T(8,128)(2,1)S(1)}, u32[]{:S(2)}, u32[]{:S(2)}) %collective-permute-start.3) | collective-permute-done | bytes 1048608 | tf_op jit(solution)/shard_map/ppermute | solution.py:25
  35.5 0.0 copy-start.4
  35.5 23.9 %collective-permute-done.2.refs_3_ = bf16[1024,512]{1,0:T(8,128)(2,1)S(1)} collective-permute-done((bf16[1024,512]{1,0:T(8,128)(2,1)S(1)}, bf16[1024,512]{1,0:T(8,128)(2,1)S(1)}, u32[]{:S(2)}, u32[]{:S(2)}) %collective-permute-start.2) | collective-permute-done | bytes 1048608 | tf_op jit(solution)/shard_map/ppermute | solution.py:25
  59.4 24.9 %collective-permute-done.1.refs_2_ = bf16[1024,512]{1,0:T(8,128)(2,1)} collective-permute-done((bf16[1024,512]{1,0:T(8,128)(2,1)S(1)}, bf16[1024,512]{1,0:T(8,128)(2,1)}, u32[]{:S(2)}, u32[]{:S(2)}) %collective-permute-start.1) | collective-permute-done | bytes 1048608 | tf_op jit(solution)/shard_map/ppermute | solution.py:25
  84.3 22.1 %collective-permute-done.refs_1_ = bf16[1024,512]{1,0:T(8,128)(2,1)} collective-permute-done((bf16[1024,512]{1,0:T(8,128)(2,1)S(1)}, bf16[1024,512]{1,0:T(8,128)(2,1)}, u32[]{:S(2)}, u32[]{:S(2)}) %collective-permute-start) | collective-permute-done | bytes 1048608 | tf_op jit(solution)/shard_map/ppermute | solution.py:25
  106.5 0.0 copy-done.4
  106.5 0.0 copy-start
  106.5 1.0 copy-done
  107.5 0.0 copy-start.1
  107.5 0.7 copy-done.1
  108.2 30.8 %window.1 = bf16[1024,256]{1,0:T(8,128)(2,1)S(1)} custom-call(f32[1]{0:T(128)} %bitcast.lam_ref, bf16[1024,256]{1,0:T(8,128)(2,1)S(1)} %bitcast.19, f32[1,256]{1,0:T(1,128)S(1)} %bitcast.21, bf16[1024,512]{1,0:T(8,128)(2,1)S(1)} %bitcast.17, bf16[1024,512]{1,0:T(8,128)(2,1)} %collective-permute-done.refs_1_, ...), custom_call_target="tpu_custom_call" | custom-call | tf_op jit(solution)/shard_map/window/pallas_call | solution.py:92
  139.0 10.3 %convolution_convert_fusion = bf16[1024,8192]{1,0:T(8,128)(2,1)} fusion(bf16[1024,256]{1,0:T(8,128)(2,1)S(1)} %window.1, bf16[256,8192]{1,0:T(8,128)(2,1)} %param.13), kind=kOutput, calls=%fused_computation | convolution fusion | flops 4303355904 | bytes 21495808 | tf_op jit(solution)/shard_map/dot_general | solution.py:185
  149.3 0.0 copy-start.3
  149.3 0.0 copy-start.5
  149.3 0.0 reduce-scatter.2.cloned.1.call-update
  149.3 0.2 all-gather.2.cloned.1.call-start
  149.5 144.2 %reduce-scatter.2.cloned.1.call-done = bf16[64,8192]{1,0:T(8,128)(2,1)} async-done(((bf16[1024,8192]{1,0:T(8,128)(2,1)}), bf16[64,8192]{1,0:T(8,128)(2,1)}) %reduce-scatter.2.cloned.1.call-update) | async-done | bytes 1048592 | tf_op jit(solution)/shard_map/reduce_scatter | solution.py:184
  293.7 0.0 copy-done.3
  293.7 1.7 fusion
  295.4 0.0 copy-start.2
  295.5 0.0 copy-done.5
  295.5 1.3 fusion.2
  296.8 0.0 all-gather.2.cloned.1.call-update
  296.8 16.8 %copy.13 = bf16[8192,1,3,256]{0,3,2,1:T(8,128)(2,1)} copy(bf16[8192,1,3,256]{3,0,2,1:T(8,128)(2,1)} %param.15) | data formatting | bytes 25165824 | tf_op args[7]
  313.6 0.0 copy-done.2
  313.6 91.5 %all-gather.2.cloned.1.call-done = bf16[1024,8192]{1,0:T(8,128)(2,1)} async-done(((bf16[64,8192]{1,0:T(8,128)(2,1)}), bf16[1024,8192]{1,0:T(8,128)(2,1)}) %all-gather.2.cloned.1.call-update) | async-done | bytes 16777232 | tf_op jit(solution)/shard_map/all_gather | solution.py:193
  405.1 18.8 %convolution_convert_fusion.1 = bf16[1024,768]{1,0:T(8,128)(2,1)S(1)} fusion(bf16[1024,8192]{1,0:T(8,128)(2,1)} %all-gather.2.cloned.1.call-done, bf16[8192,768]{0,1:T(8,128)(2,1)} %bitcast.22), kind=kOutput, calls=%fused_computation.7 | convolution fusion | flops 12885688320 | bytes 30932992 | tf_op jit(solution)/shard_map/dot_general | solution.py:192
  423.9 0.1 slice.25.kv0_ref
  424.0 5.1 %collective-permute-start.5 = (bf16[1024,512]{1,0:T(8,128)(2,1)S(1)}, bf16[1024,512]{1,0:T(8,128)(2,1)S(1)}, u32[]{:S(2)}, u32[]{:S(2)}) collective-permute-start(bf16[1024,512]{1,0:T(8,128)(2,1)S(1)} %slice.25.kv0_ref), channel_id=1, source_target_pairs={{0,32},{16,48},{32,64},{48,80},{64,96},{80,112},{1,33},{17,49},{33... | collective-permute-start | bytes 3145736 | tf_op jit(solution)/shard_map/ppermute | solution.py:25
  429.0 2.8 collective-permute-start.4
  431.9 21.8 %collective-permute-done.5.kv2_ref = bf16[1024,512]{1,0:T(8,128)(2,1)S(1)} collective-permute-done((bf16[1024,512]{1,0:T(8,128)(2,1)S(1)}, bf16[1024,512]{1,0:T(8,128)(2,1)S(1)}, u32[]{:S(2)}, u32[]{:S(2)}) %collective-permute-start.5) | collective-permute-done | bytes 1048608 | tf_op jit(solution)/shard_map/ppermute | solution.py:25
  453.7 23.0 %collective-permute-done.4.kv1_ref = bf16[1024,512]{1,0:T(8,128)(2,1)S(1)} collective-permute-done((bf16[1024,512]{1,0:T(8,128)(2,1)S(1)}, bf16[1024,512]{1,0:T(8,128)(2,1)S(1)}, u32[]{:S(2)}, u32[]{:S(2)}) %collective-permute-start.4) | collective-permute-done | bytes 1048608 | tf_op jit(solution)/shard_map/ppermute | solution.py:25
  476.7 17.7 %cycle.1 = (f32[2,1024,256]{2,1,0:T(8,128)S(1)}, f32[2,1024]{1,0:T(2,128)S(1)}) custom-call(bf16[1024,256]{1,0:T(8,128)(2,1)S(1)} %slice.24.q_ref, bf16[1024,512]{1,0:T(8,128)(2,1)S(1)} %slice.25.kv0_ref, bf16[1024,512]{1,0:T(8,128)(2,1)S(1)} %collective-permute-done.4.kv1_ref, bf16[1024,512]{1,0:T(8,128)(2,1)S(1)} %collective-permute-done.5.kv2_ref), custom_call_target="tpu_custom_call" | custom-call | tf_op jit(solution)/shard_map/cycle/pallas_call | solution.py:145
  494.5 3.5 copy.14
  498.0 0.6 copy.15
  (2 shorter events, 0.0 us)
Async XLA Ops:
  7.2 286.6 %reduce-scatter.2.cloned.1.call-start = ((), (), s32[]{:S(2)}) async-start(), calls=%async_computation.1 | async-start | bytes 17825792 | tf_op jit(solution)/shard_map/reduce_scatter | solution.py:184
  8.7 26.8 %collective-permute-start.3 = (bf16[1024,512]{1,0:T(8,128)(2,1)S(1)}, bf16[1024,512]{1,0:T(8,128)(2,1)S(1)}, u32[]{:S(2)}, u32[]{:S(2)}) collective-permute-start(bf16[1024,512]{1,0:T(8,128)(2,1)S(1)} %bitcast.13), channel_id=1, source_target_pairs={{0,64},{16,80},{32,96},{48,112},{1,65},{17,81},{33,97},{49,113},{2... | collective-permute-start | bytes 3145736 | tf_op jit(solution)/shard_map/ppermute | solution.py:25
  10.0 49.4 %collective-permute-start.2 = (bf16[1024,512]{1,0:T(8,128)(2,1)S(1)}, bf16[1024,512]{1,0:T(8,128)(2,1)S(1)}, u32[]{:S(2)}, u32[]{:S(2)}) collective-permute-start(bf16[1024,512]{1,0:T(8,128)(2,1)S(1)} %bitcast.14), channel_id=1, source_target_pairs={{0,48},{16,64},{32,80},{48,96},{64,112},{1,49},{17,65},{33,81},{49... | collective-permute-start | bytes 3145736 | tf_op jit(solution)/shard_map/ppermute | solution.py:25
  15.9 68.4 %collective-permute-start.1 = (bf16[1024,512]{1,0:T(8,128)(2,1)S(1)}, bf16[1024,512]{1,0:T(8,128)(2,1)}, u32[]{:S(2)}, u32[]{:S(2)}) collective-permute-start(bf16[1024,512]{1,0:T(8,128)(2,1)S(1)} %bitcast.15), channel_id=1, source_target_pairs={{0,32},{16,48},{32,64},{48,80},{64,96},{80,112},{1,33},{17,49},{33... | collective-permute-start | bytes 3145736 | tf_op jit(solution)/shard_map/ppermute | solution.py:25
  17.8 88.6 %collective-permute-start = (bf16[1024,512]{1,0:T(8,128)(2,1)S(1)}, bf16[1024,512]{1,0:T(8,128)(2,1)}, u32[]{:S(2)}, u32[]{:S(2)}) collective-permute-start(bf16[1024,512]{1,0:T(8,128)(2,1)S(1)} %bitcast.16), channel_id=1, source_target_pairs={{0,16},{16,32},{32,48},{48,64},{64,80},{80,96},{96,112},{1,17},{17... | collective-permute-start | bytes 3145736 | tf_op jit(solution)/shard_map/ppermute | solution.py:25
  35.5 71.0 %copy-start.4 = (bf16[1024,512]{1,0:T(8,128)(2,1)}, bf16[1024,512]{1,0:T(8,128)(2,1)S(1)}, u32[]{:S(2)}) copy-start(bf16[1024,512]{1,0:T(8,128)(2,1)S(1)} %collective-permute-done.3.refs_4_) | copy-start | bytes 3145732
  106.5 1.0 copy-start
  107.5 0.7 copy-start.1
  149.3 144.5 %copy-start.3 = (bf16[64,8192]{1,0:T(8,128)(2,1)S(1)}, bf16[64,8192]{1,0:T(8,128)(2,1)}, u32[]{:S(2)}) copy-start(bf16[64,8192]{1,0:T(8,128)(2,1)} %param.8) | copy-start | bytes 3145732
  149.3 146.2 %copy-start.5 = (f32[8192]{0:T(1024)S(1)}, f32[8192]{0:T(1024)}, u32[]{:S(2)}) copy-start(f32[8192]{0:T(1024)} %param.14) | copy-start | bytes 98308
  149.3 255.8 %all-gather.2.cloned.1.call-start = ((), (), s32[]{:S(2)}) async-start(), calls=%async_computation.2 | async-start | bytes 17825792 | tf_op jit(solution)/shard_map/all_gather | solution.py:193
  295.4 18.2 %copy-start.2 = (bf16[64,8192]{1,0:T(8,128)(2,1)}, bf16[64,8192]{1,0:T(8,128)(2,1)S(1)}, u32[]{:S(2)}) copy-start(bf16[64,8192]{1,0:T(8,128)(2,1)S(1)} %get-tuple-element.16) | copy-start | bytes 3145732
  424.0 29.7 %collective-permute-start.5 = (bf16[1024,512]{1,0:T(8,128)(2,1)S(1)}, bf16[1024,512]{1,0:T(8,128)(2,1)S(1)}, u32[]{:S(2)}, u32[]{:S(2)}) collective-permute-start(bf16[1024,512]{1,0:T(8,128)(2,1)S(1)} %slice.25.kv0_ref), channel_id=1, source_target_pairs={{0,32},{16,48},{32,64},{48,80},{64,96},{80,112},{1,33},{17,49},{33... | collective-permute-start | bytes 3145736 | tf_op jit(solution)/shard_map/ppermute | solution.py:25
  429.0 47.7 %collective-permute-start.4 = (bf16[1024,512]{1,0:T(8,128)(2,1)S(1)}, bf16[1024,512]{1,0:T(8,128)(2,1)S(1)}, u32[]{:S(2)}, u32[]{:S(2)}) collective-permute-start(bf16[1024,512]{1,0:T(8,128)(2,1)S(1)} %slice.25.kv0_ref), channel_id=1, source_target_pairs={{0,16},{16,32},{32,48},{48,64},{64,80},{80,96},{96,112},{1,17},{17... | collective-permute-start | bytes 3145736 | tf_op jit(solution)/shard_map/ppermute | solution.py:25
Sparse Core Ops, SparseCore 0:
  149.4 144.2 reduce-scatter.1
  297.0 108.0 all-gather.1

commit v2 on v1

--- a/solution.py
+++ b/solution.py
@@ -164,10 +164,260 @@
     )(queries, *blocks)
 
 
-def rms_rows(values_in, gain_row):
-    widened = values_in.astype(jnp.float32)
-    factor = lax.rsqrt(jnp.mean(widened * widened, axis=-1, keepdims=True) + EPSILON)
-    return (widened * factor * gain_row).astype(jnp.bfloat16)
+MESH = pl.DeviceIdType.MESH
+CHUNKS = 4
+SUB = 16
+
+
+def place():
+    head = lax.axis_index("head")
+    return lax.axis_index("ctx"), head // 4, (head // 2) % 2, head % 2
+
+
+def mid_kernel(
+    x_cols,
+    normed_ref,
+    w_own_hbm,
+    w_sib_hbm,
+    residual_ref,
+    gain_ref,
+    w_qkv_hbm,
+    hidden_ref,
+    qkv_ref,
+    w_own,
+    w_sib,
+    w_qkv,
+    n_sib,
+    part,
+    x1_in,
+    y1_in,
+    x2_out,
+    x2_in,
+    y2_out,
+    y2_in,
+    rows_all,
+    acc,
+    load_sem,
+    n_sem,
+    x1_sem,
+    x2_sem,
+    y1_sem,
+    y2_sem,
+    h1_sem,
+    h2_sem,
+    g1_sem,
+    g2_sem,
+    s_sem,
+):
+    ctx, x, y, core = place()
+    width = w_own.shape[1]
+    low, high = pl.ds(0, x_cols), pl.ds(x_cols, width - x_cols)
+
+    def across(d):
+        return (ctx, lax.rem(x + d, 4) * 4 + y * 2 + core)
+
+    over_y = (ctx, x * 4 + (1 - y) * 2 + core)
+    sibling = (ctx, x * 4 + y * 2 + 1 - core)
+
+    loads = [
+        pltpu.make_async_copy(source, target, load_sem.at[n])
+        for n, (source, target) in enumerate(
+            [(w_own_hbm, w_own), (w_sib_hbm, w_sib), (w_qkv_hbm, w_qkv)]
+        )
+    ]
+    for load in loads:
+        load.start()
+
+    barrier = pltpu.get_barrier_semaphore()
+    for peer in (across(1), across(2), across(3), over_y, sibling):
+        pl.semaphore_signal(barrier, inc=1, device_id=peer, device_id_type=MESH)
+    pl.semaphore_wait(barrier, 5)
+
+    started = []
+
+    def send(source, target, sems, device):
+        copy = pltpu.make_async_remote_copy(
+            src_ref=source,
+            dst_ref=target,
+            send_sem=sems.at[0],
+            recv_sem=sems.at[1],
+            device_id=device,
+            device_id_type=MESH,
+        )
+        copy.start()
+        started.append(copy)
+        return copy
+
+    n_copy = send(normed_ref.at[:, 1 - core], n_sib, n_sem, sibling)
+    loads[0].wait()
+    loads[1].wait()
+    n_copy.wait_recv()
+
+    state = [dict() for _ in range(CHUNKS)]
+    tile = min(1024, width)
+
+    def stage_a(r):
+        own_rows = normed_ref[:, core, r].reshape(8 * SUB, 256)
+        sib_rows = n_sib[:, r].reshape(8 * SUB, 256)
+
+        def columns(j, carry):
+            span = pl.ds(pl.multiple_of(j * tile, tile), tile)
+            value = jnp.dot(own_rows, w_own[:, span], preferred_element_type=jnp.float32)
+            value += jnp.dot(sib_rows, w_sib[:, span], preferred_element_type=jnp.float32)
+            part[r, :, :, :, span] = value.astype(jnp.bfloat16).reshape(4, 2, SUB, tile)
+            return carry
+
+        lax.fori_loop(0, width // tile, columns, 0)
+        state[r]["1"] = [
+            send(part.at[r, :, 1 - y, :, high], y1_in.at[r], y1_sem.at[r], over_y)
+        ] + [
+            send(
+                part.at[r, lax.rem(x + d, 4), :, :, low],
+                x1_in.at[r, d - 1],
+                x1_sem.at[r, d - 1],
+                across(d),
+            )
+            for d in (2, 1, 3)
+        ]
+
+    def wide(value):
+        return value.astype(jnp.float32)
+
+    def stage_b(r):
+        for copy in state[r]["1"]:
+            copy.wait_recv()
+        for d in (1, 2, 3):
+            other = lax.rem(x + d, 4)
+            y2_out[r, d - 1] = (
+                wide(part[r, other, y, :, high]) + wide(y1_in[r, other])
+            ).astype(jnp.bfloat16)
+        total = wide(part[r, x, 1 - y, :, low])
+        for d in (1, 2, 3):
+            total += wide(x1_in[r, d - 1, 1 - y])
+        x2_out[r] = total.astype(jnp.bfloat16)
+        state[r]["2"] = [send(x2_out.at[r], x2_in.at[r], x2_sem.at[r], over_y)] + [
+            send(y2_out.at[r, d - 1], y2_in.at[r, d - 1], y2_sem.at[r, d - 1], across(d))
+            for d in (2, 1, 3)
+        ]
+
+    def stage_c(r):
+        for copy in state[r]["2"]:
+            copy.wait_recv()
+        left = wide(part[r, x, y, :, low]) + wide(x2_in[r])
+        right = wide(part[r, x, y, :, high]) + wide(y1_in[r, x])
+        for d in (1, 2, 3):
+            left += wide(x1_in[r, d - 1, y])
+            right += wide(y2_in[r, d - 1])
+        left = (wide(residual_ref[r, :, low]) + left).astype(jnp.bfloat16)
+        right = (wide(residual_ref[r, :, high]) + right).astype(jnp.bfloat16)
+        hidden_ref[r, :, low] = left
+        hidden_ref[r, :, high] = right
+        left, right = wide(left), wide(right)
+        squares = jnp.sum(left * left, axis=-1, keepdims=True)
+        squares += jnp.sum(right * right, axis=-1, keepdims=True)
+        factor = lax.rsqrt(squares / width + EPSILON)
+        mine = rows_all.at[r, x, y, core]
+        mine[:, low] = (left * factor * gain_ref[:, low]).astype(jnp.bfloat16)
+        mine[:, high] = (right * factor * gain_ref[:, high]).astype(jnp.bfloat16)
+        state[r]["3"] = [send(mine.at[:, high], mine.at[:, high], g1_sem.at[r], over_y)] + [
+            send(mine.at[:, low], mine.at[:, low], h1_sem.at[r, d - 1], across(d))
+            for d in (2, 1, 3)
+        ]
+
+    def stage_d(r):
+        for copy in state[r]["3"]:
+            copy.wait_recv()
+        row = rows_all.at[r, :, y, core, :, low]
+        column = rows_all.at[r, x, :, core, :, high]
+        state[r]["4"] = [send(row, row, h2_sem.at[r], over_y)] + [
+            send(column, column, g2_sem.at[r, d - 1], across(d)) for d in (2, 1, 3)
+        ]
+
+    def stage_e(r):
+        for copy in state[r]["4"]:
+            copy.wait_recv()
+        ours = rows_all.at[r, :, :, core]
+        state[r]["5"] = send(ours, ours, s_sem.at[r], sibling)
+
+    def stage_f(r):
+        state[r]["5"].wait_recv()
+        if r == 0:
+            loads[2].wait()
+
+        def depth(j, carry):
+            span = pl.ds(pl.multiple_of(j * tile, tile), tile)
+            rows = rows_all[r, :, :, :, :, span].reshape(16 * SUB, tile)
+            acc[...] += jnp.dot(rows, w_qkv[span, :], preferred_element_type=jnp.float32)
+            return carry
+
+        acc[...] = jnp.zeros_like(acc)
+        lax.fori_loop(0, width // tile, depth, 0)
+        qkv_ref[:, r] = acc[...].astype(jnp.bfloat16).reshape(16, SUB, acc.shape[1])
+
+    stages = [stage_a, stage_b, stage_c, stage_d, stage_e, stage_f]
+    for step in range(CHUNKS - 1 + len(stages)):
+        for r in reversed(range(CHUNKS)):
+            if 0 <= step - r < len(stages):
+                stages[step - r](r)
+    for copy in started:
+        copy.wait_send()
+
+
+def project_and_spread(normed, w_own, w_sib, residual, gain, w_qkv):
+    width = w_own.shape[1]
+    x_cols = width * 13 // 32
+    out_cols = w_qkv.shape[1]
+    bf16 = jnp.bfloat16
+    any_space = pl.BlockSpec(memory_space=pl.ANY)
+    vmem = pl.BlockSpec(memory_space=pltpu.VMEM)
+    sem = pltpu.SemaphoreType.DMA
+    hidden, qkv = pl.pallas_call(
+        functools.partial(mid_kernel, x_cols),
+        name="project_and_spread",
+        out_shape=(
+            jax.ShapeDtypeStruct((CHUNKS, SUB, width), bf16),
+            jax.ShapeDtypeStruct((16, CHUNKS, SUB, out_cols), bf16),
+        ),
+        in_specs=[vmem, any_space, any_space, vmem, vmem, any_space],
+        out_specs=(vmem, vmem),
+        scratch_shapes=[
+            pltpu.VMEM((256, width), bf16),
+            pltpu.VMEM((256, width), bf16),
+            pltpu.VMEM((width, out_cols), bf16),
+            pltpu.VMEM((8, CHUNKS, SUB, 256), bf16),
+            pltpu.VMEM((CHUNKS, 4, 2, SUB, width), bf16),
+            pltpu.VMEM((CHUNKS, 3, 2, SUB, x_cols), bf16),
+            pltpu.VMEM((CHUNKS, 4, SUB, width - x_cols), bf16),
+            pltpu.VMEM((CHUNKS, SUB, x_cols), bf16),
+            pltpu.VMEM((CHUNKS, SUB, x_cols), bf16),
+            pltpu.VMEM((CHUNKS, 3, SUB, width - x_cols), bf16),
+            pltpu.VMEM((CHUNKS, 3, SUB, width - x_cols), bf16),
+            pltpu.VMEM((CHUNKS, 4, 2, 2, SUB, width), bf16),
+            pltpu.VMEM((16 * SUB, out_cols), jnp.float32),
+            sem((3,)),
+            sem((2,)),
+            sem((CHUNKS, 3, 2)),
+            sem((CHUNKS, 2)),
+            sem((CHUNKS, 2)),
+            sem((CHUNKS, 3, 2)),
+            sem((CHUNKS, 3, 2)),
+            sem((CHUNKS, 2)),
+            sem((CHUNKS, 2)),
+            sem((CHUNKS, 3, 2)),
+            sem((CHUNKS, 2)),
+        ],
+        compiler_params=pltpu.CompilerParams(
+            collective_id=0, has_side_effects=True, vmem_limit_bytes=63 * 2**20
+        ),
+    )(
+        normed.reshape(8, 2, CHUNKS, SUB, 256),
+        w_own,
+        w_sib,
+        residual.reshape(CHUNKS, SUB, width),
+        gain.reshape(1, width),
+        w_qkv,
+    )
+    return hidden.reshape(CHUNKS * SUB, width), qkv.reshape(16 * CHUNKS * SUB, out_cols)
 
 
 def on_device(residual, q_win, kv_win, lam_win, gn_gain, w_out_a, norm_gain, w_qkv):
@@ -177,23 +427,13 @@
         - jnp.exp(jnp.sum(lam_win[2] * lam_win[3]))
         + LAMBDA_INIT
     )
+    w_sib = lax.ppermute(w_out_a, "head", [(i, i ^ 1) for i in range(lax.axis_size("head"))])
     kv_here = kv_win.reshape(tokens_here, 512)
     blocks = [kv_here] + [passed_along(kv_here, "ctx", behind) for behind in (1, 2, 3, 4)]
     normed = window_attention(q_win.reshape(tokens_here, 256), blocks, lambda_full, gn_gain)
-    w_flat = w_qkv.reshape(w_qkv.shape[0], -1)
-    summed_out = lax.psum_scatter(
-        jnp.dot(normed, w_out_a, preferred_element_type=jnp.float32).astype(jnp.bfloat16),
-        "head",
-        scatter_dimension=0,
-        tiled=True,
-    ).astype(jnp.float32)
-    h_rows = (residual.astype(jnp.float32) + summed_out).astype(jnp.bfloat16)
-    normal_rows = rms_rows(h_rows, norm_gain)
-    qkv = jnp.dot(
-        lax.all_gather(normal_rows, "head", axis=0, tiled=True),
-        w_flat,
-        preferred_element_type=jnp.float32,
-    ).astype(jnp.bfloat16)
+    h_rows, qkv = project_and_spread(
+        normed, w_out_a, w_sib, residual, norm_gain, w_qkv.reshape(w_qkv.shape[0], -1)
+    )
     kv_next = qkv[:, 256:]
     next_blocks = [kv_next] + [passed_along(kv_next, "ctx", behind) for behind in (1, 2)]
     part_out, log_out = cycle_attention(qkv[:, :256], next_blocks)

time: 507 us -> 418 us (0.82)
  the two profiles are of different devices: /device:TPU:24 before, /device:TPU:40 now
where the time goes in v2:
time: 418 us; the launch traced here: 417 us
  Pallas kernels  206 us (49%)
  waiting for transfers between devices  108 us (26%)
  starting transfers between devices  54.9 us (13%)
  local copies, waits for them, and re-layouts  44.1 us (11%)
    pallas_call x1, Pallas kernels, project_and_spread(): pl.pallas_call(functools.partial(mid_kernel, x_cols), name='project_and_s...  158 us
    ppermute x6, waiting for transfers between devices, passed_along(): return lax.ppermute(block, axis, route)  108 us
    ppermute x6, starting transfers between devices, passed_along(): return lax.ppermute(block, axis, route)  54.8 us
    pallas_call x1, Pallas kernels, window_attention(): pl.pallas_call(window_kernel, name='window', grid=(tokens // ROWS,), out_...  30.5 us
    unnamed x13, local copies, waits for them, and re-layouts  25.1 us
    pallas_call x1, Pallas kernels, cycle_attention(): pl.pallas_call(cycle_kernel, name='cycle', grid=(tokens // ROWS,), out_sh...  17.7 us
    reshape x1, local copies, waits for them, and re-layouts, on_device(): w_qkv.reshape(w_qkv.shape[0], -1)  16.6 us
  transfers between devices with their start and end apart: 7, of which 4 were waited for; matrix products, arithmetic and copies ran while one was open for 9% of the time, Pallas kernels for 7%

profile of v2, /device:TPU:40, one launch (start us, length us, event | category | flops | bytes accessed | tf_op | source)
XLA Modules:
  0.0 416.6 jit_solution(5670541635226344110)
XLA Ops:
  0.6 0.1 collective-permute-start.4
  0.7 1.4 copy.18
  2.2 3.8 collective-permute-start
  6.0 2.4 collective-permute-start.1
  8.4 1.3 collective-permute-start.2
  9.7 1.3 collective-permute-start.3
  11.0 1.4 multiply_reduce_fusion
  13.8 16.7 %copy.14 = bf16[8192,1,3,256]{0,3,2,1:T(8,128)(2,1)} copy(bf16[8192,1,3,256]{3,0,2,1:T(8,128)(2,1)} %param.15) | data formatting | bytes 25165824 | tf_op args[7]
  30.5 0.0 copy-start.2
  30.5 16.6 %copy.15.w_qkv_hbm = bf16[8192,768]{1,0:T(8,128)(2,1)} copy(bf16[8192,768]{0,1:T(8,128)(2,1)} %bitcast.24) | data formatting | bytes 25165824 | tf_op jit(solution)/shard_map/reshape | solution.py:435
  47.2 4.4 %collective-permute-done.refs_1_ = bf16[1024,512]{1,0:T(8,128)(2,1)S(1)} collective-permute-done((bf16[1024,512]{1,0:T(8,128)(2,1)S(1)}, bf16[1024,512]{1,0:T(8,128)(2,1)S(1)}, u32[]{:S(2)}, u32[]{:S(2)}) %collective-permute-start) | collective-permute-done | bytes 1048608 | tf_op jit(solution)/shard_map/ppermute | solution.py:25
  51.6 41.4 %collective-permute-done.1.refs_2_ = bf16[1024,512]{1,0:T(8,128)(2,1)S(1)} collective-permute-done((bf16[1024,512]{1,0:T(8,128)(2,1)S(1)}, bf16[1024,512]{1,0:T(8,128)(2,1)S(1)}, u32[]{:S(2)}, u32[]{:S(2)}) %collective-permute-start.1) | collective-permute-done | bytes 1048608 | tf_op jit(solution)/shard_map/ppermute | solution.py:25
  93.0 2.5 collective-permute-done.2.refs_3_
  95.5 0.0 collective-permute-done.3.refs_4_
  95.5 0.0 copy-done.2
  95.5 0.0 copy-start.1
  95.5 1.0 copy-done.1
  96.5 30.5 %window.1 = bf16[1024,256]{1,0:T(8,128)(2,1)S(1)} custom-call(f32[1]{0:T(128)} %bitcast.lam_ref, bf16[1024,256]{1,0:T(8,128)(2,1)S(1)} %bitcast.21, f32[1,256]{1,0:T(1,128)S(1)} %bitcast.23, bf16[1024,512]{1,0:T(8,128)(2,1)S(1)} %bitcast.18, bf16[1024,512]{1,0:T(8,128)(2,1)S(1)} %collective-permute-done.refs_1_, ...), custom_call_target="tpu_custom_call" | custom-call | tf_op jit(solution)/shard_map/window/pallas_call | solution.py:92
  127.0 0.0 copy-start
  127.0 0.8 copy-done
  127.8 0.0 collective-permute-done.4.w_sib_hbm
  127.8 158.3 %project_and_spread.1 = (bf16[4,16,8192]{2,1,0:T(8,128)(2,1)}, bf16[16,4,16,768]{3,2,1,0:T(8,128)(2,1)}) custom-call(bf16[8,2,4,16,256]{4,3,2,1,0:T(8,128)(2,1)} %bitcast.20, bf16[256,8192]{1,0:T(8,128)(2,1)} %w_own_hbm.1, bf16[256,8192]{1,0:T(8,128)(2,1)} %collective-permute-done.4.w_sib_hbm, bf16[4,16,8192]{2,1,0:T(8,128)(2,1)} %bitcast.27, ...), custom_call_target="tpu_custom_call" | custom-call | tf_op jit(solution)/shard_map/project_and_spread/pallas_call | solution.py:374
  286.1 1.3 slice.25.kv0_ref
  287.4 24.2 %collective-permute-start.5 = (bf16[1024,512]{1,0:T(8,128)(2,1)S(1)}, bf16[1024,512]{1,0:T(8,128)(2,1)S(1)}, u32[]{:S(2)}, u32[]{:S(2)}) collective-permute-start(bf16[1024,512]{1,0:T(8,128)(2,1)S(1)} %slice.25.kv0_ref), channel_id=1, source_target_pairs={{0,16},{16,32},{32,48},{48,64},{64,80},{80,96},{96,112},{1,17},{17... | collective-permute-start | bytes 3145736 | tf_op jit(solution)/shard_map/ppermute | solution.py:25
  311.6 21.8 %collective-permute-start.6 = (bf16[1024,512]{1,0:T(8,128)(2,1)S(1)}, bf16[1024,512]{1,0:T(8,128)(2,1)S(1)}, u32[]{:S(2)}, u32[]{:S(2)}) collective-permute-start(bf16[1024,512]{1,0:T(8,128)(2,1)S(1)} %slice.25.kv0_ref), channel_id=1, source_target_pairs={{0,32},{16,48},{32,64},{48,80},{64,96},{80,112},{1,33},{17,49},{33... | collective-permute-start | bytes 3145736 | tf_op jit(solution)/shard_map/ppermute | solution.py:25
  333.4 1.1 slice.24.q_ref
  334.5 0.0 copy-start.3
  334.5 0.0 collective-permute-done.5.kv1_ref
  334.5 59.3 %collective-permute-done.6.kv2_ref = bf16[1024,512]{1,0:T(8,128)(2,1)S(1)} collective-permute-done((bf16[1024,512]{1,0:T(8,128)(2,1)S(1)}, bf16[1024,512]{1,0:T(8,128)(2,1)S(1)}, u32[]{:S(2)}, u32[]{:S(2)}) %collective-permute-start.6) | collective-permute-done | bytes 1048608 | tf_op jit(solution)/shard_map/ppermute | solution.py:25
  393.8 17.7 %cycle.1 = (f32[2,1024,256]{2,1,0:T(8,128)S(1)}, f32[2,1024]{1,0:T(2,128)S(1)}) custom-call(bf16[1024,256]{1,0:T(8,128)(2,1)S(1)} %slice.24.q_ref, bf16[1024,512]{1,0:T(8,128)(2,1)S(1)} %slice.25.kv0_ref, bf16[1024,512]{1,0:T(8,128)(2,1)S(1)} %collective-permute-done.5.kv1_ref, bf16[1024,512]{1,0:T(8,128)(2,1)S(1)} %collective-permute-done.6.kv2_ref), custom_call_target="tpu_custom_call" | custom-call | tf_op jit(solution)/shard_map/cycle/pallas_call | solution.py:145
  411.5 3.5 copy.16
  415.0 0.6 copy.17
  415.6 0.0 copy-done.3
  415.6 1.0 copy.20
Async XLA Ops:
  0.6 127.2 %collective-permute-start.4 = (bf16[256,8192]{1,0:T(8,128)(2,1)}, bf16[256,8192]{1,0:T(8,128)(2,1)}, u32[]{:S(2)}, u32[]{:S(2)}) collective-permute-start(bf16[256,8192]{1,0:T(8,128)(2,1)} %w_own_hbm.1), channel_id=1, source_target_pairs={{0,1},{1,0},{2,3},{3,2},{4,5},{5,4},{6,7},{7,6},{8,9},{9,8},{10,11... | collective-permute-start | bytes 12582920 | tf_op jit(solution)/shard_map/ppermute | solution.py:430
  2.2 49.4 %collective-permute-start = (bf16[1024,512]{1,0:T(8,128)(2,1)S(1)}, bf16[1024,512]{1,0:T(8,128)(2,1)S(1)}, u32[]{:S(2)}, u32[]{:S(2)}) collective-permute-start(bf16[1024,512]{1,0:T(8,128)(2,1)S(1)} %bitcast.14), channel_id=1, source_target_pairs={{0,16},{16,32},{32,48},{48,64},{64,80},{80,96},{96,112},{1,17},{17... | collective-permute-start | bytes 3145736 | tf_op jit(solution)/shard_map/ppermute | solution.py:25
  6.0 86.9 %collective-permute-start.1 = (bf16[1024,512]{1,0:T(8,128)(2,1)S(1)}, bf16[1024,512]{1,0:T(8,128)(2,1)S(1)}, u32[]{:S(2)}, u32[]{:S(2)}) collective-permute-start(bf16[1024,512]{1,0:T(8,128)(2,1)S(1)} %bitcast.15), channel_id=1, source_target_pairs={{0,32},{16,48},{32,64},{48,80},{64,96},{80,112},{1,33},{17,49},{33... | collective-permute-start | bytes 3145736 | tf_op jit(solution)/shard_map/ppermute | solution.py:25
  8.4 87.1 %collective-permute-start.2 = (bf16[1024,512]{1,0:T(8,128)(2,1)S(1)}, bf16[1024,512]{1,0:T(8,128)(2,1)}, u32[]{:S(2)}, u32[]{:S(2)}) collective-permute-start(bf16[1024,512]{1,0:T(8,128)(2,1)S(1)} %bitcast.16), channel_id=1, source_target_pairs={{0,48},{16,64},{32,80},{48,96},{64,112},{1,49},{17,65},{33,81},{49... | collective-permute-start | bytes 3145736 | tf_op jit(solution)/shard_map/ppermute | solution.py:25
  9.7 85.8 %collective-permute-start.3 = (bf16[1024,512]{1,0:T(8,128)(2,1)S(1)}, bf16[1024,512]{1,0:T(8,128)(2,1)}, u32[]{:S(2)}, u32[]{:S(2)}) collective-permute-start(bf16[1024,512]{1,0:T(8,128)(2,1)S(1)} %bitcast.17), channel_id=1, source_target_pairs={{0,64},{16,80},{32,96},{48,112},{1,65},{17,81},{33,97},{49,113},{2... | collective-permute-start | bytes 3145736 | tf_op jit(solution)/shard_map/ppermute | solution.py:25
  30.5 64.9 %copy-start.2 = (f32[256]{0:T(256)S(1)}, f32[256]{0:T(256)}, u32[]{:S(2)}) copy-start(f32[256]{0:T(256)} %param.12) | copy-start | bytes 3076
  95.5 1.0 copy-start.1
  127.0 0.8 copy-start
  287.4 47.1 %collective-permute-start.5 = (bf16[1024,512]{1,0:T(8,128)(2,1)S(1)}, bf16[1024,512]{1,0:T(8,128)(2,1)S(1)}, u32[]{:S(2)}, u32[]{:S(2)}) collective-permute-start(bf16[1024,512]{1,0:T(8,128)(2,1)S(1)} %slice.25.kv0_ref), channel_id=1, source_target_pairs={{0,16},{16,32},{32,48},{48,64},{64,80},{80,96},{96,112},{1,17},{17... | collective-permute-start | bytes 3145736 | tf_op jit(solution)/shard_map/ppermute | solution.py:25
  311.6 82.2 %collective-permute-start.6 = (bf16[1024,512]{1,0:T(8,128)(2,1)S(1)}, bf16[1024,512]{1,0:T(8,128)(2,1)S(1)}, u32[]{:S(2)}, u32[]{:S(2)}) collective-permute-start(bf16[1024,512]{1,0:T(8,128)(2,1)S(1)} %slice.25.kv0_ref), channel_id=1, source_target_pairs={{0,32},{16,48},{32,64},{48,80},{64,96},{80,112},{1,33},{17,49},{33... | collective-permute-start | bytes 3145736 | tf_op jit(solution)/shard_map/ppermute | solution.py:25
  334.5 81.1 %copy-start.3 = (bf16[4,16,8192]{2,1,0:T(8,128)(2,1)S(1)}, bf16[4,16,8192]{2,1,0:T(8,128)(2,1)}, u32[]{:S(2)}) copy-start(bf16[4,16,8192]{2,1,0:T(8,128)(2,1)} %get-tuple-element.7) | copy-start | bytes 3145732

commit v3 on v2

--- a/solution.py
+++ b/solution.py
@@ -17,12 +17,7 @@
 NEG = -1e30
 ONES = 16
 ROWS = 256
-
-
-def passed_along(block, axis, distance):
-    devices = range(lax.axis_size(axis))
-    route = [(i - distance, i) for i in devices if i - distance in devices]
-    return lax.ppermute(block, axis, route)
+MESH = pl.DeviceIdType.MESH
 
 
 def with_ones(values):
@@ -53,80 +48,166 @@
         m_ref[j] = after
 
 
-def window_kernel(lam_ref, q_ref, gain_ref, *refs):
-    kv_refs, (out_ref, vt_ref, m_ref, acc_ref) = refs[:5], refs[5:]
-    number = pl.program_id(0)
-    ctx = lax.axis_index("ctx")
-
-    @pl.when(number == 0)
+PIECES = 4
+
+
+def window_kernel(
+    lam_ref, q_ref, gain_ref, kv_ref, out_ref, kv_in, q_scaled, vt_ref, m_ref, acc_ref, up_sem, ring_sem
+):
+    ctx, head = lax.axis_index("ctx"), lax.axis_index("head")
+    ring, z = ctx // 4, lax.rem(ctx, 4)
+    tokens = kv_ref.shape[0]
+    piece = tokens // PIECES
+    over = ((1 - ring) * 4 + z, head)
+
+    def along(e):
+        return (ring * 4 + lax.rem(z + e, 4), head)
+
+    def copy_up(n):
+        rows = pl.ds(n * piece, piece)
+        return pltpu.make_async_remote_copy(
+            src_ref=kv_ref.at[rows],
+            dst_ref=kv_in.at[3, rows],
+            send_sem=up_sem.at[n, 0],
+            recv_sem=up_sem.at[n, 1],
+            device_id=over,
+            device_id_type=MESH,
+        )
+
+    def copy_along(e, n, source):
+        rows = pl.ds(n * piece, piece)
+        return pltpu.make_async_remote_copy(
+            src_ref=source.at[rows],
+            dst_ref=kv_in.at[e - 1, rows],
+            send_sem=ring_sem.at[e - 1, n, 0],
+            recv_sem=ring_sem.at[e - 1, n, 1],
+            device_id=along(e),
+            device_id_type=MESH,
+        )
+
+    barrier = pltpu.get_barrier_semaphore()
+    for peer in (along(1), along(2), along(3), over):
+        pl.semaphore_signal(barrier, inc=1, device_id=peer, device_id_type=MESH)
+    pl.semaphore_wait(barrier, 4)
+
+    @pl.when(ring == 0)
     def _():
-        for n in range(5):
-            vt_ref[n] = with_ones(kv_refs[n][:, 256:])
-
-    queries = scaled_queries(q_ref[...])
+        for n in range(PIECES):
+            copy_up(n).start()
+
+    for e in (1, 3, 2):
+
+        @pl.when(z + e <= 3)
+        def _():
+            for n in range(PIECES):
+                copy_along(e, n, kv_ref).start()
+
+    q_scaled[...] = scaled_queries(q_ref[...])
     m_ref[...] = jnp.full_like(m_ref, NEG)
     acc_ref[...] = jnp.zeros_like(acc_ref)
-    tokens = kv_refs[0].shape[0]
-    key_pos = lax.broadcasted_iota(jnp.int32, (tokens, ROWS), 0)
-    row_pos = lax.broadcasted_iota(jnp.int32, (tokens, ROWS), 1) + number * ROWS
-    online_step(queries, kv_refs[0], vt_ref[0], m_ref, acc_ref, key_pos <= row_pos)
-    for n in range(1, 5):
-
-        @pl.when(ctx >= n)
+
+    def all_queries(keys, edge):
+        vt_ref[...] = with_ones(keys[:, 256:])
+
+        def some(i, carry):
+            rows = pl.ds(pl.multiple_of(i * ROWS, ROWS), ROWS)
+            mask = None
+            if edge is not None:
+                key_pos = lax.broadcasted_iota(jnp.int32, (tokens, ROWS), 0)
+                row_pos = lax.broadcasted_iota(jnp.int32, (tokens, ROWS), 1) + i * ROWS
+                mask = key_pos <= row_pos if edge == "own" else key_pos > row_pos
+            online_step(q_scaled[rows, :], keys, vt_ref[...], m_ref.at[i], acc_ref.at[i], mask)
+            return carry
+
+        lax.fori_loop(0, tokens // ROWS, some, 0)
+
+    all_queries(kv_ref, "own")
+
+    @pl.when(ring == 1)
+    def _():
+        for n in range(PIECES):
+            copy_up(n).wait_recv()
+            for e in (1, 3, 2):
+
+                @pl.when(z + e >= 4)
+                def _():
+                    copy_along(e, n, kv_in.at[3]).start()
+
+        all_queries(kv_in.at[3], "far")
+
+    for e in (1, 3, 2):
+
+        @pl.when(ctx >= e)
         def _():
-            online_step(
-                queries, kv_refs[n], vt_ref[n], m_ref, acc_ref, key_pos > row_pos if n == 4 else None
-            )
-
-    one = acc_ref[0, :256] / acc_ref[0, 256:257]
-    two = acc_ref[1, :256] / acc_ref[1, 256:257]
-    attended = one - lam_ref[0] * two
-    factor = lax.rsqrt(jnp.mean(attended * attended, axis=0, keepdims=True) + EPSILON)
-    normed = (attended * factor).T * (gain_ref[...] * (1.0 - LAMBDA_INIT))
-    out_ref[...] = normed.astype(jnp.bfloat16)
-
-
-def window_attention(queries, blocks, lam, gain):
+            for n in range(PIECES):
+                copy_along(e, n, kv_ref).wait_recv()
+            all_queries(kv_in.at[e - 1], None)
+
+    def finish(i, carry):
+        one = acc_ref[i, 0, :256] / acc_ref[i, 0, 256:257]
+        two = acc_ref[i, 1, :256] / acc_ref[i, 1, 256:257]
+        attended = one - lam_ref[0] * two
+        factor = lax.rsqrt(jnp.mean(attended * attended, axis=0, keepdims=True) + EPSILON)
+        normed = (attended * factor).T * (gain_ref[...] * (1.0 - LAMBDA_INIT))
+        out_ref[pl.ds(pl.multiple_of(i * ROWS, ROWS), ROWS), :] = normed.astype(jnp.bfloat16)
+        return carry
+
+    lax.fori_loop(0, tokens // ROWS, finish, 0)
+
+    @pl.when(ring == 0)
+    def _():
+        for n in range(PIECES):
+            copy_up(n).wait_send()
+
+    for e in (1, 2, 3):
+
+        @pl.when((ring == 1) | (z + e <= 3))
+        def _():
+            for n in range(PIECES):
+                copy_along(e, n, kv_ref).wait_send()
+
+
+def window_attention(queries, keys_values, lam, gain):
     tokens = queries.shape[0]
-    whole = pl.BlockSpec((tokens, 512), lambda i: (0, 0))
+    vmem = pl.BlockSpec(memory_space=pltpu.VMEM)
     return pl.pallas_call(
         window_kernel,
         name="window",
-        grid=(tokens // ROWS,),
         out_shape=jax.ShapeDtypeStruct((tokens, 256), jnp.bfloat16),
-        in_specs=[
-            pl.BlockSpec(memory_space=pltpu.SMEM),
-            pl.BlockSpec((ROWS, 256), lambda i: (i, 0)),
-            pl.BlockSpec((1, 256), lambda i: (0, 0)),
-        ]
-        + [whole] * 5,
-        out_specs=pl.BlockSpec((ROWS, 256), lambda i: (i, 0)),
+        in_specs=[pl.BlockSpec(memory_space=pltpu.SMEM), vmem, vmem, vmem],
+        out_specs=vmem,
         scratch_shapes=[
-            pltpu.VMEM((5, 256 + ONES, tokens), jnp.bfloat16),
-            pltpu.VMEM((2, 1, ROWS), jnp.float32),
-            pltpu.VMEM((2, 256 + ONES, ROWS), jnp.float32),
+            pltpu.VMEM((4, tokens, 512), jnp.bfloat16),
+            pltpu.VMEM((tokens, 256), jnp.bfloat16),
+            pltpu.VMEM((256 + ONES, tokens), jnp.bfloat16),
+            pltpu.VMEM((tokens // ROWS, 2, 1, ROWS), jnp.float32),
+            pltpu.VMEM((tokens // ROWS, 2, 256 + ONES, ROWS), jnp.float32),
+            pltpu.SemaphoreType.DMA((PIECES, 2)),
+            pltpu.SemaphoreType.DMA((3, PIECES, 2)),
         ],
-        compiler_params=pltpu.CompilerParams(vmem_limit_bytes=48 * 2**20),
-    )(lam.reshape(1), queries, gain.reshape(1, 256), *blocks)
-
-
-def cycle_kernel(q_ref, kv0_ref, kv1_ref, kv2_ref, out_ref, log_ref, vt_ref, m_ref, acc_ref):
+        compiler_params=pltpu.CompilerParams(
+            collective_id=1, has_side_effects=True, vmem_limit_bytes=40 * 2**20
+        ),
+    )(lam.reshape(1), queries, gain.reshape(1, 256), keys_values)
+
+
+def cycle_kernel(qkv_ref, kv1_ref, kv2_ref, out_ref, log_ref, vt_ref, m_ref, acc_ref):
     number = pl.program_id(0)
     ctx = lax.axis_index("ctx")
-    kv_refs = (kv0_ref, kv1_ref, kv2_ref)
+    kv_refs = (qkv_ref.at[:, 256:], kv1_ref, kv2_ref)
 
     @pl.when(number == 0)
     def _():
         for n in range(3):
             vt_ref[n] = with_ones(kv_refs[n][:, 256:])
 
-    queries = scaled_queries(q_ref[...])
+    queries = scaled_queries(qkv_ref[pl.ds(pl.multiple_of(number * ROWS, ROWS), ROWS), :256])
     m_ref[...] = jnp.full_like(m_ref, NEG)
     acc_ref[...] = jnp.zeros_like(acc_ref)
-    tokens = kv0_ref.shape[0]
+    tokens = kv1_ref.shape[0]
     key_pos = lax.broadcasted_iota(jnp.int32, (tokens, ROWS), 0)
     row_pos = lax.broadcasted_iota(jnp.int32, (tokens, ROWS), 1) + number * ROWS
-    online_step(queries, kv0_ref, vt_ref[0], m_ref, acc_ref, key_pos <= row_pos)
+    online_step(queries, kv_refs[0], vt_ref[0], m_ref, acc_ref, key_pos <= row_pos)
     for n in (1, 2):
 
         @pl.when(ctx >= n)
@@ -135,24 +216,26 @@
 
     for j in range(2):
         total = acc_ref[j, 256:257]
-        out_ref[j] = (acc_ref[j, :256] / total).T
+        value = (acc_ref[j, :256] / total).T
+        for half in range(2):
+            out_ref[j, pl.ds(half, ROWS, stride=2), :] = value[:, half * 128 : half * 128 + 128]
         log_ref[j : j + 1, :] = (m_ref[j] + jnp.log2(total)) * LN2
 
 
-def cycle_attention(queries, blocks):
-    tokens = queries.shape[0]
+def cycle_attention(qkv, blocks):
+    tokens = qkv.shape[0]
     whole = pl.BlockSpec((tokens, 512), lambda i: (0, 0))
     return pl.pallas_call(
         cycle_kernel,
         name="cycle",
         grid=(tokens // ROWS,),
         out_shape=(
-            jax.ShapeDtypeStruct((2, tokens, 256), jnp.float32),
+            jax.ShapeDtypeStruct((2, 2 * tokens, 128), jnp.float32),
             jax.ShapeDtypeStruct((2, tokens), jnp.float32),
         ),
-        in_specs=[pl.BlockSpec((ROWS, 256), lambda i: (i, 0))] + [whole] * 3,
+        in_specs=[pl.BlockSpec((tokens, 768), lambda i: (0, 0))] + [whole] * 2,
         out_specs=(
-            pl.BlockSpec((2, ROWS, 256), lambda i: (0, i, 0)),
+            pl.BlockSpec((2, 2 * ROWS, 128), lambda i: (0, i, 0)),
             pl.BlockSpec((2, ROWS), lambda i: (0, i)),
         ),
         scratch_shapes=[
@@ -160,11 +243,10 @@
             pltpu.VMEM((2, 1, ROWS), jnp.float32),
             pltpu.VMEM((2, 256 + ONES, ROWS), jnp.float32),
         ],
-        compiler_params=pltpu.CompilerParams(vmem_limit_bytes=48 * 2**20),
-    )(queries, *blocks)
-
-
-MESH = pl.DeviceIdType.MESH
+        compiler_params=pltpu.CompilerParams(vmem_limit_bytes=40 * 2**20),
+    )(qkv, *blocks)
+
+
 CHUNKS = 4
 SUB = 16
 
@@ -184,6 +266,8 @@
     w_qkv_hbm,
     hidden_ref,
     qkv_ref,
+    kv1_ref,
+    kv2_ref,
     w_own,
     w_sib,
     w_qkv,
@@ -208,6 +292,7 @@
     g1_sem,
     g2_sem,
     s_sem,
+    next_sem,
 ):
     ctx, x, y, core = place()
     width = w_own.shape[1]
@@ -229,9 +314,10 @@
         load.start()
 
     barrier = pltpu.get_barrier_semaphore()
-    for peer in (across(1), across(2), across(3), over_y, sibling):
+    later = [(lax.rem(ctx + d, 8), lax.axis_index("head")) for d in (1, 2, 6, 7)]
+    for peer in [across(1), across(2), across(3), over_y, sibling] + later:
         pl.semaphore_signal(barrier, inc=1, device_id=peer, device_id_type=MESH)
-    pl.semaphore_wait(barrier, 5)
+    pl.semaphore_wait(barrier, 9)
 
     started = []
 
@@ -347,12 +433,31 @@
         def depth(j, carry):
             span = pl.ds(pl.multiple_of(j * tile, tile), tile)
             rows = rows_all[r, :, :, :, :, span].reshape(16 * SUB, tile)
-            acc[...] += jnp.dot(rows, w_qkv[span, :], preferred_element_type=jnp.float32)
+            for n in range(3):
+                acc[n] += jnp.dot(rows, w_qkv[n, span], preferred_element_type=jnp.float32)
             return carry
 
         acc[...] = jnp.zeros_like(acc)
         lax.fori_loop(0, width // tile, depth, 0)
-        qkv_ref[:, r] = acc[...].astype(jnp.bfloat16).reshape(16, SUB, acc.shape[1])
+        for n in range(3):
+            qkv_ref[:, r, :, n * 256 : n * 256 + 256] = (
+                acc[n].astype(jnp.bfloat16).reshape(16, SUB, 256)
+            )
+        for d in (1, 2):
+
+            @pl.when(ctx + d <= 7)
+            def _():
+                next_copy(d, r).start()
+
+    def next_copy(d, r):
+        return pltpu.make_async_remote_copy(
+            src_ref=qkv_ref.at[:, r, :, 256:],
+            dst_ref=(kv1_ref, kv2_ref)[d - 1].at[:, r],
+            send_sem=next_sem.at[d - 1, r, 0],
+            recv_sem=next_sem.at[d - 1, r, 1],
+            device_id=later[d - 1],
+            device_id_type=MESH,
+        )
 
     stages = [stage_a, stage_b, stage_c, stage_d, stage_e, stage_f]
     for step in range(CHUNKS - 1 + len(stages)):
@@ -361,29 +466,42 @@
                 stages[step - r](r)
     for copy in started:
         copy.wait_send()
+    for d in (1, 2):
+
+        @pl.when(ctx + d <= 7)
+        def _():
+            for r in range(CHUNKS):
+                next_copy(d, r).wait_send()
+
+        @pl.when(ctx >= d)
+        def _():
+            for r in range(CHUNKS):
+                next_copy(d, r).wait_recv()
 
 
 def project_and_spread(normed, w_own, w_sib, residual, gain, w_qkv):
     width = w_own.shape[1]
     x_cols = width * 13 // 32
-    out_cols = w_qkv.shape[1]
+    out_cols = 768
     bf16 = jnp.bfloat16
     any_space = pl.BlockSpec(memory_space=pl.ANY)
     vmem = pl.BlockSpec(memory_space=pltpu.VMEM)
     sem = pltpu.SemaphoreType.DMA
-    hidden, qkv = pl.pallas_call(
+    hidden, qkv, kv1, kv2 = pl.pallas_call(
         functools.partial(mid_kernel, x_cols),
         name="project_and_spread",
         out_shape=(
             jax.ShapeDtypeStruct((CHUNKS, SUB, width), bf16),
             jax.ShapeDtypeStruct((16, CHUNKS, SUB, out_cols), bf16),
+            jax.ShapeDtypeStruct((16, CHUNKS, SUB, 512), bf16),
+            jax.ShapeDtypeStruct((16, CHUNKS, SUB, 512), bf16),
         ),
         in_specs=[vmem, any_space, any_space, vmem, vmem, any_space],
-        out_specs=(vmem, vmem),
+        out_specs=(vmem, vmem, any_space, any_space),
         scratch_shapes=[
             pltpu.VMEM((256, width), bf16),
             pltpu.VMEM((256, width), bf16),
-            pltpu.VMEM((width, out_cols), bf16),
+            pltpu.VMEM((3, width, 256), bf16),
             pltpu.VMEM((8, CHUNKS, SUB, 256), bf16),
             pltpu.VMEM((CHUNKS, 4, 2, SUB, width), bf16),
             pltpu.VMEM((CHUNKS, 3, 2, SUB, x_cols), bf16),
@@ -393,7 +511,7 @@
             pltpu.VMEM((CHUNKS, 3, SUB, width - x_cols), bf16),
             pltpu.VMEM((CHUNKS, 3, SUB, width - x_cols), bf16),
             pltpu.VMEM((CHUNKS, 4, 2, 2, SUB, width), bf16),
-            pltpu.VMEM((16 * SUB, out_cols), jnp.float32),
+            pltpu.VMEM((3, 16 * SUB, 256), jnp.float32),
             sem((3,)),
             sem((2,)),
             sem((CHUNKS, 3, 2)),
@@ -405,6 +523,7 @@
             sem((CHUNKS, 2)),
             sem((CHUNKS, 3, 2)),
             sem((CHUNKS, 2)),
+            sem((2, CHUNKS, 2)),
         ],
         compiler_params=pltpu.CompilerParams(
             collective_id=0, has_side_effects=True, vmem_limit_bytes=63 * 2**20
@@ -417,7 +536,12 @@
         gain.reshape(1, width),
         w_qkv,
     )
-    return hidden.reshape(CHUNKS * SUB, width), qkv.reshape(16 * CHUNKS * SUB, out_cols)
+    tokens = 16 * CHUNKS * SUB
+    return (
+        hidden.reshape(CHUNKS * SUB, width),
+        qkv.reshape(tokens, out_cols),
+        (kv1.reshape(tokens, 512), kv2.reshape(tokens, 512)),
+    )
 
 
 def on_device(residual, q_win, kv_win, lam_win, gn_gain, w_out_a, norm_gain, w_qkv):
@@ -428,15 +552,13 @@
         + LAMBDA_INIT
     )
     w_sib = lax.ppermute(w_out_a, "head", [(i, i ^ 1) for i in range(lax.axis_size("head"))])
-    kv_here = kv_win.reshape(tokens_here, 512)
-    blocks = [kv_here] + [passed_along(kv_here, "ctx", behind) for behind in (1, 2, 3, 4)]
-    normed = window_attention(q_win.reshape(tokens_here, 256), blocks, lambda_full, gn_gain)
-    h_rows, qkv = project_and_spread(
-        normed, w_out_a, w_sib, residual, norm_gain, w_qkv.reshape(w_qkv.shape[0], -1)
-    )
-    kv_next = qkv[:, 256:]
-    next_blocks = [kv_next] + [passed_along(kv_next, "ctx", behind) for behind in (1, 2)]
-    part_out, log_out = cycle_attention(qkv[:, :256], next_blocks)
+    normed = window_attention(
+        q_win.reshape(tokens_here, 256), kv_win.reshape(tokens_here, 512), lambda_full, gn_gain
+    )
+    h_rows, qkv, blocks = project_and_spread(
+        normed, w_out_a, w_sib, residual, norm_gain, w_qkv[:, 0].transpose(1, 0, 2)
+    )
+    part_out, log_out = cycle_attention(qkv, blocks)
     return (
         h_rows,
         part_out.reshape(2, tokens_here, 1, 256),

time: 418 us -> 295 us (0.71)
  the two profiles are of different devices: /device:TPU:40 before, /device:TPU:24 now
where the time goes in v3:
time: 295 us; the launch traced here: 289 us
  Pallas kernels  276 us (94%)
  local copies, waits for them, and re-layouts  9.38 us (3%)
    pallas_call x1, Pallas kernels, project_and_spread(): pl.pallas_call(functools.partial(mid_kernel, x_cols), name='project_and_s...  181 us
    pallas_call x1, Pallas kernels, window_attention(): pl.pallas_call(window_kernel, name='window', out_shape=jax.ShapeDtypeStru...  76.2 us
    pallas_call x1, Pallas kernels, cycle_attention(): pl.pallas_call(cycle_kernel, name='cycle', grid=(tokens // ROWS,), out_sh...  18.4 us
    unnamed x17, local copies, waits for them, and re-layouts  9.38 us
  transfers between devices with their start and end apart: 1, of which 0 were waited for; matrix products, arithmetic and copies ran while one was open for 1% of the time, Pallas kernels for 26%

profile of v3, /device:TPU:24, one launch (start us, length us, event | category | flops | bytes accessed | tf_op | source)
XLA Modules:
  0.0 289.1 jit_solution(15966676476567158774)
XLA Ops:
  0.6 0.1 collective-permute-start
  0.7 1.4 multiply_reduce_fusion
  3.5 1.5 copy.13
  5.0 0.0 copy-start.4
  5.0 1.0 copy-done.4
  6.1 0.0 copy-start.5
  6.1 0.7 copy-done.5
  6.7 76.2 %window.1 = bf16[1024,256]{1,0:T(8,128)(2,1)S(1)} custom-call(f32[1]{0:T(128)} %bitcast.lam_ref, bf16[1024,256]{1,0:T(8,128)(2,1)S(1)} %bitcast.23, f32[1,256]{1,0:T(1,128)S(1)} %bitcast.25, bf16[1024,512]{1,0:T(8,128)(2,1)S(1)} %bitcast.18), custom_call_target="tpu_custom_call" | custom-call | tf_op jit(solution)/shard_map/window/pallas_call | solution.py:173
  83.0 0.0 copy-start
  83.0 0.8 copy-done
  83.8 0.0 collective-permute-done.w_sib_hbm
  83.8 181.4 %project_and_spread.1 = (bf16[4,16,8192]{2,1,0:T(8,128)(2,1)}, bf16[16,4,16,768]{3,2,1,0:T(8,128)(2,1)}, bf16[16,4,16,512]{3,2,1,0:T(8,128)(2,1)}, bf16[16,4,16,512]{3,2,1,0:T(8,128)(2,1)}) custom-call(bf16[8,2,4,16,256]{4,3,2,1,0:T(8,128)(2,1)} %bitcast.19, bf16[256,8192]{1,0:T(8,128)(2,1)} %w_own_hbm.1, bf16[256,8192]{1,0:T(8,128)(2,1)} %collective-permute-done.w_sib_hbm, ...), custom_call_target="tpu_custom_call" | custom-call | tf_op jit(solution)/shard_map/project_and_spread/pallas_call | solution.py:490
  265.2 0.0 copy-start.1
  265.2 1.4 copy-done.1
  266.6 0.0 copy-start.2
  266.6 1.2 copy-done.2
  267.8 0.0 copy-start.3
  267.8 1.2 copy-done.3
  269.0 0.0 copy-start.6
  269.1 18.4 %cycle.1 = (f32[2,2048,128]{2,1,0:T(8,128)}, f32[2,1024]{1,0:T(2,128)S(1)}) custom-call(bf16[1024,768]{1,0:T(8,128)(2,1)S(1)} %bitcast.20, bf16[1024,512]{1,0:T(8,128)(2,1)S(1)} %bitcast.21, bf16[1024,512]{1,0:T(8,128)(2,1)S(1)} %bitcast.22), custom_call_target="tpu_custom_call" | custom-call | tf_op jit(solution)/shard_map/cycle/pallas_call | solution.py:228
  287.5 0.6 copy.12
  288.1 0.0 copy-done.6
  288.1 1.0 copy.15
Async XLA Ops:
  0.6 83.1 %collective-permute-start = (bf16[256,8192]{1,0:T(8,128)(2,1)}, bf16[256,8192]{1,0:T(8,128)(2,1)}, u32[]{:S(2)}, u32[]{:S(2)}) collective-permute-start(bf16[256,8192]{1,0:T(8,128)(2,1)} %w_own_hbm.1), channel_id=1, source_target_pairs={{0,1},{1,0},{2,3},{3,2},{4,5},{5,4},{6,7},{7,6},{8,9},{9,8},{10,11... | collective-permute-start | bytes 12582920 | tf_op jit(solution)/shard_map/ppermute | solution.py:554
  5.0 1.0 copy-start.4
  6.1 0.7 copy-start.5
  83.0 0.8 copy-start
  265.2 1.4 copy-start.1
  266.6 1.2 copy-start.2
  267.8 1.2 copy-start.3
  269.0 19.0 %copy-start.6 = (bf16[4,16,8192]{2,1,0:T(8,128)(2,1)S(1)}, bf16[4,16,8192]{2,1,0:T(8,128)(2,1)}, u32[]{:S(2)}) copy-start(bf16[4,16,8192]{2,1,0:T(8,128)(2,1)} %get-tuple-element.9) | copy-start | bytes 3145732

commit v4 on v3

--- a/solution.py
+++ b/solution.py
@@ -95,12 +95,19 @@
         for n in range(PIECES):
             copy_up(n).start()
 
-    for e in (1, 3, 2):
-
+    def send_own(e):
         @pl.when(z + e <= 3)
         def _():
             for n in range(PIECES):
                 copy_along(e, n, kv_ref).start()
+
+    def send_on(e, n):
+        @pl.when(z + e >= 4)
+        def _():
+            copy_along(e, n, kv_in.at[3]).start()
+
+    send_own(1)
+    send_own(3)
 
     q_scaled[...] = scaled_queries(q_ref[...])
     m_ref[...] = jnp.full_like(m_ref, NEG)
@@ -127,12 +134,15 @@
     def _():
         for n in range(PIECES):
             copy_up(n).wait_recv()
-            for e in (1, 3, 2):
-
-                @pl.when(z + e >= 4)
-                def _():
-                    copy_along(e, n, kv_in.at[3]).start()
-
+            send_on(3, n)
+            send_on(1, n)
+        for n in range(PIECES):
+            send_on(2, n)
+
+    send_own(2)
+
+    @pl.when(ring == 1)
+    def _():
         all_queries(kv_in.at[3], "far")
 
     for e in (1, 3, 2):
@@ -143,10 +153,17 @@
                 copy_along(e, n, kv_ref).wait_recv()
             all_queries(kv_in.at[e - 1], None)
 
+    pairs = lam_ref[...]
+    lam = (
+        jnp.exp(jnp.sum(pairs[0:1] * pairs[1:2], axis=1, keepdims=True))
+        - jnp.exp(jnp.sum(pairs[2:3] * pairs[3:4], axis=1, keepdims=True))
+        + LAMBDA_INIT
+    )
+
     def finish(i, carry):
         one = acc_ref[i, 0, :256] / acc_ref[i, 0, 256:257]
         two = acc_ref[i, 1, :256] / acc_ref[i, 1, 256:257]
-        attended = one - lam_ref[0] * two
+        attended = one - lam * two
         factor = lax.rsqrt(jnp.mean(attended * attended, axis=0, keepdims=True) + EPSILON)
         normed = (attended * factor).T * (gain_ref[...] * (1.0 - LAMBDA_INIT))
         out_ref[pl.ds(pl.multiple_of(i * ROWS, ROWS), ROWS), :] = normed.astype(jnp.bfloat16)
@@ -167,14 +184,14 @@
                 copy_along(e, n, kv_ref).wait_send()
 
 
-def window_attention(queries, keys_values, lam, gain):
+def window_attention(queries, keys_values, lam_win, gain):
     tokens = queries.shape[0]
     vmem = pl.BlockSpec(memory_space=pltpu.VMEM)
     return pl.pallas_call(
         window_kernel,
         name="window",
         out_shape=jax.ShapeDtypeStruct((tokens, 256), jnp.bfloat16),
-        in_specs=[pl.BlockSpec(memory_space=pltpu.SMEM), vmem, vmem, vmem],
+        in_specs=[vmem] * 4,
         out_specs=vmem,
         scratch_shapes=[
             pltpu.VMEM((4, tokens, 512), jnp.bfloat16),
@@ -188,7 +205,7 @@
         compiler_params=pltpu.CompilerParams(
             collective_id=1, has_side_effects=True, vmem_limit_bytes=40 * 2**20
         ),
-    )(lam.reshape(1), queries, gain.reshape(1, 256), keys_values)
+    )(lam_win, queries, gain.reshape(1, 256), keys_values)
 
 
 def cycle_kernel(qkv_ref, kv1_ref, kv2_ref, out_ref, log_ref, vt_ref, m_ref, acc_ref):
@@ -256,6 +273,27 @@
     return lax.axis_index("ctx"), head // 4, (head // 2) % 2, head % 2
 
 
+KINDS = (
+    "normed",
+    "y1",
+    "x1_far",
+    "x1_near",
+    "x1_sum",
+    "x2",
+    "y2_far",
+    "y2_near",
+    "y2_sum",
+    "h1",
+    "h1_on",
+    "g1",
+    "h2",
+    "g2",
+    "g2_on",
+    "core",
+    "next",
+)
+
+
 def mid_kernel(
     x_cols,
     normed_ref,
@@ -273,36 +311,33 @@
     w_qkv,
     n_sib,
     part,
+    x1_far,
     x1_in,
     y1_in,
     x2_out,
     x2_in,
-    y2_out,
+    y2_far,
     y2_in,
     rows_all,
     acc,
     load_sem,
-    n_sem,
-    x1_sem,
-    x2_sem,
-    y1_sem,
-    y2_sem,
-    h1_sem,
-    h2_sem,
-    g1_sem,
-    g2_sem,
-    s_sem,
-    next_sem,
+    sems,
 ):
     ctx, x, y, core = place()
     width = w_own.shape[1]
-    low, high = pl.ds(0, x_cols), pl.ds(x_cols, width - x_cols)
-
-    def across(d):
-        return (ctx, lax.rem(x + d, 4) * 4 + y * 2 + core)
-
+    y_cols = width - x_cols
+    low, high = pl.ds(0, x_cols), pl.ds(x_cols, y_cols)
+    low_half = (pl.ds(0, x_cols // 2), pl.ds(x_cols // 2, x_cols // 2))
+    high_half = (pl.ds(x_cols, y_cols // 2), pl.ds(x_cols + y_cols // 2, y_cols // 2))
+    y_half = (pl.ds(0, y_cols // 2), pl.ds(y_cols // 2, y_cols // 2))
+    head = lax.axis_index("head")
+    beside = (lax.rem(x + 1, 4), lax.rem(x + 3, 4))
+    opposite = lax.rem(x + 2, 4)
+    along = [(ctx, place_x * 4 + y * 2 + core) for place_x in beside]
     over_y = (ctx, x * 4 + (1 - y) * 2 + core)
     sibling = (ctx, x * 4 + y * 2 + 1 - core)
+    blocks = lax.axis_size("ctx")
+    later = [(lax.rem(ctx + d, blocks), head) for d in (1, 2, blocks - 2, blocks - 1)]
 
     loads = [
         pltpu.make_async_copy(source, target, load_sem.at[n])
@@ -314,35 +349,45 @@
         load.start()
 
     barrier = pltpu.get_barrier_semaphore()
-    later = [(lax.rem(ctx + d, 8), lax.axis_index("head")) for d in (1, 2, 6, 7)]
-    for peer in [across(1), across(2), across(3), over_y, sibling] + later:
+    for peer in along + [over_y, sibling] + later:
         pl.semaphore_signal(barrier, inc=1, device_id=peer, device_id_type=MESH)
-    pl.semaphore_wait(barrier, 9)
+    pl.semaphore_wait(barrier, 8)
 
     started = []
-
-    def send(source, target, sems, device):
-        copy = pltpu.make_async_remote_copy(
+    pending = {}
+
+    def describe(kind, r, side, source, target, device):
+        kind = KINDS.index(kind)
+        return pltpu.make_async_remote_copy(
             src_ref=source,
             dst_ref=target,
-            send_sem=sems.at[0],
-            recv_sem=sems.at[1],
+            send_sem=sems.at[kind, r, side, 0],
+            recv_sem=sems.at[kind, r, side, 1],
             device_id=device,
             device_id_type=MESH,
         )
+
+    def send(kind, r, side, source, target, device):
+        copy = describe(kind, r, side, source, target, device)
         copy.start()
         started.append(copy)
-        return copy
-
-    n_copy = send(normed_ref.at[:, 1 - core], n_sib, n_sem, sibling)
+        pending[kind, r, side] = copy
+
+    def arrived(kind, r, sides=(0,)):
+        for side in sides:
+            pending[kind, r, side].wait_recv()
+
+    def wide(value):
+        return value.astype(jnp.float32)
+
+    both = (0, 1)
+    send("normed", 0, 0, normed_ref.at[:, 1 - core], n_sib, sibling)
     loads[0].wait()
     loads[1].wait()
-    n_copy.wait_recv()
-
-    state = [dict() for _ in range(CHUNKS)]
+    arrived("normed", 0)
     tile = min(1024, width)
 
-    def stage_a(r):
+    def project(r):
         own_rows = normed_ref[:, core, r].reshape(8 * SUB, 256)
         sib_rows = n_sib[:, r].reshape(8 * SUB, 256)
 
@@ -354,46 +399,56 @@
             return carry
 
         lax.fori_loop(0, width // tile, columns, 0)
-        state[r]["1"] = [
-            send(part.at[r, :, 1 - y, :, high], y1_in.at[r], y1_sem.at[r], over_y)
-        ] + [
-            send(
-                part.at[r, lax.rem(x + d, 4), :, :, low],
-                x1_in.at[r, d - 1],
-                x1_sem.at[r, d - 1],
-                across(d),
-            )
-            for d in (2, 1, 3)
-        ]
-
-    def wide(value):
-        return value.astype(jnp.float32)
-
-    def stage_b(r):
-        for copy in state[r]["1"]:
-            copy.wait_recv()
-        for d in (1, 2, 3):
-            other = lax.rem(x + d, 4)
-            y2_out[r, d - 1] = (
-                wide(part[r, other, y, :, high]) + wide(y1_in[r, other])
-            ).astype(jnp.bfloat16)
+        for s in both:
+            source = part.at[r, opposite, :, :, low_half[s]]
+            send("x1_far", r, s, source, x1_far.at[r, s], along[s])
+        send("y1", r, 0, part.at[r, :, 1 - y, :, high], y1_in.at[r], over_y)
+        for s in both:
+            source = part.at[r, beside[s], :, :, low_half[1 - s]]
+            send("x1_near", r, s, source, x1_in.at[r, s, :, :, low_half[1 - s]], along[s])
+
+    def relay_x1(r):
+        arrived("x1_far", r, both)
+        for s in both:
+            ours = part.at[r, beside[s], :, :, low_half[s]]
+            ours[...] = (wide(ours[...]) + wide(x1_far[r, s])).astype(jnp.bfloat16)
+            send("x1_sum", r, s, ours, x1_in.at[r, s, :, :, low_half[s]], along[s])
+
+    def second(r):
+        arrived("y1", r)
+        for place_x in (opposite,) + beside:
+            ours = part.at[r, place_x, y, :, high]
+            ours[...] = (wide(ours[...]) + wide(y1_in[r, place_x])).astype(jnp.bfloat16)
+        for s in both:
+            source = part.at[r, opposite, y, :, high_half[s]]
+            send("y2_far", r, s, source, y2_far.at[r, s], along[s])
+        for s in both:
+            source = part.at[r, beside[s], y, :, high_half[1 - s]]
+            send("y2_near", r, s, source, y2_in.at[r, s, :, y_half[1 - s]], along[s])
+        arrived("x1_near", r, both)
+        arrived("x1_sum", r, both)
         total = wide(part[r, x, 1 - y, :, low])
-        for d in (1, 2, 3):
-            total += wide(x1_in[r, d - 1, 1 - y])
+        for s in both:
+            total += wide(x1_in[r, s, 1 - y])
         x2_out[r] = total.astype(jnp.bfloat16)
-        state[r]["2"] = [send(x2_out.at[r], x2_in.at[r], x2_sem.at[r], over_y)] + [
-            send(y2_out.at[r, d - 1], y2_in.at[r, d - 1], y2_sem.at[r, d - 1], across(d))
-            for d in (2, 1, 3)
-        ]
-
-    def stage_c(r):
-        for copy in state[r]["2"]:
-            copy.wait_recv()
+        send("x2", r, 0, x2_out.at[r], x2_in.at[r], over_y)
+
+    def relay_y2(r):
+        arrived("y2_far", r, both)
+        for s in both:
+            ours = part.at[r, beside[s], y, :, high_half[s]]
+            ours[...] = (wide(ours[...]) + wide(y2_far[r, s])).astype(jnp.bfloat16)
+            send("y2_sum", r, s, ours, y2_in.at[r, s, :, y_half[s]], along[s])
+
+    def finish(r):
+        arrived("x2", r)
+        arrived("y2_near", r, both)
+        arrived("y2_sum", r, both)
         left = wide(part[r, x, y, :, low]) + wide(x2_in[r])
         right = wide(part[r, x, y, :, high]) + wide(y1_in[r, x])
-        for d in (1, 2, 3):
-            left += wide(x1_in[r, d - 1, y])
-            right += wide(y2_in[r, d - 1])
+        for s in both:
+            left += wide(x1_in[r, s, y])
+            right += wide(y2_in[r, s])
         left = (wide(residual_ref[r, :, low]) + left).astype(jnp.bfloat16)
         right = (wide(residual_ref[r, :, high]) + right).astype(jnp.bfloat16)
         hidden_ref[r, :, low] = left
@@ -405,28 +460,45 @@
         mine = rows_all.at[r, x, y, core]
         mine[:, low] = (left * factor * gain_ref[:, low]).astype(jnp.bfloat16)
         mine[:, high] = (right * factor * gain_ref[:, high]).astype(jnp.bfloat16)
-        state[r]["3"] = [send(mine.at[:, high], mine.at[:, high], g1_sem.at[r], over_y)] + [
-            send(mine.at[:, low], mine.at[:, low], h1_sem.at[r, d - 1], across(d))
-            for d in (2, 1, 3)
-        ]
-
-    def stage_d(r):
-        for copy in state[r]["3"]:
-            copy.wait_recv()
+        for s in both:
+            send("h1", r, s, mine.at[:, low], mine.at[:, low], along[s])
+        send("g1", r, 0, mine.at[:, high], mine.at[:, high], over_y)
+
+    def pass_h1(r):
+        arrived("h1", r, both)
+        for s in both:
+            came = rows_all.at[r, beside[1 - s], y, core, :, low_half[s]]
+            send("h1_on", r, s, came, came, along[s])
+
+    def spread(r):
+        arrived("g1", r)
+        column = rows_all.at[r, x, :, core, :, high]
+        for s in both:
+            send("g2", r, s, column, column, along[s])
+        arrived("h1_on", r, both)
         row = rows_all.at[r, :, y, core, :, low]
-        column = rows_all.at[r, x, :, core, :, high]
-        state[r]["4"] = [send(row, row, h2_sem.at[r], over_y)] + [
-            send(column, column, g2_sem.at[r, d - 1], across(d)) for d in (2, 1, 3)
-        ]
-
-    def stage_e(r):
-        for copy in state[r]["4"]:
-            copy.wait_recv()
-        ours = rows_all.at[r, :, :, core]
-        state[r]["5"] = send(ours, ours, s_sem.at[r], sibling)
-
-    def stage_f(r):
-        state[r]["5"].wait_recv()
+        send("h2", r, 0, row, row, over_y)
+
+    def pass_g2(r):
+        arrived("g2", r, both)
+        for s in both:
+            came = rows_all.at[r, beside[1 - s], :, core, :, high_half[s]]
+            send("g2_on", r, s, came, came, along[s])
+
+    def share(r):
+        arrived("h2", r)
+        ours = rows_all.at[r, :, :, core, :, low]
+        send("core", r, 0, ours, ours, sibling)
+        arrived("g2_on", r, both)
+        ours = rows_all.at[r, :, :, core, :, high]
+        send("core", r, 1, ours, ours, sibling)
+
+    def next_copy(d, r, source):
+        target = (kv1_ref, kv2_ref)[d - 1].at[:, r]
+        return describe("next", r, d - 1, source, target, later[d - 1])
+
+    def project_next(r):
+        arrived("core", r, both)
         if r == 0:
             loads[2].wait()
 
@@ -443,45 +515,71 @@
             qkv_ref[:, r, :, n * 256 : n * 256 + 256] = (
                 acc[n].astype(jnp.bfloat16).reshape(16, SUB, 256)
             )
-        for d in (1, 2):
-
-            @pl.when(ctx + d <= 7)
-            def _():
-                next_copy(d, r).start()
-
-    def next_copy(d, r):
-        return pltpu.make_async_remote_copy(
-            src_ref=qkv_ref.at[:, r, :, 256:],
-            dst_ref=(kv1_ref, kv2_ref)[d - 1].at[:, r],
-            send_sem=next_sem.at[d - 1, r, 0],
-            recv_sem=next_sem.at[d - 1, r, 1],
-            device_id=later[d - 1],
-            device_id_type=MESH,
-        )
-
-    stages = [stage_a, stage_b, stage_c, stage_d, stage_e, stage_f]
+        source = qkv_ref.at[:, r, :, 256:]
+
+        @pl.when(ctx <= 6)
+        def _():
+            next_copy(1, r, source).start()
+
+        @pl.when((ctx <= 5) & (ctx != 3))
+        def _():
+            next_copy(2, r, source).start()
+
+    def hand_on(r):
+        source = qkv_ref.at[:, r, :, 256:]
+
+        @pl.when(ctx >= 1)
+        def _():
+            next_copy(1, r, source).wait_recv()
+
+        @pl.when(ctx == 4)
+        def _():
+            copy = describe("next", r, 2, kv1_ref.at[:, r], kv2_ref.at[:, r], later[0])
+            copy.start()
+            copy.wait_send()
+
+        @pl.when(ctx == 5)
+        def _():
+            describe("next", r, 2, kv1_ref.at[:, r], kv2_ref.at[:, r], later[0]).wait_recv()
+
+    stages = [
+        project,
+        relay_x1,
+        second,
+        relay_y2,
+        finish,
+        pass_h1,
+        spread,
+        pass_g2,
+        share,
+        project_next,
+        hand_on,
+    ]
     for step in range(CHUNKS - 1 + len(stages)):
         for r in reversed(range(CHUNKS)):
             if 0 <= step - r < len(stages):
                 stages[step - r](r)
     for copy in started:
         copy.wait_send()
-    for d in (1, 2):
-
-        @pl.when(ctx + d <= 7)
-        def _():
-            for r in range(CHUNKS):
-                next_copy(d, r).wait_send()
-
-        @pl.when(ctx >= d)
-        def _():
-            for r in range(CHUNKS):
-                next_copy(d, r).wait_recv()
+    for r in range(CHUNKS):
+        source = qkv_ref.at[:, r, :, 256:]
+
+        @pl.when(ctx <= 6)
+        def _():
+            next_copy(1, r, source).wait_send()
+
+        @pl.when((ctx <= 5) & (ctx != 3))
+        def _():
+            next_copy(2, r, source).wait_send()
+
+        @pl.when((ctx >= 2) & (ctx != 5))
+        def _():
+            next_copy(2, r, source).wait_recv()
 
 
 def project_and_spread(normed, w_own, w_sib, residual, gain, w_qkv):
     width = w_own.shape[1]
-    x_cols = width * 13 // 32
+    x_cols = width * 5 // 8
     out_cols = 768
     bf16 = jnp.bfloat16
     any_space = pl.BlockSpec(memory_space=pl.ANY)
@@ -504,26 +602,17 @@
             pltpu.VMEM((3, width, 256), bf16),
             pltpu.VMEM((8, CHUNKS, SUB, 256), bf16),
             pltpu.VMEM((CHUNKS, 4, 2, SUB, width), bf16),
-            pltpu.VMEM((CHUNKS, 3, 2, SUB, x_cols), bf16),
+            pltpu.VMEM((CHUNKS, 2, 2, SUB, x_cols // 2), bf16),
+            pltpu.VMEM((CHUNKS, 2, 2, SUB, x_cols), bf16),
             pltpu.VMEM((CHUNKS, 4, SUB, width - x_cols), bf16),
             pltpu.VMEM((CHUNKS, SUB, x_cols), bf16),
             pltpu.VMEM((CHUNKS, SUB, x_cols), bf16),
-            pltpu.VMEM((CHUNKS, 3, SUB, width - x_cols), bf16),
-            pltpu.VMEM((CHUNKS, 3, SUB, width - x_cols), bf16),
+            pltpu.VMEM((CHUNKS, 2, SUB, (width - x_cols) // 2), bf16),
+            pltpu.VMEM((CHUNKS, 2, SUB, width - x_cols), bf16),
             pltpu.VMEM((CHUNKS, 4, 2, 2, SUB, width), bf16),
             pltpu.VMEM((3, 16 * SUB, 256), jnp.float32),
             sem((3,)),
-            sem((2,)),
-            sem((CHUNKS, 3, 2)),
-            sem((CHUNKS, 2)),
-            sem((CHUNKS, 2)),
-            sem((CHUNKS, 3, 2)),
-            sem((CHUNKS, 3, 2)),
-            sem((CHUNKS, 2)),
-            sem((CHUNKS, 2)),
-            sem((CHUNKS, 3, 2)),
-            sem((CHUNKS, 2)),
-            sem((2, CHUNKS, 2)),
+            sem((len(KINDS), CHUNKS, 3, 2)),
         ],
         compiler_params=pltpu.CompilerParams(
             collective_id=0, has_side_effects=True, vmem_limit_bytes=63 * 2**20
@@ -546,14 +635,9 @@
 
 def on_device(residual, q_win, kv_win, lam_win, gn_gain, w_out_a, norm_gain, w_qkv):
     tokens_here = q_win.shape[0]
-    lambda_full = (
-        jnp.exp(jnp.sum(lam_win[0] * lam_win[1]))
-        - jnp.exp(jnp.sum(lam_win[2] * lam_win[3]))
-        + LAMBDA_INIT
-    )
     w_sib = lax.ppermute(w_out_a, "head", [(i, i ^ 1) for i in range(lax.axis_size("head"))])
     normed = window_attention(
-        q_win.reshape(tokens_here, 256), kv_win.reshape(tokens_here, 512), lambda_full, gn_gain
+        q_win.reshape(tokens_here, 256), kv_win.reshape(tokens_here, 512), lam_win, gn_gain
     )
     h_rows, qkv, blocks = project_and_spread(
         normed, w_out_a, w_sib, residual, norm_gain, w_qkv[:, 0].transpose(1, 0, 2)

time: 295 us -> 312 us (1.058); the launches traced: 289 us -> 311 us
  Pallas kernels: 276 us -> 301 us
    pallas_call x1, Pallas kernels: 181 us -> 206 us  [project_and_spread(): pl.pallas_call(functools.partial(mid_kernel, x_cols), name='project_and_s...]
    unnamed x17 -> x19, local copies, waits for them, and re-layouts: 9.38 us -> 10.1 us
  transfers between devices with their start and end apart: 1 -> 1, of which waited for: 0 -> 0; matrix products, arithmetic and copies ran while one was open for 1% -> 0% of each run, Pallas kernels for 26% -> 25%
where the time goes in v4:
time: 312 us; the launch traced here: 311 us
  Pallas kernels  301 us (96%)
  local copies, waits for them, and re-layouts  10.1 us (3%)
    pallas_call x1, Pallas kernels, project_and_spread(): pl.pallas_call(functools.partial(mid_kernel, x_cols), name='project_and_s...  206 us
    pallas_call x1, Pallas kernels, window_attention(): pl.pallas_call(window_kernel, name='window', out_shape=jax.ShapeDtypeStru...  76.4 us
    pallas_call x1, Pallas kernels, cycle_attention(): pl.pallas_call(cycle_kernel, name='cycle', grid=(tokens // ROWS,), out_sh...  18.4 us
    unnamed x19, local copies, waits for them, and re-layouts  10.1 us
  transfers between devices with their start and end apart: 1, of which 0 were waited for; matrix products, arithmetic and copies ran while one was open for 0% of the time, Pallas kernels for 25%

profile of v4, /device:TPU:24, one launch (start us, length us, event | category | flops | bytes accessed | tf_op | source)
XLA Modules:
  0.0 311.4 jit_solution(14659062141228905117)
XLA Ops:
  0.6 0.1 collective-permute-start
  0.7 1.4 copy.13
  2.2 0.0 copy-start.4
  2.2 1.0 copy-done.4
  3.2 0.0 copy-start.5
  3.2 0.7 copy-done.5
  3.9 0.0 copy-start.6
  3.9 0.7 copy-done.6
  4.6 76.4 %window.1 = bf16[1024,256]{1,0:T(8,128)(2,1)S(1)} custom-call(f32[4,128]{1,0:T(4,128)S(1)} %copy-done.5, bf16[1024,256]{1,0:T(8,128)(2,1)S(1)} %bitcast.22, f32[1,256]{1,0:T(1,128)S(1)} %bitcast.24, bf16[1024,512]{1,0:T(8,128)(2,1)S(1)} %bitcast.17), custom_call_target="tpu_custom_call" | custom-call | tf_op jit(solution)/shard_map/window/pallas_call | solution.py:190
  81.0 0.0 copy-start
  81.0 0.8 copy-done
  81.8 0.0 collective-permute-done.w_sib_hbm
  81.8 205.8 %project_and_spread.1 = (bf16[4,16,8192]{2,1,0:T(8,128)(2,1)}, bf16[16,4,16,768]{3,2,1,0:T(8,128)(2,1)}, bf16[16,4,16,512]{3,2,1,0:T(8,128)(2,1)}, bf16[16,4,16,512]{3,2,1,0:T(8,128)(2,1)}) custom-call(bf16[8,2,4,16,256]{4,3,2,1,0:T(8,128)(2,1)} %bitcast.18, bf16[256,8192]{1,0:T(8,128)(2,1)} %w_own_hbm.1, bf16[256,8192]{1,0:T(8,128)(2,1)} %collective-permute-done.w_sib_hbm, ...), custom_call_target="tpu_custom_call" | custom-call | tf_op jit(solution)/shard_map/project_and_spread/pallas_call | solution.py:588
  287.6 0.0 copy-start.1
  287.6 1.4 copy-done.1
  289.0 0.0 copy-start.2
  289.0 1.2 copy-done.2
  290.2 0.0 copy-start.3
  290.2 1.2 copy-done.3
  291.4 0.0 copy-start.7
  291.4 18.4 %cycle.1 = (f32[2,2048,128]{2,1,0:T(8,128)}, f32[2,1024]{1,0:T(2,128)S(1)}) custom-call(bf16[1024,768]{1,0:T(8,128)(2,1)S(1)} %bitcast.19, bf16[1024,512]{1,0:T(8,128)(2,1)S(1)} %bitcast.20, bf16[1024,512]{1,0:T(8,128)(2,1)S(1)} %bitcast.21), custom_call_target="tpu_custom_call" | custom-call | tf_op jit(solution)/shard_map/cycle/pallas_call | solution.py:245
  309.8 0.6 copy.12
  310.5 0.0 copy-done.7
  310.5 1.0 copy.15
Async XLA Ops:
  0.6 81.2 %collective-permute-start = (bf16[256,8192]{1,0:T(8,128)(2,1)}, bf16[256,8192]{1,0:T(8,128)(2,1)}, u32[]{:S(2)}, u32[]{:S(2)}) collective-permute-start(bf16[256,8192]{1,0:T(8,128)(2,1)} %w_own_hbm.1), channel_id=1, source_target_pairs={{0,1},{1,0},{2,3},{3,2},{4,5},{5,4},{6,7},{7,6},{8,9},{9,8},{10,11... | collective-permute-start | bytes 12582920 | tf_op jit(solution)/shard_map/ppermute | solution.py:638
  2.2 1.0 copy-start.4
  3.2 0.7 copy-start.5
  3.9 0.7 copy-start.6
  81.0 0.8 copy-start
  287.6 1.4 copy-start.1
  289.0 1.2 copy-start.2
  290.2 1.2 copy-start.3
  291.4 19.0 %copy-start.7 = (bf16[4,16,8192]{2,1,0:T(8,128)(2,1)S(1)}, bf16[4,16,8192]{2,1,0:T(8,128)(2,1)}, u32[]{:S(2)}) copy-start(bf16[4,16,8192]{2,1,0:T(8,128)(2,1)} %get-tuple-element.9) | copy-start | bytes 3145732

commit v5 on v4

--- a/solution.py
+++ b/solution.py
@@ -48,11 +48,11 @@
         m_ref[j] = after
 
 
-PIECES = 4
+PIECES = 8
 
 
 def window_kernel(
-    lam_ref, q_ref, gain_ref, kv_ref, out_ref, kv_in, q_scaled, vt_ref, m_ref, acc_ref, up_sem, ring_sem
+    lam_ref, q_ref, gain_ref, kv_ref, out_ref, kv_in, q_scaled, vt_ref, m_ref, acc_ref, up_sem, ring_sem, on_sem
 ):
     ctx, head = lax.axis_index("ctx"), lax.axis_index("head")
     ring, z = ctx // 4, lax.rem(ctx, 4)
@@ -95,19 +95,28 @@
         for n in range(PIECES):
             copy_up(n).start()
 
-    def send_own(e):
+    def copy_on(side, n):
+        rows = pl.ds(n * piece, piece)
+        return pltpu.make_async_remote_copy(
+            src_ref=kv_in.at[2 * side, rows],
+            dst_ref=kv_in.at[1, rows],
+            send_sem=on_sem.at[side, n],
+            recv_sem=ring_sem.at[1, n, 1],
+            device_id=along(1 + 2 * side),
+            device_id_type=MESH,
+        )
+
+    def passes_on(side, n):
+        if side == 0:
+            return (z <= 2) & (ctx >= 1) if n % 2 == 0 else (z == 2)
+        return (ctx >= 3) & (z >= 1) if n % 2 == 1 else (ring == 1) & (z == 1)
+
+    for e in (1, 3):
+
         @pl.when(z + e <= 3)
         def _():
             for n in range(PIECES):
                 copy_along(e, n, kv_ref).start()
-
-    def send_on(e, n):
-        @pl.when(z + e >= 4)
-        def _():
-            copy_along(e, n, kv_in.at[3]).start()
-
-    send_own(1)
-    send_own(3)
 
     q_scaled[...] = scaled_queries(q_ref[...])
     m_ref[...] = jnp.full_like(m_ref, NEG)
@@ -134,12 +143,24 @@
     def _():
         for n in range(PIECES):
             copy_up(n).wait_recv()
-            send_on(3, n)
-            send_on(1, n)
+            for e in (3, 1):
+
+                @pl.when(z + e >= 4)
+                def _():
+                    copy_along(e, n, kv_in.at[3]).start()
+
+    for side in (0, 1):
+
+        @pl.when(ctx >= 1 + 2 * side)
+        def _():
+            for n in range(PIECES):
+                copy_along(1 + 2 * side, n, kv_ref).wait_recv()
+
         for n in range(PIECES):
-            send_on(2, n)
-
-    send_own(2)
+
+            @pl.when(passes_on(side, n))
+            def _():
+                copy_on(side, n).start()
 
     @pl.when(ring == 1)
     def _():
@@ -149,8 +170,9 @@
 
         @pl.when(ctx >= e)
         def _():
-            for n in range(PIECES):
-                copy_along(e, n, kv_ref).wait_recv()
+            if e == 2:
+                for n in range(PIECES):
+                    copy_along(2, n, kv_ref).wait_recv()
             all_queries(kv_in.at[e - 1], None)
 
     pairs = lam_ref[...]
@@ -176,12 +198,19 @@
         for n in range(PIECES):
             copy_up(n).wait_send()
 
-    for e in (1, 2, 3):
+    for e in (1, 3):
 
         @pl.when((ring == 1) | (z + e <= 3))
         def _():
             for n in range(PIECES):
                 copy_along(e, n, kv_ref).wait_send()
+
+    for side in (0, 1):
+        for n in range(PIECES):
+
+            @pl.when(passes_on(side, n))
+            def _():
+                copy_on(side, n).wait_send()
 
 
 def window_attention(queries, keys_values, lam_win, gain):
@@ -201,6 +230,7 @@
             pltpu.VMEM((tokens // ROWS, 2, 256 + ONES, ROWS), jnp.float32),
             pltpu.SemaphoreType.DMA((PIECES, 2)),
             pltpu.SemaphoreType.DMA((3, PIECES, 2)),
+            pltpu.SemaphoreType.DMA((2, PIECES)),
         ],
         compiler_params=pltpu.CompilerParams(
             collective_id=1, has_side_effects=True, vmem_limit_bytes=40 * 2**20
@@ -296,6 +326,7 @@
 
 def mid_kernel(
     x_cols,
+    g_cols,
     normed_ref,
     w_own_hbm,
     w_sib_hbm,
@@ -329,6 +360,11 @@
     low, high = pl.ds(0, x_cols), pl.ds(x_cols, y_cols)
     low_half = (pl.ds(0, x_cols // 2), pl.ds(x_cols // 2, x_cols // 2))
     high_half = (pl.ds(x_cols, y_cols // 2), pl.ds(x_cols + y_cols // 2, y_cols // 2))
+    g_low, g_high = pl.ds(0, g_cols), pl.ds(g_cols, width - g_cols)
+    g_low_half = (pl.ds(0, g_cols // 2), pl.ds(g_cols // 2, g_cols // 2))
+    g_high_half = tuple(
+        pl.ds(g_cols + s * ((width - g_cols) // 2), (width - g_cols) // 2) for s in (0, 1)
+    )
     y_half = (pl.ds(0, y_cols // 2), pl.ds(y_cols // 2, y_cols // 2))
     head = lax.axis_index("head")
     beside = (lax.rem(x + 1, 4), lax.rem(x + 3, 4))
@@ -461,36 +497,36 @@
         mine[:, low] = (left * factor * gain_ref[:, low]).astype(jnp.bfloat16)
         mine[:, high] = (right * factor * gain_ref[:, high]).astype(jnp.bfloat16)
         for s in both:
-            send("h1", r, s, mine.at[:, low], mine.at[:, low], along[s])
-        send("g1", r, 0, mine.at[:, high], mine.at[:, high], over_y)
+            send("h1", r, s, mine.at[:, g_low], mine.at[:, g_low], along[s])
+        send("g1", r, 0, mine.at[:, g_high], mine.at[:, g_high], over_y)
 
     def pass_h1(r):
         arrived("h1", r, both)
         for s in both:
-            came = rows_all.at[r, beside[1 - s], y, core, :, low_half[s]]
+            came = rows_all.at[r, beside[1 - s], y, core, :, g_low_half[s]]
             send("h1_on", r, s, came, came, along[s])
 
     def spread(r):
         arrived("g1", r)
-        column = rows_all.at[r, x, :, core, :, high]
+        column = rows_all.at[r, x, :, core, :, g_high]
         for s in both:
             send("g2", r, s, column, column, along[s])
         arrived("h1_on", r, both)
-        row = rows_all.at[r, :, y, core, :, low]
+        row = rows_all.at[r, :, y, core, :, g_low]
         send("h2", r, 0, row, row, over_y)
 
     def pass_g2(r):
         arrived("g2", r, both)
         for s in both:
-            came = rows_all.at[r, beside[1 - s], :, core, :, high_half[s]]
+            came = rows_all.at[r, beside[1 - s], :, core, :, g_high_half[s]]
             send("g2_on", r, s, came, came, along[s])
 
     def share(r):
         arrived("h2", r)
-        ours = rows_all.at[r, :, :, core, :, low]
+        ours = rows_all.at[r, :, :, core, :, g_low]
         send("core", r, 0, ours, ours, sibling)
         arrived("g2_on", r, both)
-        ours = rows_all.at[r, :, :, core, :, high]
+        ours = rows_all.at[r, :, :, core, :, g_high]
         send("core", r, 1, ours, ours, sibling)
 
     def next_copy(d, r, source):
@@ -521,26 +557,9 @@
         def _():
             next_copy(1, r, source).start()
 
-        @pl.when((ctx <= 5) & (ctx != 3))
+        @pl.when(ctx <= 5)
         def _():
             next_copy(2, r, source).start()
-
-    def hand_on(r):
-        source = qkv_ref.at[:, r, :, 256:]
-
-        @pl.when(ctx >= 1)
-        def _():
-            next_copy(1, r, source).wait_recv()
-
-        @pl.when(ctx == 4)
-        def _():
-            copy = describe("next", r, 2, kv1_ref.at[:, r], kv2_ref.at[:, r], later[0])
-            copy.start()
-            copy.wait_send()
-
-        @pl.when(ctx == 5)
-        def _():
-            describe("next", r, 2, kv1_ref.at[:, r], kv2_ref.at[:, r], later[0]).wait_recv()
 
     stages = [
         project,
@@ -553,7 +572,6 @@
         pass_g2,
         share,
         project_next,
-        hand_on,
     ]
     for step in range(CHUNKS - 1 + len(stages)):
         for r in reversed(range(CHUNKS)):
@@ -568,11 +586,15 @@
         def _():
             next_copy(1, r, source).wait_send()
 
-        @pl.when((ctx <= 5) & (ctx != 3))
+        @pl.when(ctx <= 5)
         def _():
             next_copy(2, r, source).wait_send()
 
-        @pl.when((ctx >= 2) & (ctx != 5))
+        @pl.when(ctx >= 1)
+        def _():
+            next_copy(1, r, source).wait_recv()
+
+        @pl.when(ctx >= 2)
         def _():
             next_copy(2, r, source).wait_recv()
 
@@ -580,13 +602,14 @@
 def project_and_spread(normed, w_own, w_sib, residual, gain, w_qkv):
     width = w_own.shape[1]
     x_cols = width * 5 // 8
+    g_cols = width * 3 // 8
     out_cols = 768
     bf16 = jnp.bfloat16
     any_space = pl.BlockSpec(memory_space=pl.ANY)
     vmem = pl.BlockSpec(memory_space=pltpu.VMEM)
     sem = pltpu.SemaphoreType.DMA
     hidden, qkv, kv1, kv2 = pl.pallas_call(
-        functools.partial(mid_kernel, x_cols),
+        functools.partial(mid_kernel, x_cols, g_cols),
         name="project_and_spread",
         out_shape=(
             jax.ShapeDtypeStruct((CHUNKS, SUB, width), bf16),
@@ -612,7 +635,7 @@
             pltpu.VMEM((CHUNKS, 4, 2, 2, SUB, width), bf16),
             pltpu.VMEM((3, 16 * SUB, 256), jnp.float32),
             sem((3,)),
-            sem((len(KINDS), CHUNKS, 3, 2)),
+            sem((len(KINDS), CHUNKS, 2, 2)),
         ],
         compiler_params=pltpu.CompilerParams(
             collective_id=0, has_side_effects=True, vmem_limit_bytes=63 * 2**20

time: 312 us -> 268 us (0.86)
  the two profiles are of different devices: /device:TPU:24 before, /device:TPU:57 now
where the time goes in v5:
time: 268 us; the launch traced here: 267 us
  Pallas kernels  256 us (96%)
  local copies, waits for them, and re-layouts  10.1 us (4%)
    pallas_call x1, Pallas kernels, project_and_spread(): pl.pallas_call(functools.partial(mid_kernel, x_cols, g_cols), name='proje...  180 us
    pallas_call x1, Pallas kernels, window_attention(): pl.pallas_call(window_kernel, name='window', out_shape=jax.ShapeDtypeStru...  57 us
    pallas_call x1, Pallas kernels, cycle_attention(): pl.pallas_call(cycle_kernel, name='cycle', grid=(tokens // ROWS,), out_sh...  18.4 us
    unnamed x19, local copies, waits for them, and re-layouts  10.1 us
  transfers between devices with their start and end apart: 1, of which 0 were waited for; matrix products, arithmetic and copies ran while one was open for 1% of the time, Pallas kernels for 21%

profile of v5, /device:TPU:57, one launch (start us, length us, event | category | flops | bytes accessed | tf_op | source)
XLA Modules:
  0.0 267.4 jit_solution(18072804308770950111)
XLA Ops:
  0.6 0.8 collective-permute-start
  1.4 1.4 copy.13
  2.8 0.0 copy-start.4
  2.9 1.0 copy-done.4
  3.9 0.0 copy-start.5
  3.9 0.7 copy-done.5
  4.6 0.0 copy-start.6
  4.6 0.7 copy-done.6
  5.2 57.0 %window.1 = bf16[1024,256]{1,0:T(8,128)(2,1)S(1)} custom-call(f32[4,128]{1,0:T(4,128)S(1)} %copy-done.5, bf16[1024,256]{1,0:T(8,128)(2,1)S(1)} %bitcast.22, f32[1,256]{1,0:T(1,128)S(1)} %bitcast.24, bf16[1024,512]{1,0:T(8,128)(2,1)S(1)} %bitcast.17), custom_call_target="tpu_custom_call" | custom-call | tf_op jit(solution)/shard_map/window/pallas_call | solution.py:219
  62.2 0.0 copy-start
  62.2 0.8 copy-done
  63.0 0.0 collective-permute-done.w_sib_hbm
  63.0 180.5 %project_and_spread.1 = (bf16[4,16,8192]{2,1,0:T(8,128)(2,1)}, bf16[16,4,16,768]{3,2,1,0:T(8,128)(2,1)}, bf16[16,4,16,512]{3,2,1,0:T(8,128)(2,1)}, bf16[16,4,16,512]{3,2,1,0:T(8,128)(2,1)}) custom-call(bf16[8,2,4,16,256]{4,3,2,1,0:T(8,128)(2,1)} %bitcast.18, bf16[256,8192]{1,0:T(8,128)(2,1)} %w_own_hbm.1, bf16[256,8192]{1,0:T(8,128)(2,1)} %collective-permute-done.w_sib_hbm, ...), custom_call_target="tpu_custom_call" | custom-call | tf_op jit(solution)/shard_map/project_and_spread/pallas_call | solution.py:611
  243.5 0.0 copy-start.1
  243.5 1.4 copy-done.1
  244.9 0.0 copy-start.2
  244.9 1.2 copy-done.2
  246.1 0.0 copy-start.3
  246.2 1.2 copy-done.3
  247.4 0.0 copy-start.7
  247.4 18.4 %cycle.1 = (f32[2,2048,128]{2,1,0:T(8,128)}, f32[2,1024]{1,0:T(2,128)S(1)}) custom-call(bf16[1024,768]{1,0:T(8,128)(2,1)S(1)} %bitcast.19, bf16[1024,512]{1,0:T(8,128)(2,1)S(1)} %bitcast.20, bf16[1024,512]{1,0:T(8,128)(2,1)S(1)} %bitcast.21), custom_call_target="tpu_custom_call" | custom-call | tf_op jit(solution)/shard_map/cycle/pallas_call | solution.py:275
  265.8 0.6 copy.12
  266.4 0.0 copy-done.7
  266.4 1.0 copy.15
Async XLA Ops:
  0.6 62.4 %collective-permute-start = (bf16[256,8192]{1,0:T(8,128)(2,1)}, bf16[256,8192]{1,0:T(8,128)(2,1)}, u32[]{:S(2)}, u32[]{:S(2)}) collective-permute-start(bf16[256,8192]{1,0:T(8,128)(2,1)} %w_own_hbm.1), channel_id=1, source_target_pairs={{0,1},{1,0},{2,3},{3,2},{4,5},{5,4},{6,7},{7,6},{8,9},{9,8},{10,11... | collective-permute-start | bytes 12582920 | tf_op jit(solution)/shard_map/ppermute | solution.py:661
  2.8 1.0 copy-start.4
  3.9 0.7 copy-start.5
  4.6 0.7 copy-start.6
  62.2 0.8 copy-start
  243.5 1.4 copy-start.1
  244.9 1.2 copy-start.2
  246.1 1.2 copy-start.3
  247.4 19.0 %copy-start.7 = (bf16[4,16,8192]{2,1,0:T(8,128)(2,1)S(1)}, bf16[4,16,8192]{2,1,0:T(8,128)(2,1)}, u32[]{:S(2)}) copy-start(bf16[4,16,8192]{2,1,0:T(8,128)(2,1)} %get-tuple-element.9) | copy-start | bytes 3145732

commit v6 on v5

--- a/solution.py
+++ b/solution.py
@@ -29,10 +29,10 @@
     return (picked.astype(jnp.float32) * SCALE).astype(jnp.bfloat16)
 
 
-def online_step(queries, keys, values_up, m_ref, acc_ref, mask):
+def online_step(queries, keys_of, values_up, m_ref, acc_ref, mask):
     for j in range(2):
         scores = lax.dot_general(
-            keys[:, j * HDIM : (j + 1) * HDIM],
+            keys_of(j),
             queries[:, j * HDIM : (j + 1) * HDIM],
             (((1,), (1,)), ((), ())),
             preferred_element_type=jnp.float32,
@@ -132,7 +132,14 @@
                 key_pos = lax.broadcasted_iota(jnp.int32, (tokens, ROWS), 0)
                 row_pos = lax.broadcasted_iota(jnp.int32, (tokens, ROWS), 1) + i * ROWS
                 mask = key_pos <= row_pos if edge == "own" else key_pos > row_pos
-            online_step(q_scaled[rows, :], keys, vt_ref[...], m_ref.at[i], acc_ref.at[i], mask)
+            online_step(
+                q_scaled[rows, :],
+                lambda j: keys[:, j * HDIM : (j + 1) * HDIM],
+                vt_ref[...],
+                m_ref.at[i],
+                acc_ref.at[i],
+                mask,
+            )
             return carry
 
         lax.fori_loop(0, tokens // ROWS, some, 0)
@@ -238,62 +245,6 @@
     )(lam_win, queries, gain.reshape(1, 256), keys_values)
 
 
-def cycle_kernel(qkv_ref, kv1_ref, kv2_ref, out_ref, log_ref, vt_ref, m_ref, acc_ref):
-    number = pl.program_id(0)
-    ctx = lax.axis_index("ctx")
-    kv_refs = (qkv_ref.at[:, 256:], kv1_ref, kv2_ref)
-
-    @pl.when(number == 0)
-    def _():
-        for n in range(3):
-            vt_ref[n] = with_ones(kv_refs[n][:, 256:])
-
-    queries = scaled_queries(qkv_ref[pl.ds(pl.multiple_of(number * ROWS, ROWS), ROWS), :256])
-    m_ref[...] = jnp.full_like(m_ref, NEG)
-    acc_ref[...] = jnp.zeros_like(acc_ref)
-    tokens = kv1_ref.shape[0]
-    key_pos = lax.broadcasted_iota(jnp.int32, (tokens, ROWS), 0)
-    row_pos = lax.broadcasted_iota(jnp.int32, (tokens, ROWS), 1) + number * ROWS
-    online_step(queries, kv_refs[0], vt_ref[0], m_ref, acc_ref, key_pos <= row_pos)
-    for n in (1, 2):
-
-        @pl.when(ctx >= n)
-        def _():
-            online_step(queries, kv_refs[n], vt_ref[n], m_ref, acc_ref, None)
-
-    for j in range(2):
-        total = acc_ref[j, 256:257]
-        value = (acc_ref[j, :256] / total).T
-        for half in range(2):
-            out_ref[j, pl.ds(half, ROWS, stride=2), :] = value[:, half * 128 : half * 128 + 128]
-        log_ref[j : j + 1, :] = (m_ref[j] + jnp.log2(total)) * LN2
-
-
-def cycle_attention(qkv, blocks):
-    tokens = qkv.shape[0]
-    whole = pl.BlockSpec((tokens, 512), lambda i: (0, 0))
-    return pl.pallas_call(
-        cycle_kernel,
-        name="cycle",
-        grid=(tokens // ROWS,),
-        out_shape=(
-            jax.ShapeDtypeStruct((2, 2 * tokens, 128), jnp.float32),
-            jax.ShapeDtypeStruct((2, tokens), jnp.float32),
-        ),
-        in_specs=[pl.BlockSpec((tokens, 768), lambda i: (0, 0))] + [whole] * 2,
-        out_specs=(
-            pl.BlockSpec((2, 2 * ROWS, 128), lambda i: (0, i, 0)),
-            pl.BlockSpec((2, ROWS), lambda i: (0, i)),
-        ),
-        scratch_shapes=[
-            pltpu.VMEM((3, 256 + ONES, tokens), jnp.bfloat16),
-            pltpu.VMEM((2, 1, ROWS), jnp.float32),
-            pltpu.VMEM((2, 256 + ONES, ROWS), jnp.float32),
-        ],
-        compiler_params=pltpu.CompilerParams(vmem_limit_bytes=40 * 2**20),
-    )(qkv, *blocks)
-
-
 CHUNKS = 4
 SUB = 16
 
@@ -334,11 +285,11 @@
     gain_ref,
     w_qkv_hbm,
     hidden_ref,
+    out_ref,
+    log_ref,
     qkv_ref,
     kv1_ref,
     kv2_ref,
-    w_own,
-    w_sib,
     w_qkv,
     n_sib,
     part,
@@ -350,12 +301,11 @@
     y2_far,
     y2_in,
     rows_all,
-    acc,
     load_sem,
     sems,
 ):
     ctx, x, y, core = place()
-    width = w_own.shape[1]
+    width = w_own_hbm.shape[1]
     y_cols = width - x_cols
     low, high = pl.ds(0, x_cols), pl.ds(x_cols, y_cols)
     low_half = (pl.ds(0, x_cols // 2), pl.ds(x_cols // 2, x_cols // 2))
@@ -373,21 +323,10 @@
     over_y = (ctx, x * 4 + (1 - y) * 2 + core)
     sibling = (ctx, x * 4 + y * 2 + 1 - core)
     blocks = lax.axis_size("ctx")
-    later = [(lax.rem(ctx + d, blocks), head) for d in (1, 2, blocks - 2, blocks - 1)]
-
-    loads = [
-        pltpu.make_async_copy(source, target, load_sem.at[n])
-        for n, (source, target) in enumerate(
-            [(w_own_hbm, w_own), (w_sib_hbm, w_sib), (w_qkv_hbm, w_qkv)]
-        )
-    ]
-    for load in loads:
-        load.start()
-
-    barrier = pltpu.get_barrier_semaphore()
-    for peer in along + [over_y, sibling] + later:
-        pl.semaphore_signal(barrier, inc=1, device_id=peer, device_id_type=MESH)
-    pl.semaphore_wait(barrier, 8)
+    others = [(lax.rem(ctx + d, blocks), head) for d in range(1, 8)]
+
+    late_load = pltpu.make_async_copy(w_qkv_hbm, w_qkv, load_sem.at[2])
+    late_load.start()
 
     started = []
     pending = {}
@@ -403,27 +342,30 @@
             device_id_type=MESH,
         )
 
-    def send(kind, r, side, source, target, device):
-        copy = describe(kind, r, side, source, target, device)
-        copy.start()
+    def send(kind, r, side, ends):
+        def copy():
+            return describe(kind, r, side, *ends())
+
+        copy().start()
         started.append(copy)
         pending[kind, r, side] = copy
 
+    every = slice(None)
+
+    def spread_rows(r, kind, side, index, device):
+        send(kind, r, side, lambda: (rows_all.at[index()], rows_all.at[index()], device))
+
     def arrived(kind, r, sides=(0,)):
         for side in sides:
-            pending[kind, r, side].wait_recv()
+            pending[kind, r, side]().wait_recv()
 
     def wide(value):
         return value.astype(jnp.float32)
 
     both = (0, 1)
-    send("normed", 0, 0, normed_ref.at[:, 1 - core], n_sib, sibling)
-    loads[0].wait()
-    loads[1].wait()
-    arrived("normed", 0)
     tile = min(1024, width)
 
-    def project(r):
+    def project(r, w_own, w_sib):
         own_rows = normed_ref[:, core, r].reshape(8 * SUB, 256)
         sib_rows = n_sib[:, r].reshape(8 * SUB, 256)
 
@@ -436,19 +378,31 @@
 
         lax.fori_loop(0, width // tile, columns, 0)
         for s in both:
-            source = part.at[r, opposite, :, :, low_half[s]]
-            send("x1_far", r, s, source, x1_far.at[r, s], along[s])
-        send("y1", r, 0, part.at[r, :, 1 - y, :, high], y1_in.at[r], over_y)
-        for s in both:
-            source = part.at[r, beside[s], :, :, low_half[1 - s]]
-            send("x1_near", r, s, source, x1_in.at[r, s, :, :, low_half[1 - s]], along[s])
+
+            def far(s=s):
+                return part.at[r, opposite, :, :, low_half[s]], x1_far.at[r, s], along[s]
+
+            send("x1_far", r, s, far)
+        send("y1", r, 0, lambda: (part.at[r, :, 1 - y, :, high], y1_in.at[r], over_y))
+        for s in both:
+
+            def near(s=s):
+                half = low_half[1 - s]
+                return part.at[r, beside[s], :, :, half], x1_in.at[r, s, :, :, half], along[s]
+
+            send("x1_near", r, s, near)
 
     def relay_x1(r):
         arrived("x1_far", r, both)
         for s in both:
             ours = part.at[r, beside[s], :, :, low_half[s]]
             ours[...] = (wide(ours[...]) + wide(x1_far[r, s])).astype(jnp.bfloat16)
-            send("x1_sum", r, s, ours, x1_in.at[r, s, :, :, low_half[s]], along[s])
+
+            def summed(s=s):
+                half = low_half[s]
+                return part.at[r, beside[s], :, :, half], x1_in.at[r, s, :, :, half], along[s]
+
+            send("x1_sum", r, s, summed)
 
     def second(r):
         arrived("y1", r)
@@ -456,25 +410,37 @@
             ours = part.at[r, place_x, y, :, high]
             ours[...] = (wide(ours[...]) + wide(y1_in[r, place_x])).astype(jnp.bfloat16)
         for s in both:
-            source = part.at[r, opposite, y, :, high_half[s]]
-            send("y2_far", r, s, source, y2_far.at[r, s], along[s])
-        for s in both:
-            source = part.at[r, beside[s], y, :, high_half[1 - s]]
-            send("y2_near", r, s, source, y2_in.at[r, s, :, y_half[1 - s]], along[s])
+
+            def far(s=s):
+                return part.at[r, opposite, y, :, high_half[s]], y2_far.at[r, s], along[s]
+
+            send("y2_far", r, s, far)
+        for s in both:
+
+            def near(s=s):
+                source = part.at[r, beside[s], y, :, high_half[1 - s]]
+                return source, y2_in.at[r, s, :, y_half[1 - s]], along[s]
+
+            send("y2_near", r, s, near)
         arrived("x1_near", r, both)
         arrived("x1_sum", r, both)
         total = wide(part[r, x, 1 - y, :, low])
         for s in both:
             total += wide(x1_in[r, s, 1 - y])
         x2_out[r] = total.astype(jnp.bfloat16)
-        send("x2", r, 0, x2_out.at[r], x2_in.at[r], over_y)
+        send("x2", r, 0, lambda: (x2_out.at[r], x2_in.at[r], over_y))
 
     def relay_y2(r):
         arrived("y2_far", r, both)
         for s in both:
             ours = part.at[r, beside[s], y, :, high_half[s]]
             ours[...] = (wide(ours[...]) + wide(y2_far[r, s])).astype(jnp.bfloat16)
-            send("y2_sum", r, s, ours, y2_in.at[r, s, :, y_half[s]], along[s])
+
+            def summed(s=s):
+                source = part.at[r, beside[s], y, :, high_half[s]]
+                return source, y2_in.at[r, s, :, y_half[s]], along[s]
+
+            send("y2_sum", r, s, summed)
 
     def finish(r):
         arrived("x2", r)
@@ -496,47 +462,62 @@
         mine = rows_all.at[r, x, y, core]
         mine[:, low] = (left * factor * gain_ref[:, low]).astype(jnp.bfloat16)
         mine[:, high] = (right * factor * gain_ref[:, high]).astype(jnp.bfloat16)
-        for s in both:
-            send("h1", r, s, mine.at[:, g_low], mine.at[:, g_low], along[s])
-        send("g1", r, 0, mine.at[:, g_high], mine.at[:, g_high], over_y)
+
+        for s in both:
+            spread_rows(r, "h1", s, lambda: (r, x, y, core, every, g_low), along[s])
+        spread_rows(r, "g1", 0, lambda: (r, x, y, core, every, g_high), over_y)
 
     def pass_h1(r):
         arrived("h1", r, both)
         for s in both:
-            came = rows_all.at[r, beside[1 - s], y, core, :, g_low_half[s]]
-            send("h1_on", r, s, came, came, along[s])
+            spread_rows(
+                r,
+                "h1_on",
+                s,
+                lambda s=s: (r, beside[1 - s], y, core, every, g_low_half[s]),
+                along[s],
+            )
 
     def spread(r):
         arrived("g1", r)
-        column = rows_all.at[r, x, :, core, :, g_high]
-        for s in both:
-            send("g2", r, s, column, column, along[s])
+        for s in both:
+            spread_rows(r, "g2", s, lambda: (r, x, every, core, every, g_high), along[s])
         arrived("h1_on", r, both)
-        row = rows_all.at[r, :, y, core, :, g_low]
-        send("h2", r, 0, row, row, over_y)
+        spread_rows(r, "h2", 0, lambda: (r, every, y, core, every, g_low), over_y)
 
     def pass_g2(r):
         arrived("g2", r, both)
         for s in both:
-            came = rows_all.at[r, beside[1 - s], :, core, :, g_high_half[s]]
-            send("g2_on", r, s, came, came, along[s])
+            spread_rows(
+                r,
+                "g2_on",
+                s,
+                lambda s=s: (r, beside[1 - s], every, core, every, g_high_half[s]),
+                along[s],
+            )
 
     def share(r):
         arrived("h2", r)
-        ours = rows_all.at[r, :, :, core, :, g_low]
-        send("core", r, 0, ours, ours, sibling)
+        spread_rows(r, "core", 0, lambda: (r, every, every, core, every, g_low), sibling)
         arrived("g2_on", r, both)
-        ours = rows_all.at[r, :, :, core, :, g_high]
-        send("core", r, 1, ours, ours, sibling)
-
-    def next_copy(d, r, source):
-        target = (kv1_ref, kv2_ref)[d - 1].at[:, r]
-        return describe("next", r, d - 1, source, target, later[d - 1])
-
-    def project_next(r):
+        spread_rows(r, "core", 1, lambda: (r, every, every, core, every, g_high), sibling)
+
+    def next_copy(d, r, target, forward=False):
+        landing = (kv1_ref, kv2_ref)[d - 1].at[:, r]
+        kind = KINDS.index("next")
+        return pltpu.make_async_remote_copy(
+            src_ref=landing if forward else qkv_ref.at[:, r, :, 256:],
+            dst_ref=landing,
+            send_sem=sems.at[kind, r, 2 if forward else d - 1, 0],
+            recv_sem=sems.at[kind, r, d - 1, 1],
+            device_id=(target, head),
+            device_id_type=MESH,
+        )
+
+    def project_next(r, acc):
         arrived("core", r, both)
         if r == 0:
-            loads[2].wait()
+            late_load.wait()
 
         def depth(j, carry):
             span = pl.ds(pl.multiple_of(j * tile, tile), tile)
@@ -551,16 +532,18 @@
             qkv_ref[:, r, :, n * 256 : n * 256 + 256] = (
                 acc[n].astype(jnp.bfloat16).reshape(16, SUB, 256)
             )
-        source = qkv_ref.at[:, r, :, 256:]
-
-        @pl.when(ctx <= 6)
-        def _():
-            next_copy(1, r, source).start()
-
-        @pl.when(ctx <= 5)
-        def _():
-            next_copy(2, r, source).start()
-
+        for d, target, sends in routes:
+
+            @pl.when(sends)
+            def _():
+                next_copy(d, r, target).start()
+
+    routes = [
+        (1, lax.rem(ctx + 1, blocks), (ctx <= 6) & (ctx != 3)),
+        (2, lax.rem(ctx + 2, blocks), (ctx <= 5) & (ctx != 3)),
+        (1, lax.rem(ctx + 5, blocks), ctx == 3),
+        (2, lax.rem(ctx + 6, blocks), ctx == 3),
+    ]
     stages = [
         project,
         relay_x1,
@@ -573,55 +556,143 @@
         share,
         project_next,
     ]
-    for step in range(CHUNKS - 1 + len(stages)):
-        for r in reversed(range(CHUNKS)):
-            if 0 <= step - r < len(stages):
-                stages[step - r](r)
+
+    def steps(first, last, *weights):
+        for step in range(first, last):
+            for r in reversed(range(CHUNKS)):
+                if 0 <= step - r < len(stages):
+                    stages[step - r](r, *(weights if step - r in (0, len(stages) - 1) else ()))
+
+    def first_steps(w_own, w_sib):
+        loads = [
+            pltpu.make_async_copy(source, target, load_sem.at[n])
+            for n, (source, target) in enumerate([(w_own_hbm, w_own), (w_sib_hbm, w_sib)])
+        ]
+        for load in loads:
+            load.start()
+        barrier = pltpu.get_barrier_semaphore()
+        for peer in along + [over_y, sibling] + others:
+            pl.semaphore_signal(barrier, inc=1, device_id=peer, device_id_type=MESH)
+        pl.semaphore_wait(barrier, 11)
+        send("normed", 0, 0, lambda: (normed_ref.at[:, 1 - core], n_sib, sibling))
+        arrived("normed", 0)
+        for load in loads:
+            load.wait()
+        steps(0, CHUNKS, w_own, w_sib)
+
+    def last_steps(acc):
+        steps(CHUNKS, CHUNKS - 1 + len(stages), acc)
+
+    pl.run_scoped(
+        first_steps, pltpu.VMEM((256, width), jnp.bfloat16), pltpu.VMEM((256, width), jnp.bfloat16)
+    )
+    pl.run_scoped(last_steps, pltpu.VMEM((3, 16 * SUB, 256), jnp.float32))
+
+    for d in (1, 2):
+
+        @pl.when(ctx == d - 1)
+        def _():
+            for r in range(CHUNKS):
+                next_copy(d, r, 0).wait_recv()
+                next_copy(d, r, lax.rem(ctx + 4, blocks), True).start()
+
+    tokens = 16 * CHUNKS * SUB
+    groups = tokens // ROWS
+    heads = 16 // groups
+
+    def attend(vt_ref, m_ref, acc_ref):
+        m_ref[...] = jnp.full_like(m_ref, NEG)
+        acc_ref[...] = jnp.zeros_like(acc_ref)
+
+        def block(kv, own):
+            def columns(start, size):
+                return kv[:, :, :, start : start + size].reshape(tokens, size)
+
+            vt_ref[...] = with_ones(columns(256, 256))
+
+            def some(i, carry):
+                queries = qkv_ref[pl.ds(i * heads, heads), :, :, :256].reshape(ROWS, 256)
+                mask = None
+                if own:
+                    key_pos = lax.broadcasted_iota(jnp.int32, (tokens, ROWS), 0)
+                    row_pos = lax.broadcasted_iota(jnp.int32, (tokens, ROWS), 1) + i * ROWS
+                    mask = key_pos <= row_pos
+                online_step(
+                    scaled_queries(queries),
+                    lambda j: columns(j * HDIM, HDIM),
+                    vt_ref[...],
+                    m_ref.at[i],
+                    acc_ref.at[i],
+                    mask,
+                )
+                return carry
+
+            lax.fori_loop(0, groups, some, 0)
+
+        block(qkv_ref.at[:, :, :, 256:], True)
+        for d, landing in ((1, kv1_ref), (2, kv2_ref)):
+
+            @pl.when(ctx >= d)
+            def _():
+                for r in range(CHUNKS):
+                    next_copy(d, r, 0).wait_recv()
+                block(landing, False)
+
+        for i in range(groups):
+            for j in range(2):
+                total = acc_ref[i, j, 256:257]
+                value = (acc_ref[i, j, :256] / total).T
+                for half in range(2):
+                    out_ref[j, pl.ds(i * 2 * ROWS + half, ROWS, stride=2), :] = value[
+                        :, half * 128 : half * 128 + 128
+                    ]
+                log_ref[j : j + 1, i * ROWS : (i + 1) * ROWS] = (m_ref[i, j] + jnp.log2(total)) * LN2
+
+    pl.run_scoped(
+        attend,
+        pltpu.VMEM((256 + ONES, tokens), jnp.bfloat16),
+        pltpu.VMEM((groups, 2, 1, ROWS), jnp.float32),
+        pltpu.VMEM((groups, 2, 256 + ONES, ROWS), jnp.float32),
+    )
     for copy in started:
-        copy.wait_send()
+        copy().wait_send()
     for r in range(CHUNKS):
-        source = qkv_ref.at[:, r, :, 256:]
-
-        @pl.when(ctx <= 6)
-        def _():
-            next_copy(1, r, source).wait_send()
-
-        @pl.when(ctx <= 5)
-        def _():
-            next_copy(2, r, source).wait_send()
-
-        @pl.when(ctx >= 1)
-        def _():
-            next_copy(1, r, source).wait_recv()
-
-        @pl.when(ctx >= 2)
-        def _():
-            next_copy(2, r, source).wait_recv()
+        for d, target, sends in routes:
+
+            @pl.when(sends)
+            def _():
+                next_copy(d, r, target).wait_send()
+
+        for d in (1, 2):
+
+            @pl.when(ctx == d - 1)
+            def _():
+                next_copy(d, r, 0, True).wait_send()
 
 
 def project_and_spread(normed, w_own, w_sib, residual, gain, w_qkv):
     width = w_own.shape[1]
     x_cols = width * 5 // 8
     g_cols = width * 3 // 8
-    out_cols = 768
+    tokens = 16 * CHUNKS * SUB
     bf16 = jnp.bfloat16
     any_space = pl.BlockSpec(memory_space=pl.ANY)
     vmem = pl.BlockSpec(memory_space=pltpu.VMEM)
     sem = pltpu.SemaphoreType.DMA
-    hidden, qkv, kv1, kv2 = pl.pallas_call(
+    hidden, part_out, log_sums = pl.pallas_call(
         functools.partial(mid_kernel, x_cols, g_cols),
         name="project_and_spread",
         out_shape=(
             jax.ShapeDtypeStruct((CHUNKS, SUB, width), bf16),
-            jax.ShapeDtypeStruct((16, CHUNKS, SUB, out_cols), bf16),
-            jax.ShapeDtypeStruct((16, CHUNKS, SUB, 512), bf16),
-            jax.ShapeDtypeStruct((16, CHUNKS, SUB, 512), bf16),
+            jax.ShapeDtypeStruct((2, 2 * tokens, 128), jnp.float32),
+            jax.ShapeDtypeStruct((2, tokens), jnp.float32),
         ),
         in_specs=[vmem, any_space, any_space, vmem, vmem, any_space],
-        out_specs=(vmem, vmem, any_space, any_space),
+        out_specs=(vmem, vmem, vmem),
         scratch_shapes=[
-            pltpu.VMEM((256, width), bf16),
-            pltpu.VMEM((256, width), bf16),
+            pltpu.VMEM((16, CHUNKS, SUB, 768), bf16),
+            pltpu.VMEM((16, CHUNKS, SUB, 512), bf16),
+            pltpu.VMEM((16, CHUNKS, SUB, 512), bf16),
             pltpu.VMEM((3, width, 256), bf16),
             pltpu.VMEM((8, CHUNKS, SUB, 256), bf16),
             pltpu.VMEM((CHUNKS, 4, 2, SUB, width), bf16),
@@ -633,9 +704,8 @@
             pltpu.VMEM((CHUNKS, 2, SUB, (width - x_cols) // 2), bf16),
             pltpu.VMEM((CHUNKS, 2, SUB, width - x_cols), bf16),
             pltpu.VMEM((CHUNKS, 4, 2, 2, SUB, width), bf16),
-            pltpu.VMEM((3, 16 * SUB, 256), jnp.float32),
             sem((3,)),
-            sem((len(KINDS), CHUNKS, 2, 2)),
+            sem((len(KINDS), CHUNKS, 3, 2)),
         ],
         compiler_params=pltpu.CompilerParams(
             collective_id=0, has_side_effects=True, vmem_limit_bytes=63 * 2**20
@@ -648,12 +718,7 @@
         gain.reshape(1, width),
         w_qkv,
     )
-    tokens = 16 * CHUNKS * SUB
-    return (
-        hidden.reshape(CHUNKS * SUB, width),
-        qkv.reshape(tokens, out_cols),
-        (kv1.reshape(tokens, 512), kv2.reshape(tokens, 512)),
-    )
+    return hidden.reshape(CHUNKS * SUB, width), part_out, log_sums
 
 
 def on_device(residual, q_win, kv_win, lam_win, gn_gain, w_out_a, norm_gain, w_qkv):
@@ -662,10 +727,9 @@
     normed = window_attention(
         q_win.reshape(tokens_here, 256), kv_win.reshape(tokens_here, 512), lam_win, gn_gain
     )
-    h_rows, qkv, blocks = project_and_spread(
+    h_rows, part_out, log_out = project_and_spread(
         normed, w_out_a, w_sib, residual, norm_gain, w_qkv[:, 0].transpose(1, 0, 2)
     )
-    part_out, log_out = cycle_attention(qkv, blocks)
     return (
         h_rows,
         part_out.reshape(2, tokens_here, 1, 256),

time: 268 us -> 252 us (0.940)
  the two profiles are of different devices: /device:TPU:57 before, /device:TPU:24 now
where the time goes in v6:
time: 252 us; the launch traced here: 250 us
  Pallas kernels  237 us (94%)
  local copies, waits for them, and re-layouts  12.5 us (5%)
    pallas_call x1, Pallas kernels, project_and_spread(): pl.pallas_call(functools.partial(mid_kernel, x_cols, g_cols), name='proje...  171 us
    pallas_call x1, Pallas kernels, window_attention(): pl.pallas_call(window_kernel, name='window', out_shape=jax.ShapeDtypeStru...  65.7 us
    unnamed x12, local copies, waits for them, and re-layouts  12.5 us
  transfers between devices with their start and end apart: 1, of which 0 were waited for; matrix products, arithmetic and copies ran while one was open for 1% of the time, Pallas kernels for 26%

profile of v6, /device:TPU:24, one launch (start us, length us, event | category | flops | bytes accessed | tf_op | source)
XLA Modules:
  0.0 250.4 jit_solution(6407221920702339509)
XLA Ops:
  0.6 0.1 collective-permute-start
  0.7 1.4 copy.13
  2.2 0.0 copy-start.1
  2.2 1.0 copy-done.1
  3.2 0.0 copy-start.2
  3.2 0.7 copy-done.2
  3.9 0.0 copy-start.3
  3.9 0.7 copy-done.3
  4.6 65.7 %window.1 = bf16[1024,256]{1,0:T(8,128)(2,1)S(1)} custom-call(f32[4,128]{1,0:T(4,128)S(1)} %copy-done.2, bf16[1024,256]{1,0:T(8,128)(2,1)S(1)} %bitcast.16, f32[1,256]{1,0:T(1,128)S(1)} %bitcast.17, bf16[1024,512]{1,0:T(8,128)(2,1)S(1)} %bitcast.14), custom_call_target="tpu_custom_call" | custom-call | tf_op jit(solution)/shard_map/window/pallas_call | solution.py:226
  70.3 0.0 copy-start
  70.4 0.8 copy-done
  71.1 0.0 collective-permute-done.w_sib_hbm
  71.1 171.3 %project_and_spread.1 = (bf16[4,16,8192]{2,1,0:T(8,128)(2,1)}, f32[2,2048,128]{2,1,0:T(8,128)}, f32[2,1024]{1,0:T(2,128)}) custom-call(bf16[8,2,4,16,256]{4,3,2,1,0:T(8,128)(2,1)} %bitcast.15, bf16[256,8192]{1,0:T(8,128)(2,1)} %w_own_hbm.1, bf16[256,8192]{1,0:T(8,128)(2,1)} %collective-permute-done.w_sib_hbm, bf16[4,16,8192]{2,1,0:T(8,128)(2,1)} %bitcast.20, ...), custom_call_target="tpu_custom_call" | custom-call | tf_op jit(solution)/shard_map/project_and_spread/pallas_call | solution.py:682
  242.4 1.3 copy.12
  243.7 2.3 copy.16
  246.0 4.3 %copy.17 = f32[2,1024,1,256]{3,2,1,0:T(1,128)} copy(f32[2,1024,1,256]{3,2,1,0:T(1,128)} %bitcast.19) | data formatting | bytes 4194304
Async XLA Ops:
  0.6 70.5 %collective-permute-start = (bf16[256,8192]{1,0:T(8,128)(2,1)}, bf16[256,8192]{1,0:T(8,128)(2,1)}, u32[]{:S(2)}, u32[]{:S(2)}) collective-permute-start(bf16[256,8192]{1,0:T(8,128)(2,1)} %w_own_hbm.1), channel_id=1, source_target_pairs={{0,1},{1,0},{2,3},{3,2},{4,5},{5,4},{6,7},{7,6},{8,9},{9,8},{10,11... | collective-permute-start | bytes 12582920 | tf_op jit(solution)/shard_map/ppermute | solution.py:726
  2.2 1.0 copy-start.1
  3.2 0.7 copy-start.2
  3.9 0.7 copy-start.3
  70.3 0.8 copy-start

commit v7 on v6

--- a/solution.py
+++ b/solution.py
@@ -240,7 +240,7 @@
             pltpu.SemaphoreType.DMA((2, PIECES)),
         ],
         compiler_params=pltpu.CompilerParams(
-            collective_id=1, has_side_effects=True, vmem_limit_bytes=40 * 2**20
+            collective_id=1, has_side_effects=True, vmem_limit_bytes=62 * 2**20
         ),
     )(lam_win, queries, gain.reshape(1, 256), keys_values)
 
@@ -285,8 +285,8 @@
     gain_ref,
     w_qkv_hbm,
     hidden_ref,
-    out_ref,
-    log_ref,
+    acc_ref,
+    m_ref,
     qkv_ref,
     kv1_ref,
     kv2_ref,
@@ -559,7 +559,7 @@
 
     def steps(first, last, *weights):
         for step in range(first, last):
-            for r in reversed(range(CHUNKS)):
+            for r in range(CHUNKS):
                 if 0 <= step - r < len(stages):
                     stages[step - r](r, *(weights if step - r in (0, len(stages) - 1) else ()))
 
@@ -600,7 +600,7 @@
     groups = tokens // ROWS
     heads = 16 // groups
 
-    def attend(vt_ref, m_ref, acc_ref):
+    def attend(vt_ref):
         m_ref[...] = jnp.full_like(m_ref, NEG)
         acc_ref[...] = jnp.zeros_like(acc_ref)
 
@@ -638,22 +638,7 @@
                     next_copy(d, r, 0).wait_recv()
                 block(landing, False)
 
-        for i in range(groups):
-            for j in range(2):
-                total = acc_ref[i, j, 256:257]
-                value = (acc_ref[i, j, :256] / total).T
-                for half in range(2):
-                    out_ref[j, pl.ds(i * 2 * ROWS + half, ROWS, stride=2), :] = value[
-                        :, half * 128 : half * 128 + 128
-                    ]
-                log_ref[j : j + 1, i * ROWS : (i + 1) * ROWS] = (m_ref[i, j] + jnp.log2(total)) * LN2
-
-    pl.run_scoped(
-        attend,
-        pltpu.VMEM((256 + ONES, tokens), jnp.bfloat16),
-        pltpu.VMEM((groups, 2, 1, ROWS), jnp.float32),
-        pltpu.VMEM((groups, 2, 256 + ONES, ROWS), jnp.float32),
-    )
+    pl.run_scoped(attend, pltpu.VMEM((256 + ONES, tokens), jnp.bfloat16))
     for copy in started:
         copy().wait_send()
     for r in range(CHUNKS):
@@ -672,20 +657,20 @@
 
 def project_and_spread(normed, w_own, w_sib, residual, gain, w_qkv):
     width = w_own.shape[1]
-    x_cols = width * 5 // 8
-    g_cols = width * 3 // 8
+    x_cols = width * 9 // 16
+    g_cols = width * 7 // 16
     tokens = 16 * CHUNKS * SUB
     bf16 = jnp.bfloat16
     any_space = pl.BlockSpec(memory_space=pl.ANY)
     vmem = pl.BlockSpec(memory_space=pltpu.VMEM)
     sem = pltpu.SemaphoreType.DMA
-    hidden, part_out, log_sums = pl.pallas_call(
+    hidden, sums, highest = pl.pallas_call(
         functools.partial(mid_kernel, x_cols, g_cols),
         name="project_and_spread",
         out_shape=(
             jax.ShapeDtypeStruct((CHUNKS, SUB, width), bf16),
-            jax.ShapeDtypeStruct((2, 2 * tokens, 128), jnp.float32),
-            jax.ShapeDtypeStruct((2, tokens), jnp.float32),
+            jax.ShapeDtypeStruct((tokens // ROWS, 2, 256 + ONES, ROWS), jnp.float32),
+            jax.ShapeDtypeStruct((tokens // ROWS, 2, 1, ROWS), jnp.float32),
         ),
         in_specs=[vmem, any_space, any_space, vmem, vmem, any_space],
         out_specs=(vmem, vmem, vmem),
@@ -718,7 +703,43 @@
         gain.reshape(1, width),
         w_qkv,
     )
-    return hidden.reshape(CHUNKS * SUB, width), part_out, log_sums
+    return hidden.reshape(CHUNKS * SUB, width), sums, highest
+
+
+def settle_kernel(hidden_in, acc_ref, m_ref, hidden_ref, out_ref, log_ref):
+    hidden_ref[...] = hidden_in[...]
+    for j in range(2):
+        total = acc_ref[0, j, 256:257]
+        value = (acc_ref[0, j, :256] / total).T
+        for half in range(2):
+            out_ref[j, pl.ds(half, ROWS, stride=2), :] = value[:, half * 128 : half * 128 + 128]
+        log_ref[j] = (m_ref[0, j] + jnp.log2(total)) * LN2
+
+
+def settle(hidden, sums, highest):
+    groups = sums.shape[0]
+    rows, width = hidden.shape
+    return pl.pallas_call(
+        settle_kernel,
+        name="settle",
+        grid=(groups,),
+        out_shape=(
+            jax.ShapeDtypeStruct((rows, width), jnp.bfloat16),
+            jax.ShapeDtypeStruct((2, 2 * groups * ROWS, 128), jnp.float32),
+            jax.ShapeDtypeStruct((2, 1, groups * ROWS), jnp.float32),
+        ),
+        in_specs=[
+            pl.BlockSpec((rows // groups, width), lambda i: (i, 0)),
+            pl.BlockSpec((1, 2, 256 + ONES, ROWS), lambda i: (i, 0, 0, 0)),
+            pl.BlockSpec((1, 2, 1, ROWS), lambda i: (i, 0, 0, 0)),
+        ],
+        out_specs=(
+            pl.BlockSpec((rows // groups, width), lambda i: (i, 0)),
+            pl.BlockSpec((2, 2 * ROWS, 128), lambda i: (0, i, 0)),
+            pl.BlockSpec((2, 1, ROWS), lambda i: (0, 0, i)),
+        ),
+        compiler_params=pltpu.CompilerParams(vmem_limit_bytes=62 * 2**20),
+    )(hidden, sums, highest)
 
 
 def on_device(residual, q_win, kv_win, lam_win, gn_gain, w_out_a, norm_gain, w_qkv):
@@ -727,13 +748,15 @@
     normed = window_attention(
         q_win.reshape(tokens_here, 256), kv_win.reshape(tokens_here, 512), lam_win, gn_gain
     )
-    h_rows, part_out, log_out = project_and_spread(
-        normed, w_out_a, w_sib, residual, norm_gain, w_qkv[:, 0].transpose(1, 0, 2)
+    h_rows, part_out, log_out = settle(
+        *project_and_spread(
+            normed, w_out_a, w_sib, residual, norm_gain, w_qkv[:, 0].transpose(1, 0, 2)
+        )
     )
     return (
         h_rows,
         part_out.reshape(2, tokens_here, 1, 256),
-        log_out.reshape(2, 1, tokens_here),
+        log_out,
     )
 
 

time: 252 us -> 242 us (0.960)
  local copies, waits for them, and re-layouts: 12.5 us -> 2.42 us
    unnamed x12 -> x1, local copies, waits for them, and re-layouts: 12.5 us -> 2.42 us
    pallas_call x1, Pallas kernels: 171 us -> 166 us  [project_and_spread(): pl.pallas_call(functools.partial(mid_kernel, x_cols, g_cols), name='proje...]
    pallas_call x0 -> x1, Pallas kernels: none -> 4.37 us  [settle(): pl.pallas_call(settle_kernel, name='settle', grid=(groups,), out_shape=(j...]
  transfers between devices with their start and end apart: 1 -> 1, of which waited for: 0 -> 0; matrix products, arithmetic and copies ran while one was open for 1% -> 1% of each run, Pallas kernels for 26% -> 28%
where the time goes in v7:
time: 242 us
  Pallas kernels  239 us (99%)
  local copies, waits for them, and re-layouts  2.42 us (1%)
    pallas_call x1, Pallas kernels, project_and_spread(): pl.pallas_call(functools.partial(mid_kernel, x_cols, g_cols), name='proje...  166 us
    pallas_call x1, Pallas kernels, window_attention(): pl.pallas_call(window_kernel, name='window', out_shape=jax.ShapeDtypeStru...  68 us
  transfers between devices with their start and end apart: 1, of which 0 were waited for; matrix products, arithmetic and copies ran while one was open for 1% of the time, Pallas kernels for 28%

profile of v7, /device:TPU:24, one launch (start us, length us, event | category | flops | bytes accessed | tf_op | source)
XLA Modules:
  0.0 241.7 jit_solution(8488744662875120282)
XLA Ops:
  0.6 0.1 collective-permute-start
  0.7 2.4 %copy.12 = bf16[128,8,2,256]{3,1,2,0:T(8,128)(2,1)} copy(bf16[128,8,2,256]{3,2,1,0:T(2,128)(2,1)} %bitcast.18) | data formatting | bytes 2097152
  3.1 68.0 %window.1 = bf16[1024,256]{1,0:T(8,128)(2,1)} custom-call(f32[4,128]{1,0:T(4,128)} %lam_ref.1, bf16[1024,256]{1,0:T(8,128)(2,1)} %bitcast.19, f32[1,256]{1,0:T(1,128)} %bitcast.21, bf16[1024,512]{1,0:T(8,128)(2,1)} %bitcast.14), custom_call_target="tpu_custom_call" | custom-call | tf_op jit(solution)/shard_map/window/pallas_call | solution.py:226
  71.2 0.0 collective-permute-done.w_sib_hbm
  71.2 166.1 %project_and_spread.1 = (bf16[4,16,8192]{2,1,0:T(8,128)(2,1)}, f32[4,2,272,256]{3,2,1,0:T(8,128)}, f32[4,2,1,256]{3,2,1,0:T(1,128)}) custom-call(bf16[8,2,4,16,256]{4,3,2,1,0:T(8,128)(2,1)} %bitcast.15, bf16[256,8192]{1,0:T(8,128)(2,1)} %w_own_hbm.1, bf16[256,8192]{1,0:T(8,128)(2,1)} %collective-permute-done.w_sib_hbm, bf16[4,16,8192]{2,1,0:T(8,128)(2,1)} %bitcast.16, ...), custom_call_target="tpu_custom_call" | custom-call | tf_op jit(solution)/shard_map/project_and_spread/pallas_call | solution.py:667
  237.4 4.4 %settle.1 = (bf16[64,8192]{1,0:T(8,128)(2,1)}, f32[2,2048,128]{2,1,0:T(8,128)}, f32[2,1,1024]{2,1,0:T(1,128)}) custom-call(bf16[64,8192]{1,0:T(8,128)(2,1)} %bitcast.17, f32[4,2,272,256]{3,2,1,0:T(8,128)} %get-tuple-element.10.acc_ref, f32[4,2,1,256]{3,2,1,0:T(1,128)} %get-tuple-element.11.m_ref), custom_call_target="tpu_custom_call" | custom-call | tf_op jit(solution)/shard_map/settle/pallas_call | solution.py:722
Async XLA Ops:
  0.6 70.6 %collective-permute-start = (bf16[256,8192]{1,0:T(8,128)(2,1)}, bf16[256,8192]{1,0:T(8,128)(2,1)}, u32[]{:S(2)}, u32[]{:S(2)}) collective-permute-start(bf16[256,8192]{1,0:T(8,128)(2,1)} %w_own_hbm.1), channel_id=1, source_target_pairs={{0,1},{1,0},{2,3},{3,2},{4,5},{5,4},{6,7},{7,6},{8,9},{9,8},{10,11... | collective-permute-start | bytes 12582920 | tf_op jit(solution)/shard_map/ppermute | solution.py:747

commit v8 on v7

--- a/solution.py
+++ b/solution.py
@@ -123,7 +123,8 @@
     acc_ref[...] = jnp.zeros_like(acc_ref)
 
     def all_queries(keys, edge):
-        vt_ref[...] = with_ones(keys[:, 256:])
+        count = keys.shape[0]
+        vt_ref[:, :count] = with_ones(keys[:, 256:])
 
         def some(i, carry):
             rows = pl.ds(pl.multiple_of(i * ROWS, ROWS), ROWS)
@@ -135,7 +136,7 @@
             online_step(
                 q_scaled[rows, :],
                 lambda j: keys[:, j * HDIM : (j + 1) * HDIM],
-                vt_ref[...],
+                vt_ref[:, :count],
                 m_ref.at[i],
                 acc_ref.at[i],
                 mask,
@@ -177,10 +178,13 @@
 
         @pl.when(ctx >= e)
         def _():
-            if e == 2:
-                for n in range(PIECES):
+            if e != 2:
+                all_queries(kv_in.at[e - 1], None)
+                return
+            for half in range(2):
+                for n in range(half * PIECES // 2, (half + 1) * PIECES // 2):
                     copy_along(2, n, kv_ref).wait_recv()
-            all_queries(kv_in.at[e - 1], None)
+                all_queries(kv_in.at[1, pl.ds(half * tokens // 2, tokens // 2)], None)
 
     pairs = lam_ref[...]
     lam = (
@@ -604,11 +608,13 @@
         m_ref[...] = jnp.full_like(m_ref, NEG)
         acc_ref[...] = jnp.zeros_like(acc_ref)
 
-        def block(kv, own):
+        def block(kv, own, first=0, last=CHUNKS):
+            count = 16 * (last - first) * SUB
+
             def columns(start, size):
-                return kv[:, :, :, start : start + size].reshape(tokens, size)
-
-            vt_ref[...] = with_ones(columns(256, 256))
+                return kv[:, first:last, :, start : start + size].reshape(count, size)
+
+            vt_ref[:, :count] = with_ones(columns(256, 256))
 
             def some(i, carry):
                 queries = qkv_ref[pl.ds(i * heads, heads), :, :, :256].reshape(ROWS, 256)
@@ -620,7 +626,7 @@
                 online_step(
                     scaled_queries(queries),
                     lambda j: columns(j * HDIM, HDIM),
-                    vt_ref[...],
+                    vt_ref[:, :count],
                     m_ref.at[i],
                     acc_ref.at[i],
                     mask,
@@ -630,13 +636,14 @@
             lax.fori_loop(0, groups, some, 0)
 
         block(qkv_ref.at[:, :, :, 256:], True)
-        for d, landing in ((1, kv1_ref), (2, kv2_ref)):
-
-            @pl.when(ctx >= d)
-            def _():
-                for r in range(CHUNKS):
-                    next_copy(d, r, 0).wait_recv()
-                block(landing, False)
+        for first, last in ((0, CHUNKS - 1), (CHUNKS - 1, CHUNKS)):
+            for d, landing in ((1, kv1_ref), (2, kv2_ref)):
+
+                @pl.when(ctx >= d)
+                def _():
+                    for r in range(first, last):
+                        next_copy(d, r, 0).wait_recv()
+                    block(landing, False, first, last)
 
     pl.run_scoped(attend, pltpu.VMEM((256 + ONES, tokens), jnp.bfloat16))
     for copy in started:

time: 242 us -> 237 us (0.979)
  Pallas kernels: 239 us -> 234 us
    pallas_call x1, Pallas kernels: 166 us -> 164 us  [project_and_spread(): pl.pallas_call(functools.partial(mid_kernel, x_cols, g_cols), name='proje...]
where the time goes in v8:
time: 237 us
  Pallas kernels  234 us (99%)
  local copies, waits for them, and re-layouts  2.42 us (1%)
    pallas_call x1, Pallas kernels, project_and_spread(): pl.pallas_call(functools.partial(mid_kernel, x_cols, g_cols), name='proje...  164 us
    pallas_call x1, Pallas kernels, window_attention(): pl.pallas_call(window_kernel, name='window', out_shape=jax.ShapeDtypeStru...  65.8 us
  transfers between devices with their start and end apart: 1, of which 0 were waited for; matrix products, arithmetic and copies ran while one was open for 1% of the time, Pallas kernels for 28%

profile of v8, /device:TPU:24, one launch (start us, length us, event | category | flops | bytes accessed | tf_op | source)
XLA Modules:
  0.0 236.9 jit_solution(13416477300968031997)
XLA Ops:
  0.6 0.1 collective-permute-start
  0.7 2.4 %copy.12 = bf16[128,8,2,256]{3,1,2,0:T(8,128)(2,1)} copy(bf16[128,8,2,256]{3,2,1,0:T(2,128)(2,1)} %bitcast.18) | data formatting | bytes 2097152
  3.1 65.8 %window.1 = bf16[1024,256]{1,0:T(8,128)(2,1)} custom-call(f32[4,128]{1,0:T(4,128)} %lam_ref.1, bf16[1024,256]{1,0:T(8,128)(2,1)} %bitcast.19, f32[1,256]{1,0:T(1,128)} %bitcast.21, bf16[1024,512]{1,0:T(8,128)(2,1)} %bitcast.14), custom_call_target="tpu_custom_call" | custom-call | tf_op jit(solution)/shard_map/window/pallas_call | solution.py:230
  69.0 0.0 collective-permute-done.w_sib_hbm
  69.0 163.5 %project_and_spread.1 = (bf16[4,16,8192]{2,1,0:T(8,128)(2,1)}, f32[4,2,272,256]{3,2,1,0:T(8,128)}, f32[4,2,1,256]{3,2,1,0:T(1,128)}) custom-call(bf16[8,2,4,16,256]{4,3,2,1,0:T(8,128)(2,1)} %bitcast.15, bf16[256,8192]{1,0:T(8,128)(2,1)} %w_own_hbm.1, bf16[256,8192]{1,0:T(8,128)(2,1)} %collective-permute-done.w_sib_hbm, bf16[4,16,8192]{2,1,0:T(8,128)(2,1)} %bitcast.16, ...), custom_call_target="tpu_custom_call" | custom-call | tf_op jit(solution)/shard_map/project_and_spread/pallas_call | solution.py:674
  232.5 4.4 %settle.1 = (bf16[64,8192]{1,0:T(8,128)(2,1)}, f32[2,2048,128]{2,1,0:T(8,128)}, f32[2,1,1024]{2,1,0:T(1,128)}) custom-call(bf16[64,8192]{1,0:T(8,128)(2,1)} %bitcast.17, f32[4,2,272,256]{3,2,1,0:T(8,128)} %get-tuple-element.10.acc_ref, f32[4,2,1,256]{3,2,1,0:T(1,128)} %get-tuple-element.11.m_ref), custom_call_target="tpu_custom_call" | custom-call | tf_op jit(solution)/shard_map/settle/pallas_call | solution.py:729
Async XLA Ops:
  0.6 68.4 %collective-permute-start = (bf16[256,8192]{1,0:T(8,128)(2,1)}, bf16[256,8192]{1,0:T(8,128)(2,1)}, u32[]{:S(2)}, u32[]{:S(2)}) collective-permute-start(bf16[256,8192]{1,0:T(8,128)(2,1)} %w_own_hbm.1), channel_id=1, source_target_pairs={{0,1},{1,0},{2,3},{3,2},{4,5},{5,4},{6,7},{7,6},{8,9},{9,8},{10,11... | collective-permute-start | bytes 12582920 | tf_op jit(solution)/shard_map/ppermute | solution.py:754

commit v9 on v8

--- a/solution.py
+++ b/solution.py
@@ -127,12 +127,24 @@
         vt_ref[:, :count] = with_ones(keys[:, 256:])
 
         def some(i, carry):
+            if edge == "far":
+                rows = pl.ds(i * ROWS, ROWS)
+                seen = (tokens - i * ROWS, ROWS)
+                online_step(
+                    q_scaled[rows, :],
+                    lambda j: keys[i * ROWS : tokens, j * HDIM : (j + 1) * HDIM],
+                    vt_ref[:, i * ROWS : tokens],
+                    m_ref.at[i],
+                    acc_ref.at[i],
+                    lax.broadcasted_iota(jnp.int32, seen, 0) > lax.broadcasted_iota(jnp.int32, seen, 1),
+                )
+                return carry
             rows = pl.ds(pl.multiple_of(i * ROWS, ROWS), ROWS)
             mask = None
             if edge is not None:
                 key_pos = lax.broadcasted_iota(jnp.int32, (tokens, ROWS), 0)
                 row_pos = lax.broadcasted_iota(jnp.int32, (tokens, ROWS), 1) + i * ROWS
-                mask = key_pos <= row_pos if edge == "own" else key_pos > row_pos
+                mask = key_pos <= row_pos
             online_step(
                 q_scaled[rows, :],
                 lambda j: keys[:, j * HDIM : (j + 1) * HDIM],
@@ -143,7 +155,11 @@
             )
             return carry
 
-        lax.fori_loop(0, tokens // ROWS, some, 0)
+        if edge == "far":
+            for i in range(tokens // ROWS):
+                some(i, 0)
+        else:
+            lax.fori_loop(0, tokens // ROWS, some, 0)
 
     all_queries(kv_ref, "own")
 
@@ -619,21 +635,34 @@
             def some(i, carry):
                 queries = qkv_ref[pl.ds(i * heads, heads), :, :, :256].reshape(ROWS, 256)
                 mask = None
+                seen = count
                 if own:
-                    key_pos = lax.broadcasted_iota(jnp.int32, (tokens, ROWS), 0)
-                    row_pos = lax.broadcasted_iota(jnp.int32, (tokens, ROWS), 1) + i * ROWS
+                    seen = (i + 1) * ROWS
+                    key_pos = lax.broadcasted_iota(jnp.int32, (seen, ROWS), 0)
+                    row_pos = lax.broadcasted_iota(jnp.int32, (seen, ROWS), 1) + i * ROWS
                     mask = key_pos <= row_pos
+
+                def keys_of(j):
+                    if own:
+                        part_of = kv[: (i + 1) * heads, :, :, j * HDIM : (j + 1) * HDIM]
+                        return part_of.reshape(seen, HDIM)
+                    return columns(j * HDIM, HDIM)
+
                 online_step(
                     scaled_queries(queries),
-                    lambda j: columns(j * HDIM, HDIM),
-                    vt_ref[:, :count],
+                    keys_of,
+                    vt_ref[:, :seen],
                     m_ref.at[i],
                     acc_ref.at[i],
                     mask,
                 )
                 return carry
 
-            lax.fori_loop(0, groups, some, 0)
+            if own:
+                for i in range(groups):
+                    some(i, 0)
+            else:
+                lax.fori_loop(0, groups, some, 0)
 
         block(qkv_ref.at[:, :, :, 256:], True)
         for first, last in ((0, CHUNKS - 1), (CHUNKS - 1, CHUNKS)):

time: 237 us -> 237 us (level)
  no operation moved by 1% of the time
where the time goes in v9:
time: 237 us
  Pallas kernels  234 us (99%)
  local copies, waits for them, and re-layouts  2.42 us (1%)
    pallas_call x1, Pallas kernels, project_and_spread(): pl.pallas_call(functools.partial(mid_kernel, x_cols, g_cols), name='proje...  164 us
    pallas_call x1, Pallas kernels, window_attention(): pl.pallas_call(window_kernel, name='window', out_shape=jax.ShapeDtypeStru...  65.8 us
  transfers between devices with their start and end apart: 1, of which 0 were waited for; matrix products, arithmetic and copies ran while one was open for 1% of the time, Pallas kernels for 28%

profile of v9, /device:TPU:24, one launch (start us, length us, event | category | flops | bytes accessed | tf_op | source)
XLA Modules:
  0.0 236.9 jit_solution(7383879458666355697)
XLA Ops:
  0.6 0.1 collective-permute-start
  0.7 2.4 %copy.12 = bf16[128,8,2,256]{3,1,2,0:T(8,128)(2,1)} copy(bf16[128,8,2,256]{3,2,1,0:T(2,128)(2,1)} %bitcast.18) | data formatting | bytes 2097152
  3.1 65.8 %window.1 = bf16[1024,256]{1,0:T(8,128)(2,1)} custom-call(f32[4,128]{1,0:T(4,128)} %lam_ref.1, bf16[1024,256]{1,0:T(8,128)(2,1)} %bitcast.19, f32[1,256]{1,0:T(1,128)} %bitcast.21, bf16[1024,512]{1,0:T(8,128)(2,1)} %bitcast.14), custom_call_target="tpu_custom_call" | custom-call | tf_op jit(solution)/shard_map/window/pallas_call | solution.py:246
  69.0 0.0 collective-permute-done.w_sib_hbm
  69.0 163.5 %project_and_spread.1 = (bf16[4,16,8192]{2,1,0:T(8,128)(2,1)}, f32[4,2,272,256]{3,2,1,0:T(8,128)}, f32[4,2,1,256]{3,2,1,0:T(1,128)}) custom-call(bf16[8,2,4,16,256]{4,3,2,1,0:T(8,128)(2,1)} %bitcast.15, bf16[256,8192]{1,0:T(8,128)(2,1)} %w_own_hbm.1, bf16[256,8192]{1,0:T(8,128)(2,1)} %collective-permute-done.w_sib_hbm, bf16[4,16,8192]{2,1,0:T(8,128)(2,1)} %bitcast.16, ...), custom_call_target="tpu_custom_call" | custom-call | tf_op jit(solution)/shard_map/project_and_spread/pallas_call | solution.py:703
  232.5 4.4 %settle.1 = (bf16[64,8192]{1,0:T(8,128)(2,1)}, f32[2,2048,128]{2,1,0:T(8,128)}, f32[2,1,1024]{2,1,0:T(1,128)}) custom-call(bf16[64,8192]{1,0:T(8,128)(2,1)} %bitcast.17, f32[4,2,272,256]{3,2,1,0:T(8,128)} %get-tuple-element.10.acc_ref, f32[4,2,1,256]{3,2,1,0:T(1,128)} %get-tuple-element.11.m_ref), custom_call_target="tpu_custom_call" | custom-call | tf_op jit(solution)/shard_map/settle/pallas_call | solution.py:758
Async XLA Ops:
  0.6 68.3 %collective-permute-start = (bf16[256,8192]{1,0:T(8,128)(2,1)}, bf16[256,8192]{1,0:T(8,128)(2,1)}, u32[]{:S(2)}, u32[]{:S(2)}) collective-permute-start(bf16[256,8192]{1,0:T(8,128)(2,1)} %w_own_hbm.1), channel_id=1, source_target_pairs={{0,1},{1,0},{2,3},{3,2},{4,5},{5,4},{6,7},{7,6},{8,9},{9,8},{10,11... | collective-permute-start | bytes 12582920 | tf_op jit(solution)/shard_map/ppermute | solution.py:783
